TPU v7x, 32 devices: a whole 2x2x4 slice. The times are simulated.
32 devices in a mesh: pts: 16 (over z, y, core), cam: 2 (over x).
Axes of the slice: x: 2, y: 2, z: 4, core: 2. Of those that a mesh axis runs over, the one named last changes fastest.
Arguments:
- rhs: float32 [2, 128, 576], P('cam', 'pts'), may hold values from -6 to 6
- damp_cam: float32 [2, 128, 576], P('cam', 'pts'), may hold values from 0.2 to 1
- precond: float32 [2, 128, 576], P('cam', 'pts'), may hold values from 0.3 to 3
- cam_jac: float32 [2, 1536, 8, 18, 128], P('cam', 'pts'), may hold values from -0.3125 to 0.3125
- pt_jac: float32 [2, 1536, 8, 6, 128], P('cam', 'pts'), may hold values from -6 to 6
- damp_pt: float32 [2, 1536, 3, 128], P('cam', 'pts'), may hold values from 0.5 to 8
- cam_index: int32 [2, 1536, 8, 128], P('cam', 'pts'), may hold values from 0 to 63
- tile_ids: int32 [2, 1536, 8], P('cam', 'pts'), may hold values from 0 to 255, as said below
- counts: int32 [2, 1536], P('cam', 'pts'), may hold values from 2 to 8, as said below
Outputs:
- solution: float32 [2, 128, 576], P('cam', 'pts')
- residual: float32 [2, 128, 576], P('cam', 'pts')
Inputs may be any that keep to these rules, and one draw needn't show every extreme that they name: `tile_ids`: point tile t of a group (t from 0 to 1535) lists only window tiles from (t * 128) // 1536 to that plus 128; entries at or beyond the tile's count are padding within the same range. `counts`: in every group the first point tile has all 8 entries live.
All inputs are finite; a program needn't handle non-finite values.
Results may differ from a plain program's by a relative error of at most 0.0003.
Values sent between devices are 32-bit elements; how exact they have to be, the bound alone decides.
No kernel may reach another device: no remote copies, remote signals or barrier semaphores. Data moves between devices by JAX's collectives and lax.ppermute only.
A program may use at most 64 MiB of HBM per device.

v0:
```python
import math

import jax
import jax.numpy as jnp
from jax import lax
from jax.sharding import PartitionSpec as P

ITERS = 3


def from_behind(shard, axis, by):
    devices = lax.axis_size(axis)
    return lax.ppermute(shard, axis, [(i, (i + by) % devices) for i in range(devices)])


def point_inverse(pt_jac, counts, damp_pt):
    tiles = pt_jac.shape[0]
    slots = pt_jac.shape[1]
    points = pt_jac.shape[-1]
    live = (lax.iota(jnp.int32, slots)[None, :] < counts[:, None]).astype(jnp.float32)
    shaped = pt_jac.reshape(tiles, slots, 2, 3, points)
    gram = jnp.sum(
        live[:, :, None, None, None, None]
        * shaped[:, :, :, :, None, :]
        * shaped[:, :, :, None, :, :],
        axis=(1, 2),
    )
    gram = gram + damp_pt[:, :, None, :] * jnp.eye(3, dtype=jnp.float32)[None, :, :, None]
    first = jnp.roll(jnp.roll(gram, -1, axis=1), -1, axis=2)
    second = jnp.roll(jnp.roll(gram, -2, axis=1), -2, axis=2)
    mixed_one = jnp.roll(jnp.roll(gram, -1, axis=1), -2, axis=2)
    mixed_two = jnp.roll(jnp.roll(gram, -2, axis=1), -1, axis=2)
    cofactor = first * second - mixed_one * mixed_two
    determinant = jnp.sum(gram[:, 0] * cofactor[:, 0], axis=1)
    return cofactor / determinant[:, None, None, :]


def block_term(window, total, item):
    jac_cam, jac_point, index_cam, index_tile, live_block, inverse_block = item
    blocks, slots, points = index_cam.shape
    cameras = window.shape[1] // 9
    picked_tiles = jnp.take(window, index_tile, axis=0).reshape(blocks, slots, 9, cameras)
    selector = (
        index_cam[:, :, None, :] == lax.iota(jnp.int32, cameras)[None, None, :, None]
    ).astype(jnp.float32)
    picked = jnp.einsum("bsjc,bscp->bsjp", picked_tiles, selector, precision=lax.Precision.HIGHEST)
    cam_rows = jac_cam.reshape(blocks, slots, 2, 9, points)
    point_rows = jac_point.reshape(blocks, slots, 2, 3, points)
    masked = live_block[:, :, None, None]
    residual_rows = jnp.sum(cam_rows * picked[:, :, None], axis=3) * masked
    point_side = jnp.sum(point_rows * residual_rows[:, :, :, None, :], axis=(1, 2))
    solved = jnp.sum(inverse_block * point_side[:, None, :, :], axis=2)
    errors = (residual_rows - jnp.sum(point_rows * solved[:, None, None, :, :], axis=3)) * masked
    returned = jnp.sum(cam_rows * errors[:, :, :, None, :], axis=2)
    spread = jnp.einsum("bsjp,bscp->bsjc", returned, selector, precision=lax.Precision.HIGHEST)
    spread = spread.reshape(blocks * slots, 9 * cameras)
    return total + jax.ops.segment_sum(spread, index_tile.reshape(-1), num_segments=total.shape[0])


def local_product(window, jac_cam, jac_point, index_cam, index_tile, live, inverse):
    tiles = jac_cam.shape[0]
    block = math.gcd(tiles, 8)
    turns = tiles // block

    def split(array):
        return array.reshape((turns, block) + array.shape[1:])

    items = (
        split(jac_cam),
        split(jac_point),
        split(index_cam),
        split(index_tile),
        split(live),
        split(inverse),
    )

    def advance(total, item):
        return (block_term(window, total, item), None)

    total, unused = lax.scan(advance, jnp.zeros(window.shape, jnp.float32), items)
    return total


def camera_product(vector, damp_cam, jac_cam, jac_point, index_cam, index_tile, live, inverse):
    group_tiles = lax.axis_size("pts") * vector.shape[1]
    halfway = group_tiles // 2
    panel = lax.all_gather(vector, "pts", axis=1, tiled=True)
    lower = from_behind(panel, "cam", 1)
    upper = from_behind(panel, "cam", -1)
    window = jnp.concatenate([lower[:, halfway:], panel, upper[:, :halfway]], axis=1)
    partial_value = local_product(
        window[0], jac_cam, jac_point, index_cam, index_tile, live, inverse
    )[None]
    from_above = from_behind(partial_value[:, :halfway], "cam", -1)
    from_below = from_behind(partial_value[:, halfway + group_tiles :], "cam", 1)
    summed = partial_value[:, halfway : halfway + group_tiles] + jnp.concatenate(
        [from_below, from_above], axis=1
    )
    return lax.psum_scatter(summed, "pts", scatter_dimension=1, tiled=True) + damp_cam * vector


def on_device(rhs, damp_cam, precond, cam_jac, pt_jac, damp_pt, cam_index, tile_ids, counts):
    slots = cam_jac.shape[2]
    live = (lax.iota(jnp.int32, slots)[None, :] < counts[0][:, None]).astype(jnp.float32)
    inverse = point_inverse(pt_jac[0], counts[0], damp_pt[0])

    def norm_total(residual, scaled):
        return lax.psum(jnp.sum(residual * scaled), ("pts", "cam"))

    solution = jnp.zeros(rhs.shape, jnp.float32)
    residual = rhs
    scaled = precond * residual
    direction = scaled
    energy = norm_total(residual, scaled)
    for iteration in range(ITERS):
        mapped = camera_product(
            direction, damp_cam, cam_jac[0], pt_jac[0], cam_index[0], tile_ids[0], live, inverse
        )
        step_size = energy / lax.psum(jnp.sum(direction * mapped), ("pts", "cam"))
        solution = solution + step_size * direction
        residual = residual - step_size * mapped
        if iteration + 1 < ITERS:
            scaled = precond * residual
            energy_next = norm_total(residual, scaled)
            direction = scaled + energy_next / energy * direction
            energy = energy_next
    return (solution, residual)


def solution(mesh):
    return jax.shard_map(
        on_device,
        mesh=mesh,
        in_specs=(
            P("cam", "pts", None),
            P("cam", "pts", None),
            P("cam", "pts", None),
            P("cam", "pts", None, None, None),
            P("cam", "pts", None, None, None),
            P("cam", "pts", None, None),
            P("cam", "pts", None, None),
            P("cam", "pts", None),
            P("cam", "pts"),
        ),
        out_specs=(P("cam", "pts", None), P("cam", "pts", None)),
        check_vma=False,
    )
```

profile of v0, /device:TPU:0, one launch (start us, length us, event | category | flops | bytes accessed | tf_op | source)
XLA Modules:
  0.0 936.2 jit_solution(17738219224348371561)
XLA Ops:
  8.0 24.0 %all_gather.9 = f32[1,128,576]{2,1,0:T(8,128)S(1)} all-gather(f32[1,8,576]{2,1,0:T(8,128)S(1)} %mul.381), channel_id=1, replica_groups=mesh['pts'=16,'cam'=2] {'pts'}, dimensions={1}, use_global_device_ids=true | all-gather | bytes 313344 | tf_op jit(solution)/shard_map/all_gather | solution.py:87
  31.9 1.5 collective-permute-start
  34.2 2.0 broadcast_multiply_fusion.3
  36.5 2.3 multiply_reduce_fusion.12
  43.6 105.1 %while.30 = (s32[]{:T(128)}, f32[256,576]{1,0:T(8,128)S(1)}, s32[12,8,8]{2,1,0:T(8,128)S(1)}, f32[12,8,8,18,128]{4,2,3,1,0:T(8,128)}, f32[256,576]{1,0:T(8,128)S...) while((s32[]{:T(128)}, f32[256,576]{1,0:T(8,128)S(1)}, ...), condition=%wide.region_12.14_spmd, body=%wide.region_4.13_spmd.sunk | while | flops 115127872 | bytes 7966729 | solution.py:80
  49.1 1.7 fusion.64
  57.9 1.7 fusion.64
  66.7 1.7 fusion.64
  75.4 1.7 fusion.64
  84.2 1.7 fusion.64
  92.9 1.7 fusion.64
  101.7 1.7 fusion.64
  110.4 1.7 fusion.64
  119.2 1.7 fusion.64
  127.9 1.7 fusion.64
  136.7 1.7 fusion.64
  145.5 1.7 fusion.64
  149.3 1.5 collective-permute-start.2
  150.8 5.0 collective-permute-done.1
  155.8 2.6 collective-permute-done.2
  160.5 83.6 %all-reduce.8.cloned.1.call-done = f32[1,128,576]{2,1,0:T(8,128)} async-done(((f32[1,128,576]{2,1,0:T(8,128)}), f32[1,128,576]{2,1,0:T(8,128)}) %all-reduce.8.cloned.1.call-update) | async-done | bytes 294928
  245.5 41.5 %all-reduce.3 = (f32[]{:T(128)}, f32[]{:T(128)}) all-reduce(f32[]{:T(128)} %get-tuple-element.148, f32[]{:T(128)} %get-tuple-element.147), channel_id=1, replica_groups=mesh['pts'=16,'cam'=2] {'pts','cam'}, use_global_device_ids=true, to_apply=%region_1.2 | all-reduce | flops 2 | bytes 16 | tf_op jit(solution)/shard_map/psum | solution.py:108
  289.7 40.5 %psum.44 = f32[]{:T(128)} all-reduce(f32[]{:T(128)} %get-tuple-element.220), channel_id=1, replica_groups=mesh['pts'=16,'cam'=2] {'pts','cam'}, use_global_device_ids=true, to_apply=%region_17.19 | all-reduce | flops 1 | bytes 8 | tf_op jit(solution)/shard_map/psum | solution.py:108
  331.5 22.3 %all_gather.10 = f32[1,128,576]{2,1,0:T(8,128)S(1)} all-gather(f32[1,8,576]{2,1,0:T(8,128)S(1)} %multiply_add_fusion.3), channel_id=1, replica_groups=mesh['pts'=16,'cam'=2] {'pts'}, dimensions={1}, use_global_device_ids=true | all-gather | bytes 313344 | tf_op jit(solution)/shard_map/all_gather | solution.py:87
  354.5 9.4 %collective-permute-done.3 = f32[1,128,576]{2,1,0:T(8,128)S(1)} collective-permute-done((f32[1,128,576]{2,1,0:T(8,128)S(1)}, f32[1,128,576]{2,1,0:T(8,128)S(1)}, u32[]{:S(2)}, u32[]{:S(2)}) %collective-permute-start.3) | collective-permute-done | bytes 294944 | tf_op jit(solution)/shard_map/ppermute | solution.py:13
  364.0 105.3 %while.31 = (s32[]{:T(128)}, f32[256,576]{1,0:T(8,128)S(1)}, s32[12,8,8]{2,1,0:T(8,128)S(1)}, f32[12,8,8,18,128]{4,2,3,1,0:T(8,128)}, f32[256,576]{1,0:T(8,128)S...) while((s32[]{:T(128)}, f32[256,576]{1,0:T(8,128)S(1)}, ...), condition=%wide.region_26.28_spmd, body=%wide.region_18.27_spmd.sunk | while | flops 115127872 | bytes 7966729 | solution.py:80
  369.5 1.8 fusion.69
  378.3 1.8 fusion.69
  387.1 1.8 fusion.69
  395.8 1.8 fusion.69
  404.6 1.8 fusion.69
  413.4 1.8 fusion.69
  422.2 1.8 fusion.69
  430.9 1.8 fusion.69
  439.7 1.8 fusion.69
  448.5 1.8 fusion.69
  457.3 1.8 fusion.69
  466.0 1.8 fusion.69
  469.9 1.4 collective-permute-start.5
  471.4 5.1 collective-permute-done.4
  476.5 2.0 collective-permute-done.5
  479.4 84.9 %all-reduce.10.cloned.1.call-done = f32[1,128,576]{2,1,0:T(8,128)} async-done(((f32[1,128,576]{2,1,0:T(8,128)}), f32[1,128,576]{2,1,0:T(8,128)}) %all-reduce.10.cloned.1.call-update) | async-done | bytes 294928
  565.7 41.4 %psum.45 = f32[]{:T(128)} all-reduce(f32[]{:T(128)} %multiply_reduce_fusion.15), channel_id=1, replica_groups=mesh['pts'=16,'cam'=2] {'pts','cam'}, use_global_device_ids=true, to_apply=%region_29.31 | all-reduce | flops 1 | bytes 8 | tf_op jit(solution)/shard_map/psum | solution.py:119
  609.9 40.5 %psum.46 = f32[]{:T(128)} all-reduce(f32[]{:T(128)} %get-tuple-element.217), channel_id=1, replica_groups=mesh['pts'=16,'cam'=2] {'pts','cam'}, use_global_device_ids=true, to_apply=%region_31.33 | all-reduce | flops 1 | bytes 8 | tf_op jit(solution)/shard_map/psum | solution.py:108
  651.7 22.2 %all_gather.11 = f32[1,128,576]{2,1,0:T(8,128)S(1)} all-gather(f32[1,8,576]{2,1,0:T(8,128)S(1)} %multiply_add_fusion.2), channel_id=1, replica_groups=mesh['pts'=16,'cam'=2] {'pts'}, dimensions={1}, use_global_device_ids=true | all-gather | bytes 313344 | tf_op jit(solution)/shard_map/all_gather | solution.py:87
  674.5 9.4 %collective-permute-done.6 = f32[1,128,576]{2,1,0:T(8,128)S(1)} collective-permute-done((f32[1,128,576]{2,1,0:T(8,128)S(1)}, f32[1,128,576]{2,1,0:T(8,128)S(1)}, u32[]{:S(2)}, u32[]{:S(2)}) %collective-permute-start.6) | collective-permute-done | bytes 294944 | tf_op jit(solution)/shard_map/ppermute | solution.py:13
  684.0 105.3 %while.32 = (s32[]{:T(128)}, f32[256,576]{1,0:T(8,128)S(1)}, s32[12,8,8]{2,1,0:T(8,128)S(1)}, f32[12,8,8,18,128]{4,2,3,1,0:T(8,128)}, f32[256,576]{1,0:T(8,128)S...) while((s32[]{:T(128)}, f32[256,576]{1,0:T(8,128)S(1)}, ...), condition=%wide.region_40.42_spmd, body=%wide.region_32.41_spmd.sunk | while | flops 115127872 | bytes 7966729 | solution.py:80
  689.5 1.8 fusion.74
  698.3 1.8 fusion.74
  707.1 1.8 fusion.74
  715.9 1.8 fusion.74
  724.6 1.8 fusion.74
  733.4 1.8 fusion.74
  742.2 1.8 fusion.74
  751.0 1.8 fusion.74
  759.7 1.8 fusion.74
  768.5 1.8 fusion.74
  777.3 1.8 fusion.74
  786.1 1.8 fusion.74
  790.0 1.4 collective-permute-start.8
  791.4 5.1 collective-permute-done.7
  796.5 2.0 collective-permute-done.8
  799.3 84.9 %all-reduce.12.cloned.1.call-done = f32[1,128,576]{2,1,0:T(8,128)} async-done(((f32[1,128,576]{2,1,0:T(8,128)}), f32[1,128,576]{2,1,0:T(8,128)}) %all-reduce.12.cloned.1.call-update) | async-done | bytes 294928
  885.6 41.4 %psum.47 = f32[]{:T(128)} all-reduce(f32[]{:T(128)} %multiply_reduce_fusion.13), channel_id=1, replica_groups=mesh['pts'=16,'cam'=2] {'pts','cam'}, use_global_device_ids=true, to_apply=%region_43.45 | all-reduce | flops 1 | bytes 8 | tf_op jit(solution)/shard_map/psum | solution.py:119
  (1004 shorter events, 269.8 us)
Async XLA Ops:
  7.2 237.0 %all-reduce.8.cloned.1.call-start = ((), (), s32[]{:S(2)}) async-start(), calls=%async_computation | async-start | bytes 655360
  31.9 11.5 %collective-permute-start = (f32[1,128,576]{2,1,0:T(8,128)S(1)}, f32[1,128,576]{2,1,0:T(8,128)S(1)}, u32[]{:S(2)}, u32[]{:S(2)}) collective-permute-start(f32[1,128,576]{2,1,0:T(8,128)S(1)} %all_gather.9), channel_id=1, source_target_pairs={{0,1},{1,0},{2,3},{3,2},{4,5},{5,4},{6,7},{7,6},{8,9},{9,8},{10,11... | collective-permute-start | bytes 884744 | tf_op jit(solution)/shard_map/ppermute | solution.py:13
  34.2 2.4 copy-start
  36.5 2.3 copy-start.4
  39.4 1.6 copy-start.6
  39.4 2.5 copy-start.5
  43.5 115.8 %copy-start.7 = (u32[32]{0:T(128)S(1)}, u32[32]{0:T(128)}, u32[]{:S(2)}) copy-start(u32[32]{0:T(128)} %constant.74) | copy-start | bytes 388
  43.6 200.6 %copy-start.1 = (f32[1,8,576]{2,1,0:T(8,128)S(1)}, f32[1,8,576]{2,1,0:T(8,128)}, u32[]{:S(2)}) copy-start(f32[1,8,576]{2,1,0:T(8,128)} %param.18) | copy-start | bytes 55300
  43.6 200.6 %copy-start.3 = (f32[1,8,576]{2,1,0:T(8,128)S(1)}, f32[1,8,576]{2,1,0:T(8,128)}, u32[]{:S(2)}) copy-start(f32[1,8,576]{2,1,0:T(8,128)} %param.17) | copy-start | bytes 55300
  43.6 244.7 %copy-start.2 = (f32[1,8,576]{2,1,0:T(8,128)S(1)}, f32[1,8,576]{2,1,0:T(8,128)}, u32[]{:S(2)}) copy-start(f32[1,8,576]{2,1,0:T(8,128)} %param.19) | copy-start | bytes 55300
  148.7 7.1 collective-permute-start.1
  149.3 9.1 collective-permute-start.2
  159.2 405.0 %all-reduce.10.cloned.1.call-start = ((), (), s32[]{:S(2)}) async-start(), calls=%async_computation.1 | async-start | bytes 655360
  353.9 10.0 %collective-permute-start.3 = (f32[1,128,576]{2,1,0:T(8,128)S(1)}, f32[1,128,576]{2,1,0:T(8,128)S(1)}, u32[]{:S(2)}, u32[]{:S(2)}) collective-permute-start(f32[1,128,576]{2,1,0:T(8,128)S(1)} %all_gather.10), channel_id=1, source_target_pairs={{0,1},{1,0},{2,3},{3,2},{4,5},{5,4},{6,7},{7,6},{8,9},{9,8},{10,11... | collective-permute-start | bytes 884744 | tf_op jit(solution)/shard_map/ppermute | solution.py:13
  469.3 7.2 collective-permute-start.4
  469.9 8.6 collective-permute-start.5
  479.3 404.9 %all-reduce.12.cloned.1.call-start = ((), (), s32[]{:S(2)}) async-start(), calls=%async_computation.2 | async-start | bytes 655360
  673.9 10.0 %collective-permute-start.6 = (f32[1,128,576]{2,1,0:T(8,128)S(1)}, f32[1,128,576]{2,1,0:T(8,128)S(1)}, u32[]{:S(2)}, u32[]{:S(2)}) collective-permute-start(f32[1,128,576]{2,1,0:T(8,128)S(1)} %all_gather.11), channel_id=1, source_target_pairs={{0,1},{1,0},{2,3},{3,2},{4,5},{5,4},{6,7},{7,6},{8,9},{9,8},{10,11... | collective-permute-start | bytes 884744 | tf_op jit(solution)/shard_map/ppermute | solution.py:13
  789.3 7.2 collective-permute-start.7
  790.0 8.6 collective-permute-start.8
Sparse Core Ops, SparseCore 0:
  159.4 84.7 all-reduce.7
  479.4 84.7 all-reduce.9
  799.5 84.7 all-reduce.11
where the time goes:
time: 942 us; the launch traced here: 936 us
  waiting for transfers between devices  294 us (31%)
  blocking collectives  274 us (29%)
  other arithmetic  118 us (13%)
  local copies, waits for them, and re-layouts  113 us (12%)
  matrix products  103 us (11%)
  between operations  21.5 us (2%)
    unnamed x6, waiting for transfers between devices  253 us
    psum x3, blocking collectives, norm_total(): return lax.psum(jnp.sum(residual * scaled), ('pts', 'cam'))  122 us
    psum x2, blocking collectives, on_device(): step_size = energy / lax.psum(jnp.sum(direction * mapped), ('pts', 'cam'))  82.9 us
    all_gather x3, blocking collectives, camera_product(): panel = lax.all_gather(vector, 'pts', axis=1, tiled=True)  68.5 us
    dot_general x36, matrix products, block_term(): jnp.einsum('bsjp,bscp->bsjc', returned, selector, precision=lax.Precision...  62.9 us
    scatter-add x36, other arithmetic, block_term(): jax.ops.segment_sum(spread, index_tile.reshape(-1), num_segments=total.sh...  45.3 us
    ppermute x9, waiting for transfers between devices, from_behind(): lax.ppermute(shard, axis, [(i, (i + by) % devices) for i in range(devices)])  40.7 us
    dot_general x36, matrix products, block_term(): jnp.einsum('bsjc,bscp->bsjp', picked_tiles, selector, precision=lax.Preci...  40.4 us
  transfers between devices with their start and end apart: 12, of which 11 were waited for; matrix products, arithmetic and copies ran while one was open for 1% of the time, Pallas kernels for 0%

commit v1 on v0

v1 whole, which is shorter than its diff:
```python
import functools

import jax
import jax.numpy as jnp
from jax import lax
from jax.experimental import pallas as pl
from jax.experimental.pallas import tpu as pltpu
from jax.sharding import PartitionSpec as P

ITERS = 3
CPAR = 9
CAMERAS = 64
SLOTS = 8
POINTS = 128
TILE = CPAR * CAMERAS
PAIRS = 5
WIDTH = PAIRS * 128
BLOCK = 16
AXES = ("pts", "cam")
VMEM = pltpu.MemorySpace.VMEM


def split_two(value):
    high = value.astype(jnp.bfloat16)
    low = (value - high.astype(jnp.float32)).astype(jnp.bfloat16)
    return high, low


def over_slots(value):
    return jnp.sum(value, axis=0, keepdims=True)


def invert(gram):
    a, b, c, d, e, f = gram
    aa = d * f - e * e
    bb = c * e - b * f
    cc = b * e - c * d
    dd = a * f - c * c
    ee = b * c - a * e
    ff = a * d - b * b
    scale = 1.0 / (a * aa + b * bb + c * cc)
    return [entry * scale for entry in (aa, bb, cc, dd, ee, ff)]


def tile_product(count, cam, point, index, picked_from, row, inverse, damp, put_to):
    slot = lax.broadcasted_iota(jnp.int32, (SLOTS, POINTS), 0)
    lane = lax.broadcasted_iota(jnp.int32, (SLOTS, POINTS), 1)
    live = (slot < count).astype(jnp.float32)
    other = index + CAMERAS
    pairs = [picked_from[pl.ds(row, SLOTS), p * 128 : (p + 1) * 128] for p in range(PAIRS)]
    picked = [
        jnp.take_along_axis(
            pairs[j // 2], other if j % 2 else index, axis=1, mode="promise_in_bounds"
        )
        for j in range(CPAR)
    ]
    rows = [point(r) * live for r in range(6)]
    if inverse is None:
        entries = [(0, 0), (0, 1), (0, 2), (1, 1), (1, 2), (2, 2)]
        gram = [over_slots(rows[i] * rows[j] + rows[3 + i] * rows[3 + j]) for i, j in entries]
        for a, place in enumerate((0, 3, 5)):
            gram[place] = gram[place] + damp[a]
        inverse = invert(gram)
    q = []
    for r in range(2):
        total = cam(9 * r) * picked[0]
        for j in range(1, CPAR):
            total = total + cam(9 * r + j) * picked[j]
        q.append(total * live)
    y = [over_slots(rows[a] * q[0] + rows[3 + a] * q[1]) for a in range(3)]
    i0, i1, i2, i3, i4, i5 = inverse
    z = [
        i0 * y[0] + i1 * y[1] + i2 * y[2],
        i1 * y[0] + i3 * y[1] + i4 * y[2],
        i2 * y[0] + i4 * y[1] + i5 * y[2],
    ]
    e = [
        (q[r] - (rows[3 * r] * z[0] + rows[3 * r + 1] * z[1] + rows[3 * r + 2] * z[2])) * live
        for r in range(2)
    ]
    slot_twice = lax.broadcasted_iota(jnp.int32, (2 * SLOTS, POINTS), 0) & 1
    odd = slot_twice.astype(jnp.bfloat16)
    even = (1 - slot_twice).astype(jnp.bfloat16)
    left = []
    for j in range(CPAR):
        returned = cam(j) * e[0] + cam(9 + j) * e[1]
        high = returned.astype(jnp.bfloat16).astype(jnp.float32)
        both = jnp.concatenate([high, returned - high], axis=0).astype(jnp.bfloat16)
        left.append(jnp.concatenate([both * even, both * odd], axis=1))
    left = jnp.concatenate(left, axis=0)
    camera = lax.broadcasted_iota(jnp.int32, (CAMERAS, POINTS), 0)
    selector = []
    for pair in range(SLOTS // 2):
        halves = [
            (camera == index[k : k + 1, :]).astype(jnp.float32).astype(jnp.bfloat16)
            for k in (2 * pair, 2 * pair + 1)
        ]
        selector.append(jnp.concatenate(halves, axis=1))
    selector = jnp.concatenate(selector, axis=0)
    spread = lax.dot_general(
        left, selector, (((1,), (1,)), ((), ())), preferred_element_type=jnp.float32
    )
    side = (slot >> 1) & 1
    first_side = side == 0
    keep = (lane >> 6) == side
    sums = []
    for j in range(CPAR):
        both = spread[16 * j : 16 * j + 8] + spread[16 * j + 8 : 16 * j + 16]
        sums.append(jnp.where(slot < 4, both[:, :128], both[:, 128:]))
    sums.append(jnp.zeros_like(sums[0]))
    for p in range(PAIRS):
        one, two = sums[2 * p], sums[2 * p + 1]
        stay = jnp.where(first_side, one, two)
        move = pltpu.roll(jnp.where(first_side, two, one), CAMERAS, 1)
        put_to[pl.ds(row, SLOTS), p * 128 : (p + 1) * 128] = jnp.where(keep, stay, move)
    return q[0] * e[0] + q[1] * e[1], inverse


def product_steps(counts, cam, point, index, extra, pick, put, vector, out, inverse_out, dot, picked_from, put_to, before, after):
    step = pl.program_id(0)
    block = cam.shape[0]
    first = inverse_out is not None

    @pl.when(step == 0)
    def _():
        before()
        high, low = split_two(vector[...])
        picked_from[...] = jnp.dot(
            pick[...], high, preferred_element_type=jnp.float32
        ) + jnp.dot(pick[...], low, preferred_element_type=jnp.float32)
        dot[...] = jnp.zeros_like(dot)

    def advance(i, total):
        tile = step * block + i
        rows = [extra[a, pl.ds(i, 1), :] for a in range(extra.shape[0])]
        term, inverse = tile_product(
            counts[tile],
            lambda r: cam[i, r],
            lambda r: point[i, r],
            index[i],
            picked_from,
            pl.multiple_of(tile * SLOTS, SLOTS),
            None if first else rows,
            rows,
            put_to,
        )
        if first:
            for a in range(6):
                inverse_out[a, pl.ds(i, 1), :] = inverse[a]
        return total + term

    dot[...] += lax.fori_loop(0, block, advance, jnp.zeros(dot.shape, jnp.float32), unroll=True)

    @pl.when(step == pl.num_programs(0) - 1)
    def _():
        high, low = split_two(put_to[...])
        out[...] = jnp.dot(put[...], high, preferred_element_type=jnp.float32) + jnp.dot(
            put[...], low, preferred_element_type=jnp.float32
        )
        after()


def total_of(value):
    return jnp.sum(value, keepdims=True).reshape(1, 1)


def finish(place, damp, vector, out, dot):
    rows = damp.shape[0]
    own = pl.ds(pl.multiple_of(place[0] * rows, rows), rows)
    damped = damp[...] * vector[own, :]
    out[own, :] += damped
    part = total_of(dot[...]) + total_of(damped * vector[own, :])
    lane = lax.broadcasted_iota(jnp.int32, (out.shape[0], 128), 1)
    out[:, WIDTH - 128 :] += jnp.where(lane >= TILE - (WIDTH - 128), part, 0.0)


def first_kernel(ranks, counts, place, cam, point, index, extra, pick, put, damp, *refs):
    pieces, (out, inverse, residual, scaling, vector, energy, dot, picked_from, put_to) = refs[:ranks], refs[ranks:]

    def before():
        ring, _, rows, _ = pieces[0].shape
        for r in range(ranks):
            for away in range(ring):
                at = pl.multiple_of((r * ring + (away ^ place[0])) * rows, rows)
                residual[pl.ds(at, rows), :] = pieces[r][away, 0]
                scaling[pl.ds(at, rows), :] = pieces[r][away, 1]
        scaled = residual[...] * scaling[...]
        vector[...] = scaled
        energy[...] = jnp.broadcast_to(total_of(scaled * residual[...]), energy.shape)

    product_steps(
        counts, cam, point, index, extra, pick, put, vector, out, inverse, dot, picked_from, put_to, before,
        lambda: finish(place, damp, vector, out, dot),
    )


def next_kernel(ranks, counts, place, cam, point, index, extra, pick, put, damp, *refs):
    pieces = refs[:ranks]
    old_residual, scaling, old_vector, old_energy, old_answer = refs[ranks : ranks + 5]
    out, residual, vector, energy, answer, dot, picked_from, put_to = refs[ranks + 5 :]

    def before():
        many = pieces[0].shape[0]
        rows = damp.shape[0]
        step_size = old_energy[0:1, 0:1] / pieces[0][0:1, TILE : TILE + 1]
        own = pl.ds(pl.multiple_of(place[0] * rows, rows), rows)
        answer[...] = old_answer[...] + step_size * old_vector[own, :]
        power = jnp.zeros((1, 1), jnp.float32)
        for r in range(ranks):
            part = slice(r * many, (r + 1) * many)
            left = old_residual[part, :] - step_size * pieces[r][...]
            residual[part, :] = left
            scaled = scaling[part, :] * left
            vector[part, :] = scaled
            power = power + total_of(scaled * left)
        vector[...] += (power / old_energy[0:1, 0:1]) * old_vector[...]
        energy[...] = jnp.broadcast_to(power, energy.shape)

    product_steps(
        counts, cam, point, index, extra, pick, put, vector, out, None, dot, picked_from, put_to, before,
        lambda: finish(place, damp, vector, out, dot),
    )


def plain_kernel(counts, cam, point, index, extra, pick, put, vector, out, inverse, dot, picked_from, put_to):
    product_steps(
        counts, cam, point, index, extra, pick, put, vector, out, inverse, dot, picked_from, put_to,
        lambda: None, lambda: None,
    )


def last_kernel(place, piece, old_residual, old_vector, energy, old_answer, answer, residual):
    rows = old_answer.shape[0]
    step_size = energy[0:1, 0:1] / piece[0:1, TILE : TILE + 1]
    own = pl.ds(pl.multiple_of(place[0] * rows, rows), rows)
    answer[0] = (old_answer[...] + step_size * old_vector[own, :])[:, :TILE]
    residual[0] = (old_residual[own, :] - step_size * piece[own, :])[:, :TILE]


def whole(shape):
    return pl.BlockSpec(shape, lambda s, *refs: (0,) * len(shape))


def call_product(kernel, scalars, problem, extra, tables, others, outs):
    cam, point, index = problem
    tiles = cam.shape[0]
    block = BLOCK if tiles % BLOCK == 0 else tiles
    in_specs = [
        pl.BlockSpec((block,) + cam.shape[1:], lambda s, *refs: (s, 0, 0, 0)),
        pl.BlockSpec((block,) + point.shape[1:], lambda s, *refs: (s, 0, 0, 0)),
        pl.BlockSpec((block,) + index.shape[1:], lambda s, *refs: (s, 0, 0)),
        pl.BlockSpec((extra.shape[0], block, POINTS), lambda s, *refs: (0, s, 0)),
    ]
    in_specs += [whole(array.shape) for array in tables + others]
    out_specs = [
        pl.BlockSpec((shape[0], block, shape[2]), lambda s, *refs: (0, s, 0)) if split else whole(shape)
        for shape, split in outs
    ]
    scratch = pltpu.VMEM((tiles * SLOTS, WIDTH), jnp.float32)
    return pl.pallas_call(
        kernel,
        out_shape=[jax.ShapeDtypeStruct(shape, jnp.float32) for shape, split in outs],
        grid_spec=pltpu.PrefetchScalarGridSpec(
            num_scalar_prefetch=len(scalars),
            grid=(tiles // block,),
            in_specs=in_specs,
            out_specs=out_specs,
            scratch_shapes=[pltpu.VMEM((8, 128), jnp.float32), scratch, scratch],
        ),
        compiler_params=pltpu.CompilerParams(
            vmem_limit_bytes=32 * 2**20, dimension_semantics=("arbitrary",)
        ),
    )(*scalars, cam, point, index, extra, *tables, *others)


def tables_of(rows, window):
    listed = rows.reshape(-1)
    places = lax.iota(jnp.int32, window)
    pick = (listed[:, None] == places[None, :]).astype(jnp.bfloat16)
    put = (places[:, None] == listed[None, :]).astype(jnp.bfloat16)
    return [pick, put]


def widen(array):
    return jnp.pad(array, [(0, 0)] * (array.ndim - 1) + [(0, WIDTH - TILE)])


def exchange(array, mask):
    devices = lax.axis_size("pts") * lax.axis_size("cam")
    return lax.ppermute(array, AXES, [(i, i ^ mask) for i in range(devices)])


def two_groups(rhs, damp_cam, precond, problem, damp_point, tile_ids, counts):
    CAM, CORE, Y = 1, 2, 4
    shards = lax.axis_size("pts")
    tiles = rhs.shape[0]
    ring = shards // 4
    group, shard = lax.axis_index("cam"), lax.axis_index("pts")
    group_tiles = shards * tiles
    window = 2 * group_tiles
    place = (shard >> 2).reshape(1)
    where = (group * group_tiles + tile_ids - group_tiles // 2) % window
    owner_group, owner = where // group_tiles, where % group_tiles // tiles
    apart = owner ^ shard
    rank = (apart & 1) * 4 + (owner_group ^ group) * 2 + ((apart >> 1) & 1)
    tables = tables_of((rank * ring + (owner >> 2)) * tiles + where % tiles, window)
    scalars = [counts, place]
    damp = widen(damp_cam)

    def gather(own):
        near = [own, exchange(own, Y), exchange(own, CAM), exchange(own, CAM | Y)]
        return near + [exchange(piece, CORE) for piece in near]

    def reduce(partial):
        half = window // 2
        mine = partial[:half] + exchange(partial[half:], CORE)
        part = half // 4
        mine = (
            mine[:part]
            + exchange(mine[part : 2 * part], Y)
            + exchange(mine[2 * part : 3 * part], CAM)
            + exchange(mine[3 * part :], CAM | Y)
        )
        away = 1
        while away < ring:
            mine = mine + exchange(mine, 8 * away)
            away *= 2
        return mine

    both = widen(jnp.stack([rhs, precond]))[None]
    away = 1
    while away < ring:
        both = jnp.concatenate([both, exchange(both, 8 * away)], axis=0)
        away *= 2
    pieces = gather(both)
    full, small, own = (window, WIDTH), (8, 128), (tiles, WIDTH)
    inverse_shape = (6, problem[0].shape[0], POINTS)
    partial, inverse, residual, scaling, vector, energy = call_product(
        functools.partial(first_kernel, 8), scalars, problem, damp_point, tables, [damp] + pieces,
        [(full, 0), (inverse_shape, 1), (full, 0), (full, 0), (full, 0), (small, 0)],
    )
    answer = jnp.zeros(own, jnp.float32)
    for iteration in range(1, ITERS):
        pieces = gather(reduce(partial))
        partial, residual, vector, energy, answer = call_product(
            functools.partial(next_kernel, 8), scalars, problem, inverse, tables,
            [damp] + pieces + [residual, scaling, vector, energy, answer],
            [(full, 0), (full, 0), (full, 0), (small, 0), (own, 0)],
        )
    mine = reduce(partial)
    return pl.pallas_call(
        last_kernel,
        out_shape=[jax.ShapeDtypeStruct((1, tiles, TILE), jnp.float32)] * 2,
        in_specs=[pl.BlockSpec(memory_space=pltpu.SMEM)] + [pl.BlockSpec(memory_space=VMEM)] * 5,
    )(place, mine, residual[: mine.shape[0]], vector[: mine.shape[0]], energy, answer)


def from_behind(shard, axis, by):
    devices = lax.axis_size(axis)
    return lax.ppermute(shard, axis, [(i, (i + by) % devices) for i in range(devices)])


def many_groups(rhs, damp_cam, precond, problem, damp_point, tile_ids, counts):
    group_tiles = lax.axis_size("pts") * rhs.shape[0]
    halfway = group_tiles // 2
    window = 2 * group_tiles
    tables = tables_of(tile_ids, window)
    inverse_shape = (6, problem[0].shape[0], POINTS)

    def product(vector):
        panel = lax.all_gather(widen(vector), "pts", axis=0, tiled=True)
        lower = from_behind(panel[halfway:], "cam", 1)
        upper = from_behind(panel[:halfway], "cam", -1)
        whole_window = jnp.concatenate([lower, panel, upper], axis=0)
        partial = call_product(
            plain_kernel, [counts], problem, damp_point, tables, [whole_window],
            [((window, WIDTH), 0), (inverse_shape, 1)],
        )[0]
        from_above = from_behind(partial[:halfway], "cam", -1)
        from_below = from_behind(partial[halfway + group_tiles :], "cam", 1)
        summed = partial[halfway : halfway + group_tiles] + jnp.concatenate(
            [from_below, from_above], axis=0
        )
        return lax.psum_scatter(summed, "pts", scatter_dimension=0, tiled=True)[:, :TILE] + damp_cam * vector

    def inner(one, two):
        return lax.psum(jnp.sum(one * two), AXES)

    answer, residual = jnp.zeros(rhs.shape, jnp.float32), rhs
    scaled = precond * residual
    direction = scaled
    energy = inner(residual, scaled)
    for iteration in range(ITERS):
        mapped = product(direction)
        step_size = energy / inner(direction, mapped)
        answer = answer + step_size * direction
        residual = residual - step_size * mapped
        scaled = precond * residual
        energy_next = inner(residual, scaled)
        direction = scaled + energy_next / energy * direction
        energy = energy_next
    return answer[None], residual[None]


def on_device(rhs, damp_cam, precond, cam_jac, pt_jac, damp_pt, cam_index, tile_ids, counts):
    problem = (
        jnp.transpose(cam_jac[0], (0, 2, 1, 3)),
        jnp.transpose(pt_jac[0], (0, 2, 1, 3)),
        cam_index[0],
    )
    groups, shards = lax.axis_size("cam"), lax.axis_size("pts")
    plan = two_groups if groups == 2 and shards in (4, 8, 16, 32) else many_groups
    outputs = plan(
        rhs[0], damp_cam[0], precond[0], problem, jnp.transpose(damp_pt[0], (1, 0, 2)), tile_ids[0], counts[0]
    )
    return tuple(outputs)


def solution(mesh):
    return jax.shard_map(
        on_device,
        mesh=mesh,
        in_specs=(
            P("cam", "pts", None),
            P("cam", "pts", None),
            P("cam", "pts", None),
            P("cam", "pts", None, None, None),
            P("cam", "pts", None, None, None),
            P("cam", "pts", None, None),
            P("cam", "pts", None, None),
            P("cam", "pts", None),
            P("cam", "pts"),
        ),
        out_specs=(P("cam", "pts", None), P("cam", "pts", None)),
        check_vma=False,
    )
```

time: 942 us -> 137 us (0.15)
  blocking collectives: 274 us -> 0 us
  waiting for transfers between devices: 294 us -> 48.1 us
  other arithmetic: 118 us -> 2.6 us
  local copies, waits for them, and re-layouts: 113 us -> 9.59 us
  matrix products: 103 us -> 0 us
  starting transfers between devices: 9.05 us -> 44.2 us
  Pallas kernels: 0 us -> 31.1 us
  between operations: 21.5 us -> 0.85 us
    unnamed x6 -> x0, waiting for transfers between devices: 253 us -> none
    psum x5 -> x0, blocking collectives: 205 us -> none  [the longest x3 122 us: norm_total(): return lax.psum(jnp.sum(residual * scaled), ('pts', 'cam'))]
    dot_general x72 -> x0, matrix products: 103 us -> none  [the longest x36 62.9 us: block_term(): jnp.einsum('bsjp,bscp->bsjc', returned, selector, precision=lax.Precision...]
    all_gather x3 -> x0, blocking collectives: 68.5 us -> none  [camera_product(): panel = lax.all_gather(vector, 'pts', axis=1, tiled=True)]
    reduce_sum x223 -> x0, other arithmetic: 52.3 us -> none  [the longest x72 36.1 us: block_term(): jnp.sum(point_rows * residual_rows[:, :, :, None, :], axis=(1, 2))]
    scatter-add x36 -> x0, other arithmetic: 45.3 us -> none  [block_term(): jax.ops.segment_sum(spread, index_tile.reshape(-1), num_segments=total.sh...]
    dynamic_slice x36 -> x0, local copies, waits for them, and re-layouts: 39.9 us -> none  [local_product(): lax.scan(advance, jnp.zeros(window.shape, jnp.float32), items)]
    ppermute x9 -> x41, starting transfers between devices: 8.93 us -> 44.2 us  [exchange(): return lax.ppermute(array, AXES, [(i, i ^ mask) for i in range(devices)])]
  transfers between devices with their start and end apart: 12 -> 41, of which waited for: 11 -> 35; matrix products, arithmetic and copies ran while one was open for 1% -> 2% of each run, Pallas kernels for 0% -> 0%
where the time goes in v1:
time: 137 us; the launch traced here: 136 us
  waiting for transfers between devices  48.1 us (35%)
  starting transfers between devices  44.2 us (32%)
  Pallas kernels  31.1 us (23%)
  local copies, waits for them, and re-layouts  9.59 us (7%)
  other arithmetic  2.6 us (2%)
    ppermute x41, waiting for transfers between devices, exchange(): return lax.ppermute(array, AXES, [(i, i ^ mask) for i in range(devices)])  48.1 us
    ppermute x41, starting transfers between devices, exchange(): return lax.ppermute(array, AXES, [(i, i ^ mask) for i in range(devices)])  44.2 us
    pallas_call x3, Pallas kernels, call_product(): pl.pallas_call(kernel, out_shape=[jax.ShapeDtypeStruct(shape, jnp.float32...  29.5 us
    unnamed x14, local copies, waits for them, and re-layouts  7.24 us
  transfers between devices with their start and end apart: 41, of which 35 were waited for; matrix products, arithmetic and copies ran while one was open for 2% of the time, Pallas kernels for 0%

profile of v1, /device:TPU:0, one launch (start us, length us, event | category | flops | bytes accessed | tf_op | source)
XLA Modules:
  0.0 136.5 jit_solution(4775197126939093398)
XLA Ops:
  0.6 0.8 fusion.8
  1.4 3.0 %collective-permute-start = (f32[1,2,8,640]{3,2,1,0:T(8,128)S(1)}, f32[1,2,8,640]{3,2,1,0:T(8,128)S(1)}, u32[]{:S(2)}, u32[]{:S(2)}) collective-permute-start(f32[1,2,8,640]{3,2,1,0:T(8,128)S(1)} %fusion.8), channel_id=1, source_target_pairs={{0,8},{1,9},{2,10},{3,11},{4,12},{5,13},{6,14},{7,15},{8,0},{9,1},... | collective-permute-start | bytes 122888 | tf_op jit(solution)/shard_map/ppermute | solution.py:290
  4.4 0.7 add_add_fusion
  5.3 1.1 collective-permute-done
  6.4 3.0 %collective-permute-start.1 = (f32[2,2,8,640]{3,2,1,0:T(8,128)S(1)}, f32[2,2,8,640]{3,2,1,0:T(8,128)S(1)}, u32[]{:S(2)}, u32[]{:S(2)}) collective-permute-start(f32[2,2,8,640]{3,2,1,0:T(8,128)S(1)} %pad_maximum_fusion.1), channel_id=1, source_target_pairs={{0,16},{1,17},{2,18},{3,19},{4,20},{5,21},{6,22},{7,23},{8,24},{9,... | collective-permute-start | bytes 245768 | tf_op jit(solution)/shard_map/ppermute | solution.py:290
  9.5 0.7 pad.8.damp
  10.2 1.6 %collective-permute-done.1 = f32[2,2,8,640]{3,2,1,0:T(8,128)S(1)} collective-permute-done((f32[2,2,8,640]{3,2,1,0:T(8,128)S(1)}, f32[2,2,8,640]{3,2,1,0:T(8,128)S(1)}, u32[]{:S(2)}, u32[]{:S(2)}) %collective-permute-start.1) | collective-permute-done | bytes 81952 | tf_op jit(solution)/shard_map/ppermute | solution.py:290
  11.9 2.8 %collective-permute-start.4 = (f32[4,2,8,640]{3,2,1,0:T(8,128)S(1)}, f32[4,2,8,640]{3,2,1,0:T(8,128)S(1)}, u32[]{:S(2)}, u32[]{:S(2)}) collective-permute-start(f32[4,2,8,640]{3,2,1,0:T(8,128)S(1)} %pad_maximum_fusion.refs_0_), channel_id=1, source_target_pairs={{0,5},{1,4},{2,7},{3,6},{4,1},{5,0},{6,3},{7,2},{8,13},{9,12},{10,... | collective-permute-start | bytes 491528 | tf_op jit(solution)/shard_map/ppermute | solution.py:290
  15.6 2.9 %collective-permute-done.4.refs_3_ = f32[4,2,8,640]{3,2,1,0:T(8,128)S(1)} collective-permute-done((f32[4,2,8,640]{3,2,1,0:T(8,128)S(1)}, f32[4,2,8,640]{3,2,1,0:T(8,128)S(1)}, u32[]{:S(2)}, u32[]{:S(2)}) %collective-permute-start.4) | collective-permute-done | bytes 163872 | tf_op jit(solution)/shard_map/ppermute | solution.py:290
  18.5 1.9 %collective-permute-done.3.refs_2_ = f32[4,2,8,640]{3,2,1,0:T(8,128)S(1)} collective-permute-done((f32[4,2,8,640]{3,2,1,0:T(8,128)S(1)}, f32[4,2,8,640]{3,2,1,0:T(8,128)S(1)}, u32[]{:S(2)}, u32[]{:S(2)}) %collective-permute-start.3) | collective-permute-done | bytes 163872 | tf_op jit(solution)/shard_map/ppermute | solution.py:290
  21.1 0.7 collective-permute-done.7.refs_6_
  22.0 3.0 %copy-done = f32[1,96,8,18,128]{4,2,3,1,0:T(8,128)S(1)} copy-done((f32[1,96,8,18,128]{4,2,3,1,0:T(8,128)S(1)}, f32[1,96,8,18,128]{4,2,3,1,0:T(8,128)}, u32[]{:S(2)}) %copy-start) | copy-done | bytes 7077912
  25.0 1.7 %copy-done.1 = f32[1,96,8,6,128]{4,2,3,1,0:T(8,128)S(1)} copy-done((f32[1,96,8,6,128]{4,2,3,1,0:T(8,128)S(1)}, f32[1,96,8,6,128]{4,2,3,1,0:T(8,128)}, u32[]{:S(2)}) %copy-start.1) | copy-done | bytes 2359320
  26.7 1.0 copy-done.2
  27.7 0.9 copy-done.3
  28.6 0.7 copy-done.5
  29.2 10.3 %shard_map.104 = (f32[256,640]{1,0:T(8,128)S(1)}, f32[6,96,128]{2,1,0:T(8,128)S(1)}, f32[256,640]{1,0:T(8,128)S(1)}, f32[256,640]{1,0:T(8,128)S(1)}, f32[256,640]{1,0:T(8,128)S(1)}, /*index=5*/f32[8,128]{1,0:T(8,128)S(1)}) custom-call(s32[96]{0:T(128)S(1)} %bitcast.25, s32[1]{0:T(128)} %bitcast.place, f32[96,18,8,128]{3,2,1,0:T(8,128)S(1)} %bitcast.15, ...), custom_call_target="tpu_custom_call" | custom-call | tf_op jit(solution)/shard_map/pallas_call | solution.py:260
  39.9 1.4 collective-permute-done.9
  41.3 1.3 collective-permute-start.10
  42.6 1.7 %collective-permute-start.12 = (f32[32,640]{1,0:T(8,128)S(1)}, f32[32,640]{1,0:T(8,128)S(1)}, u32[]{:S(2)}, u32[]{:S(2)}) collective-permute-start(f32[32,640]{1,0:T(8,128)S(1)} %get-tuple-element.41), channel_id=1, source_target_pairs={{0,5},{1,4},{2,7},{3,6},{4,1},{5,0},{6,3},{7,2},{8,13},{9,12},{10,... | collective-permute-start | bytes 245768 | tf_op jit(solution)/shard_map/ppermute | solution.py:290
  44.9 1.1 collective-permute-done.10
  46.0 2.7 %collective-permute-done.12 = f32[32,640]{1,0:T(8,128)S(1)} collective-permute-done((f32[32,640]{1,0:T(8,128)S(1)}, f32[32,640]{1,0:T(8,128)S(1)}, u32[]{:S(2)}, u32[]{:S(2)}) %collective-permute-start.12) | collective-permute-done | bytes 81952 | tf_op jit(solution)/shard_map/ppermute | solution.py:290
  49.1 1.9 %collective-permute-start.13 = (f32[32,640]{1,0:T(8,128)S(1)}, f32[32,640]{1,0:T(8,128)S(1)}, u32[]{:S(2)}, u32[]{:S(2)}) collective-permute-start(f32[32,640]{1,0:T(8,128)S(1)} %fusion.7), channel_id=1, source_target_pairs={{0,8},{1,9},{2,10},{3,11},{4,12},{5,13},{6,14},{7,15},{8,0},{9,1},... | collective-permute-start | bytes 245768 | tf_op jit(solution)/shard_map/ppermute | solution.py:290
  51.0 2.6 %collective-permute-done.13 = f32[32,640]{1,0:T(8,128)S(1)} collective-permute-done((f32[32,640]{1,0:T(8,128)S(1)}, f32[32,640]{1,0:T(8,128)S(1)}, u32[]{:S(2)}, u32[]{:S(2)}) %collective-permute-start.13) | collective-permute-done | bytes 81952 | tf_op jit(solution)/shard_map/ppermute | solution.py:290
  53.6 3.0 %collective-permute-start.14 = (f32[32,640]{1,0:T(8,128)S(1)}, f32[32,640]{1,0:T(8,128)S(1)}, u32[]{:S(2)}, u32[]{:S(2)}) collective-permute-start(f32[32,640]{1,0:T(8,128)S(1)} %add.196), channel_id=1, source_target_pairs={{0,16},{1,17},{2,18},{3,19},{4,20},{5,21},{6,22},{7,23},{8,24},{9,... | collective-permute-start | bytes 245768 | tf_op jit(solution)/shard_map/ppermute | solution.py:290
  56.6 2.4 %collective-permute-done.14 = f32[32,640]{1,0:T(8,128)S(1)} collective-permute-done((f32[32,640]{1,0:T(8,128)S(1)}, f32[32,640]{1,0:T(8,128)S(1)}, u32[]{:S(2)}, u32[]{:S(2)}) %collective-permute-start.14) | collective-permute-done | bytes 81952 | tf_op jit(solution)/shard_map/ppermute | solution.py:290
  59.0 2.0 %collective-permute-start.17 = (f32[32,640]{1,0:T(8,128)S(1)}, f32[32,640]{1,0:T(8,128)S(1)}, u32[]{:S(2)}, u32[]{:S(2)}) collective-permute-start(f32[32,640]{1,0:T(8,128)S(1)} %add.197.refs_0_), channel_id=1, source_target_pairs={{0,5},{1,4},{2,7},{3,6},{4,1},{5,0},{6,3},{7,2},{8,13},{9,12},{10,... | collective-permute-start | bytes 245768 | tf_op jit(solution)/shard_map/ppermute | solution.py:290
  61.0 0.8 collective-permute-start.16
  61.8 0.8 collective-permute-start.15
  62.6 1.8 %collective-permute-done.17.refs_3_ = f32[32,640]{1,0:T(8,128)S(1)} collective-permute-done((f32[32,640]{1,0:T(8,128)S(1)}, f32[32,640]{1,0:T(8,128)S(1)}, u32[]{:S(2)}, u32[]{:S(2)}) %collective-permute-start.17) | collective-permute-done | bytes 81952 | tf_op jit(solution)/shard_map/ppermute | solution.py:290
  64.4 1.0 collective-permute-done.16.refs_2_
  65.4 0.8 collective-permute-done.15.refs_1_
  66.7 0.8 collective-permute-done.19.refs_5_
  67.5 9.6 %shard_map.105 = (f32[256,640]{1,0:T(8,128)S(1)}, f32[256,640]{1,0:T(8,128)S(1)}, f32[256,640]{1,0:T(8,128)S(1)}, f32[8,128]{1,0:T(8,128)S(1)}, f32[8,640]{1,0:T(8,128)S(1)}) custom-call(s32[96]{0:T(128)S(1)} %bitcast.26, s32[1]{0:T(128)} %bitcast.place, f32[96,18,8,128]{3,2,1,0:T(8,128)S(1)} %bitcast.16, f32[96,6,8,128]{3,2,1,0:T(8,128)S(1)} %bitcast.19, ...), custom_call_target="tpu_custom_call" | custom-call | tf_op jit(solution)/shard_map/pallas_call | solution.py:260
  77.3 1.5 %collective-permute-done.22 = f32[128,640]{1,0:T(8,128)S(1)} collective-permute-done((f32[128,640]{1,0:T(8,128)S(1)}, f32[128,640]{1,0:T(8,128)S(1)}, u32[]{:S(2)}, u32[]{:S(2)}) %collective-permute-start.22) | collective-permute-done | bytes 327712 | tf_op jit(solution)/shard_map/ppermute | solution.py:290
  78.9 0.9 collective-permute-start.23
  79.7 1.9 %collective-permute-start.25 = (f32[32,640]{1,0:T(8,128)S(1)}, f32[32,640]{1,0:T(8,128)S(1)}, u32[]{:S(2)}, u32[]{:S(2)}) collective-permute-start(f32[32,640]{1,0:T(8,128)S(1)} %get-tuple-element.38), channel_id=1, source_target_pairs={{0,5},{1,4},{2,7},{3,6},{4,1},{5,0},{6,3},{7,2},{8,13},{9,12},{10,... | collective-permute-start | bytes 245768 | tf_op jit(solution)/shard_map/ppermute | solution.py:290
  81.7 0.8 collective-permute-start.24
  82.4 2.0 %collective-permute-done.23 = f32[32,640]{1,0:T(8,128)S(1)} collective-permute-done((f32[32,640]{1,0:T(8,128)S(1)}, f32[32,640]{1,0:T(8,128)S(1)}, u32[]{:S(2)}, u32[]{:S(2)}) %collective-permute-start.23) | collective-permute-done | bytes 81952 | tf_op jit(solution)/shard_map/ppermute | solution.py:290
  84.4 1.5 %collective-permute-done.25 = f32[32,640]{1,0:T(8,128)S(1)} collective-permute-done((f32[32,640]{1,0:T(8,128)S(1)}, f32[32,640]{1,0:T(8,128)S(1)}, u32[]{:S(2)}, u32[]{:S(2)}) %collective-permute-start.25) | collective-permute-done | bytes 81952 | tf_op jit(solution)/shard_map/ppermute | solution.py:290
  86.5 2.1 %collective-permute-start.26 = (f32[32,640]{1,0:T(8,128)S(1)}, f32[32,640]{1,0:T(8,128)S(1)}, u32[]{:S(2)}, u32[]{:S(2)}) collective-permute-start(f32[32,640]{1,0:T(8,128)S(1)} %fusion.5), channel_id=1, source_target_pairs={{0,8},{1,9},{2,10},{3,11},{4,12},{5,13},{6,14},{7,15},{8,0},{9,1},... | collective-permute-start | bytes 245768 | tf_op jit(solution)/shard_map/ppermute | solution.py:290
  88.6 2.4 %collective-permute-done.26 = f32[32,640]{1,0:T(8,128)S(1)} collective-permute-done((f32[32,640]{1,0:T(8,128)S(1)}, f32[32,640]{1,0:T(8,128)S(1)}, u32[]{:S(2)}, u32[]{:S(2)}) %collective-permute-start.26) | collective-permute-done | bytes 81952 | tf_op jit(solution)/shard_map/ppermute | solution.py:290
  91.0 3.3 %collective-permute-start.27 = (f32[32,640]{1,0:T(8,128)S(1)}, f32[32,640]{1,0:T(8,128)S(1)}, u32[]{:S(2)}, u32[]{:S(2)}) collective-permute-start(f32[32,640]{1,0:T(8,128)S(1)} %add.202), channel_id=1, source_target_pairs={{0,16},{1,17},{2,18},{3,19},{4,20},{5,21},{6,22},{7,23},{8,24},{9,... | collective-permute-start | bytes 245768 | tf_op jit(solution)/shard_map/ppermute | solution.py:290
  94.3 2.4 %collective-permute-done.27 = f32[32,640]{1,0:T(8,128)S(1)} collective-permute-done((f32[32,640]{1,0:T(8,128)S(1)}, f32[32,640]{1,0:T(8,128)S(1)}, u32[]{:S(2)}, u32[]{:S(2)}) %collective-permute-start.27) | collective-permute-done | bytes 81952 | tf_op jit(solution)/shard_map/ppermute | solution.py:290
  96.8 1.6 %collective-permute-start.30 = (f32[32,640]{1,0:T(8,128)S(1)}, f32[32,640]{1,0:T(8,128)S(1)}, u32[]{:S(2)}, u32[]{:S(2)}) collective-permute-start(f32[32,640]{1,0:T(8,128)S(1)} %add.203.refs_0_), channel_id=1, source_target_pairs={{0,5},{1,4},{2,7},{3,6},{4,1},{5,0},{6,3},{7,2},{8,13},{9,12},{10,... | collective-permute-start | bytes 245768 | tf_op jit(solution)/shard_map/ppermute | solution.py:290
  98.3 0.9 collective-permute-start.29
  99.2 1.1 collective-permute-start.28
  100.3 1.8 %collective-permute-done.30.refs_3_ = f32[32,640]{1,0:T(8,128)S(1)} collective-permute-done((f32[32,640]{1,0:T(8,128)S(1)}, f32[32,640]{1,0:T(8,128)S(1)}, u32[]{:S(2)}, u32[]{:S(2)}) %collective-permute-start.30) | collective-permute-done | bytes 81952 | tf_op jit(solution)/shard_map/ppermute | solution.py:290
  102.8 0.9 collective-permute-done.28.refs_1_
  104.1 0.9 collective-permute-done.32.refs_5_
  104.9 9.6 %shard_map.106 = (f32[256,640]{1,0:T(8,128)S(1)}, f32[256,640]{1,0:T(8,128)S(1)}, f32[256,640]{1,0:T(8,128)S(1)}, f32[8,128]{1,0:T(8,128)S(1)}, f32[8,640]{1,0:T(8,128)S(1)}) custom-call(s32[96]{0:T(128)S(1)} %bitcast.27, s32[1]{0:T(128)} %bitcast.place, f32[96,18,8,128]{3,2,1,0:T(8,128)S(1)} %bitcast.17, f32[96,6,8,128]{3,2,1,0:T(8,128)S(1)} %bitcast.20, ...), custom_call_target="tpu_custom_call" | custom-call | tf_op jit(solution)/shard_map/pallas_call | solution.py:260
  114.8 1.5 %collective-permute-done.35 = f32[128,640]{1,0:T(8,128)S(1)} collective-permute-done((f32[128,640]{1,0:T(8,128)S(1)}, f32[128,640]{1,0:T(8,128)S(1)}, u32[]{:S(2)}, u32[]{:S(2)}) %collective-permute-start.35) | collective-permute-done | bytes 327712 | tf_op jit(solution)/shard_map/ppermute | solution.py:290
  116.3 1.2 collective-permute-start.36
  117.5 1.5 %collective-permute-start.38 = (f32[32,640]{1,0:T(8,128)S(1)}, f32[32,640]{1,0:T(8,128)S(1)}, u32[]{:S(2)}, u32[]{:S(2)}) collective-permute-start(f32[32,640]{1,0:T(8,128)S(1)} %get-tuple-element.35), channel_id=1, source_target_pairs={{0,5},{1,4},{2,7},{3,6},{4,1},{5,0},{6,3},{7,2},{8,13},{9,12},{10,... | collective-permute-start | bytes 245768 | tf_op jit(solution)/shard_map/ppermute | solution.py:290
  119.0 0.8 collective-permute-start.37
  119.9 1.0 collective-permute-done.36
  120.9 2.6 %collective-permute-done.38 = f32[32,640]{1,0:T(8,128)S(1)} collective-permute-done((f32[32,640]{1,0:T(8,128)S(1)}, f32[32,640]{1,0:T(8,128)S(1)}, u32[]{:S(2)}, u32[]{:S(2)}) %collective-permute-start.38) | collective-permute-done | bytes 81952 | tf_op jit(solution)/shard_map/ppermute | solution.py:290
  123.9 2.1 %collective-permute-start.39 = (f32[32,640]{1,0:T(8,128)S(1)}, f32[32,640]{1,0:T(8,128)S(1)}, u32[]{:S(2)}, u32[]{:S(2)}) collective-permute-start(f32[32,640]{1,0:T(8,128)S(1)} %fusion.3), channel_id=1, source_target_pairs={{0,8},{1,9},{2,10},{3,11},{4,12},{5,13},{6,14},{7,15},{8,0},{9,1},... | collective-permute-start | bytes 245768 | tf_op jit(solution)/shard_map/ppermute | solution.py:290
  126.0 2.4 %collective-permute-done.39 = f32[32,640]{1,0:T(8,128)S(1)} collective-permute-done((f32[32,640]{1,0:T(8,128)S(1)}, f32[32,640]{1,0:T(8,128)S(1)}, u32[]{:S(2)}, u32[]{:S(2)}) %collective-permute-start.39) | collective-permute-done | bytes 81952 | tf_op jit(solution)/shard_map/ppermute | solution.py:290
  128.4 3.3 %collective-permute-start.40 = (f32[32,640]{1,0:T(8,128)S(1)}, f32[32,640]{1,0:T(8,128)S(1)}, u32[]{:S(2)}, u32[]{:S(2)}) collective-permute-start(f32[32,640]{1,0:T(8,128)S(1)} %add.208), channel_id=1, source_target_pairs={{0,16},{1,17},{2,18},{3,19},{4,20},{5,21},{6,22},{7,23},{8,24},{9,... | collective-permute-start | bytes 245768 | tf_op jit(solution)/shard_map/ppermute | solution.py:290
  131.7 0.7 slice.78.old_residual
  132.4 0.7 slice.79.old_vector
  133.0 1.1 collective-permute-done.40
  134.8 1.7 %shard_map.107 = (f32[1,8,576]{2,1,0:T(8,128)}, f32[1,8,576]{2,1,0:T(8,128)}) custom-call(s32[1]{0:T(128)} %bitcast.place, f32[32,640]{1,0:T(8,128)} %add.209.piece, f32[32,640]{1,0:T(8,128)} %slice.78.old_residual, f32[32,640]{1,0:T(8,128)} %slice.79.old_vector, f32[8,128]{1,0:T(8,128)} %copy-done.6, f32[8,640]{1,0:T(8,128)} %copy-done.4), custom_call_target="tpu_custom_call" | custom-call | tf_op jit(solution)/shard_map/pallas_call | solution.py:351
  (67 shorter events, 7.1 us)
Async XLA Ops:
  1.4 5.0 %collective-permute-start = (f32[1,2,8,640]{3,2,1,0:T(8,128)S(1)}, f32[1,2,8,640]{3,2,1,0:T(8,128)S(1)}, u32[]{:S(2)}, u32[]{:S(2)}) collective-permute-start(f32[1,2,8,640]{3,2,1,0:T(8,128)S(1)} %fusion.8), channel_id=1, source_target_pairs={{0,8},{1,9},{2,10},{3,11},{4,12},{5,13},{6,14},{7,15},{8,0},{9,1},... | collective-permute-start | bytes 122888 | tf_op jit(solution)/shard_map/ppermute | solution.py:290
  6.4 5.5 %collective-permute-start.1 = (f32[2,2,8,640]{3,2,1,0:T(8,128)S(1)}, f32[2,2,8,640]{3,2,1,0:T(8,128)S(1)}, u32[]{:S(2)}, u32[]{:S(2)}) collective-permute-start(f32[2,2,8,640]{3,2,1,0:T(8,128)S(1)} %pad_maximum_fusion.1), channel_id=1, source_target_pairs={{0,16},{1,17},{2,18},{3,19},{4,20},{5,21},{6,22},{7,23},{8,24},{9,... | collective-permute-start | bytes 245768 | tf_op jit(solution)/shard_map/ppermute | solution.py:290
  11.9 6.6 %collective-permute-start.4 = (f32[4,2,8,640]{3,2,1,0:T(8,128)S(1)}, f32[4,2,8,640]{3,2,1,0:T(8,128)S(1)}, u32[]{:S(2)}, u32[]{:S(2)}) collective-permute-start(f32[4,2,8,640]{3,2,1,0:T(8,128)S(1)} %pad_maximum_fusion.refs_0_), channel_id=1, source_target_pairs={{0,5},{1,4},{2,7},{3,6},{4,1},{5,0},{6,3},{7,2},{8,13},{9,12},{10,... | collective-permute-start | bytes 491528 | tf_op jit(solution)/shard_map/ppermute | solution.py:290
  14.7 5.7 %collective-permute-start.3 = (f32[4,2,8,640]{3,2,1,0:T(8,128)S(1)}, f32[4,2,8,640]{3,2,1,0:T(8,128)S(1)}, u32[]{:S(2)}, u32[]{:S(2)}) collective-permute-start(f32[4,2,8,640]{3,2,1,0:T(8,128)S(1)} %pad_maximum_fusion.refs_0_), channel_id=1, source_target_pairs={{0,1},{1,0},{2,3},{3,2},{4,5},{5,4},{6,7},{7,6},{8,9},{9,8},{10,11... | collective-permute-start | bytes 491528 | tf_op jit(solution)/shard_map/ppermute | solution.py:290
  15.2 5.3 %collective-permute-start.2 = (f32[4,2,8,640]{3,2,1,0:T(8,128)S(1)}, f32[4,2,8,640]{3,2,1,0:T(8,128)S(1)}, u32[]{:S(2)}, u32[]{:S(2)}) collective-permute-start(f32[4,2,8,640]{3,2,1,0:T(8,128)S(1)} %pad_maximum_fusion.refs_0_), channel_id=1, source_target_pairs={{0,4},{1,5},{2,6},{3,7},{4,0},{5,1},{6,2},{7,3},{8,12},{9,13},{10,... | collective-permute-start | bytes 491528 | tf_op jit(solution)/shard_map/ppermute | solution.py:290
  15.5 5.6 %collective-permute-start.5 = (f32[4,2,8,640]{3,2,1,0:T(8,128)S(1)}, f32[4,2,8,640]{3,2,1,0:T(8,128)S(1)}, u32[]{:S(2)}, u32[]{:S(2)}) collective-permute-start(f32[4,2,8,640]{3,2,1,0:T(8,128)S(1)} %pad_maximum_fusion.refs_0_), channel_id=1, source_target_pairs={{0,2},{1,3},{2,0},{3,1},{4,6},{5,7},{6,4},{7,5},{8,10},{9,11},{10,... | collective-permute-start | bytes 491528 | tf_op jit(solution)/shard_map/ppermute | solution.py:290
  18.5 2.6 %collective-permute-start.8 = (f32[4,2,8,640]{3,2,1,0:T(8,128)S(1)}, f32[4,2,8,640]{3,2,1,0:T(8,128)S(1)}, u32[]{:S(2)}, u32[]{:S(2)}) collective-permute-start(f32[4,2,8,640]{3,2,1,0:T(8,128)S(1)} %collective-permute-done.4.refs_3_), channel_id=1, source_target_pairs={{0,2},{1,3},{2,0},{3,1},{4,6},{5,7},{6,4},{7,5},{8,10},{9,11},{10,... | collective-permute-start | bytes 491528 | tf_op jit(solution)/shard_map/ppermute | solution.py:290
  20.4 1.4 %collective-permute-start.7 = (f32[4,2,8,640]{3,2,1,0:T(8,128)S(1)}, f32[4,2,8,640]{3,2,1,0:T(8,128)S(1)}, u32[]{:S(2)}, u32[]{:S(2)}) collective-permute-start(f32[4,2,8,640]{3,2,1,0:T(8,128)S(1)} %collective-permute-done.3.refs_2_), channel_id=1, source_target_pairs={{0,2},{1,3},{2,0},{3,1},{4,6},{5,7},{6,4},{7,5},{8,10},{9,11},{10,... | collective-permute-start | bytes 491528 | tf_op jit(solution)/shard_map/ppermute | solution.py:290
  20.6 1.4 %collective-permute-start.6 = (f32[4,2,8,640]{3,2,1,0:T(8,128)S(1)}, f32[4,2,8,640]{3,2,1,0:T(8,128)S(1)}, u32[]{:S(2)}, u32[]{:S(2)}) collective-permute-start(f32[4,2,8,640]{3,2,1,0:T(8,128)S(1)} %collective-permute-done.2.refs_1_), channel_id=1, source_target_pairs={{0,2},{1,3},{2,0},{3,1},{4,6},{5,7},{6,4},{7,5},{8,10},{9,11},{10,... | collective-permute-start | bytes 491528 | tf_op jit(solution)/shard_map/ppermute | solution.py:290
  22.0 3.0 %copy-start = (f32[1,96,8,18,128]{4,2,3,1,0:T(8,128)S(1)}, f32[1,96,8,18,128]{4,2,3,1,0:T(8,128)}, u32[]{:S(2)}) copy-start(f32[1,96,8,18,128]{4,2,3,1,0:T(8,128)} %param.12) | copy-start | bytes 21233668
  25.0 1.7 %copy-start.1 = (f32[1,96,8,6,128]{4,2,3,1,0:T(8,128)S(1)}, f32[1,96,8,6,128]{4,2,3,1,0:T(8,128)}, u32[]{:S(2)}) copy-start(f32[1,96,8,6,128]{4,2,3,1,0:T(8,128)} %param.13) | copy-start | bytes 7077892
  26.7 1.0 copy-start.2
  27.7 0.9 copy-start.3
  28.6 0.7 copy-start.5
  39.6 1.7 %collective-permute-start.9 = (f32[128,640]{1,0:T(8,128)S(1)}, f32[128,640]{1,0:T(8,128)S(1)}, u32[]{:S(2)}, u32[]{:S(2)}) collective-permute-start(f32[128,640]{1,0:T(8,128)S(1)} %slice.61), channel_id=1, source_target_pairs={{0,2},{1,3},{2,0},{3,1},{4,6},{5,7},{6,4},{7,5},{8,10},{9,11},{10,... | collective-permute-start | bytes 983048 | tf_op jit(solution)/shard_map/ppermute | solution.py:290
  41.3 4.7 %collective-permute-start.10 = (f32[32,640]{1,0:T(8,128)S(1)}, f32[32,640]{1,0:T(8,128)S(1)}, u32[]{:S(2)}, u32[]{:S(2)}) collective-permute-start(f32[32,640]{1,0:T(8,128)S(1)} %get-tuple-element.40), channel_id=1, source_target_pairs={{0,4},{1,5},{2,6},{3,7},{4,0},{5,1},{6,2},{7,3},{8,12},{9,13},{10,... | collective-permute-start | bytes 245768 | tf_op jit(solution)/shard_map/ppermute | solution.py:290
  42.6 6.1 %collective-permute-start.12 = (f32[32,640]{1,0:T(8,128)S(1)}, f32[32,640]{1,0:T(8,128)S(1)}, u32[]{:S(2)}, u32[]{:S(2)}) collective-permute-start(f32[32,640]{1,0:T(8,128)S(1)} %get-tuple-element.41), channel_id=1, source_target_pairs={{0,5},{1,4},{2,7},{3,6},{4,1},{5,0},{6,3},{7,2},{8,13},{9,12},{10,... | collective-permute-start | bytes 245768 | tf_op jit(solution)/shard_map/ppermute | solution.py:290
  44.3 4.7 %collective-permute-start.11 = (f32[32,640]{1,0:T(8,128)S(1)}, f32[32,640]{1,0:T(8,128)S(1)}, u32[]{:S(2)}, u32[]{:S(2)}) collective-permute-start(f32[32,640]{1,0:T(8,128)S(1)} %get-tuple-element.42), channel_id=1, source_target_pairs={{0,1},{1,0},{2,3},{3,2},{4,5},{5,4},{6,7},{7,6},{8,9},{9,8},{10,11... | collective-permute-start | bytes 245768 | tf_op jit(solution)/shard_map/ppermute | solution.py:290
  49.1 4.5 %collective-permute-start.13 = (f32[32,640]{1,0:T(8,128)S(1)}, f32[32,640]{1,0:T(8,128)S(1)}, u32[]{:S(2)}, u32[]{:S(2)}) collective-permute-start(f32[32,640]{1,0:T(8,128)S(1)} %fusion.7), channel_id=1, source_target_pairs={{0,8},{1,9},{2,10},{3,11},{4,12},{5,13},{6,14},{7,15},{8,0},{9,1},... | collective-permute-start | bytes 245768 | tf_op jit(solution)/shard_map/ppermute | solution.py:290
  53.6 5.4 %collective-permute-start.14 = (f32[32,640]{1,0:T(8,128)S(1)}, f32[32,640]{1,0:T(8,128)S(1)}, u32[]{:S(2)}, u32[]{:S(2)}) collective-permute-start(f32[32,640]{1,0:T(8,128)S(1)} %add.196), channel_id=1, source_target_pairs={{0,16},{1,17},{2,18},{3,19},{4,20},{5,21},{6,22},{7,23},{8,24},{9,... | collective-permute-start | bytes 245768 | tf_op jit(solution)/shard_map/ppermute | solution.py:290
  59.0 5.4 %collective-permute-start.17 = (f32[32,640]{1,0:T(8,128)S(1)}, f32[32,640]{1,0:T(8,128)S(1)}, u32[]{:S(2)}, u32[]{:S(2)}) collective-permute-start(f32[32,640]{1,0:T(8,128)S(1)} %add.197.refs_0_), channel_id=1, source_target_pairs={{0,5},{1,4},{2,7},{3,6},{4,1},{5,0},{6,3},{7,2},{8,13},{9,12},{10,... | collective-permute-start | bytes 245768 | tf_op jit(solution)/shard_map/ppermute | solution.py:290
  61.0 4.4 %collective-permute-start.16 = (f32[32,640]{1,0:T(8,128)S(1)}, f32[32,640]{1,0:T(8,128)S(1)}, u32[]{:S(2)}, u32[]{:S(2)}) collective-permute-start(f32[32,640]{1,0:T(8,128)S(1)} %add.197.refs_0_), channel_id=1, source_target_pairs={{0,1},{1,0},{2,3},{3,2},{4,5},{5,4},{6,7},{7,6},{8,9},{9,8},{10,11... | collective-permute-start | bytes 245768 | tf_op jit(solution)/shard_map/ppermute | solution.py:290
  61.8 4.4 %collective-permute-start.15 = (f32[32,640]{1,0:T(8,128)S(1)}, f32[32,640]{1,0:T(8,128)S(1)}, u32[]{:S(2)}, u32[]{:S(2)}) collective-permute-start(f32[32,640]{1,0:T(8,128)S(1)} %add.197.refs_0_), channel_id=1, source_target_pairs={{0,4},{1,5},{2,6},{3,7},{4,0},{5,1},{6,2},{7,3},{8,12},{9,13},{10,... | collective-permute-start | bytes 245768 | tf_op jit(solution)/shard_map/ppermute | solution.py:290
  62.6 3.6 %collective-permute-start.18 = (f32[32,640]{1,0:T(8,128)S(1)}, f32[32,640]{1,0:T(8,128)S(1)}, u32[]{:S(2)}, u32[]{:S(2)}) collective-permute-start(f32[32,640]{1,0:T(8,128)S(1)} %add.197.refs_0_), channel_id=1, source_target_pairs={{0,2},{1,3},{2,0},{3,1},{4,6},{5,7},{6,4},{7,5},{8,10},{9,11},{10,... | collective-permute-start | bytes 245768 | tf_op jit(solution)/shard_map/ppermute | solution.py:290
  64.4 1.8 %collective-permute-start.21 = (f32[32,640]{1,0:T(8,128)S(1)}, f32[32,640]{1,0:T(8,128)S(1)}, u32[]{:S(2)}, u32[]{:S(2)}) collective-permute-start(f32[32,640]{1,0:T(8,128)S(1)} %collective-permute-done.17.refs_3_), channel_id=1, source_target_pairs={{0,2},{1,3},{2,0},{3,1},{4,6},{5,7},{6,4},{7,5},{8,10},{9,11},{10,... | collective-permute-start | bytes 245768 | tf_op jit(solution)/shard_map/ppermute | solution.py:290
  65.4 1.3 collective-permute-start.20
  66.2 1.3 collective-permute-start.19
  77.1 1.7 %collective-permute-start.22 = (f32[128,640]{1,0:T(8,128)S(1)}, f32[128,640]{1,0:T(8,128)S(1)}, u32[]{:S(2)}, u32[]{:S(2)}) collective-permute-start(f32[128,640]{1,0:T(8,128)S(1)} %slice.67), channel_id=1, source_target_pairs={{0,2},{1,3},{2,0},{3,1},{4,6},{5,7},{6,4},{7,5},{8,10},{9,11},{10,... | collective-permute-start | bytes 983048 | tf_op jit(solution)/shard_map/ppermute | solution.py:290
  78.9 5.6 %collective-permute-start.23 = (f32[32,640]{1,0:T(8,128)S(1)}, f32[32,640]{1,0:T(8,128)S(1)}, u32[]{:S(2)}, u32[]{:S(2)}) collective-permute-start(f32[32,640]{1,0:T(8,128)S(1)} %get-tuple-element.37), channel_id=1, source_target_pairs={{0,4},{1,5},{2,6},{3,7},{4,0},{5,1},{6,2},{7,3},{8,12},{9,13},{10,... | collective-permute-start | bytes 245768 | tf_op jit(solution)/shard_map/ppermute | solution.py:290
  79.7 6.2 %collective-permute-start.25 = (f32[32,640]{1,0:T(8,128)S(1)}, f32[32,640]{1,0:T(8,128)S(1)}, u32[]{:S(2)}, u32[]{:S(2)}) collective-permute-start(f32[32,640]{1,0:T(8,128)S(1)} %get-tuple-element.38), channel_id=1, source_target_pairs={{0,5},{1,4},{2,7},{3,6},{4,1},{5,0},{6,3},{7,2},{8,13},{9,12},{10,... | collective-permute-start | bytes 245768 | tf_op jit(solution)/shard_map/ppermute | solution.py:290
  81.7 4.8 %collective-permute-start.24 = (f32[32,640]{1,0:T(8,128)S(1)}, f32[32,640]{1,0:T(8,128)S(1)}, u32[]{:S(2)}, u32[]{:S(2)}) collective-permute-start(f32[32,640]{1,0:T(8,128)S(1)} %get-tuple-element.39), channel_id=1, source_target_pairs={{0,1},{1,0},{2,3},{3,2},{4,5},{5,4},{6,7},{7,6},{8,9},{9,8},{10,11... | collective-permute-start | bytes 245768 | tf_op jit(solution)/shard_map/ppermute | solution.py:290
  86.5 4.5 %collective-permute-start.26 = (f32[32,640]{1,0:T(8,128)S(1)}, f32[32,640]{1,0:T(8,128)S(1)}, u32[]{:S(2)}, u32[]{:S(2)}) collective-permute-start(f32[32,640]{1,0:T(8,128)S(1)} %fusion.5), channel_id=1, source_target_pairs={{0,8},{1,9},{2,10},{3,11},{4,12},{5,13},{6,14},{7,15},{8,0},{9,1},... | collective-permute-start | bytes 245768 | tf_op jit(solution)/shard_map/ppermute | solution.py:290
  91.0 5.7 %collective-permute-start.27 = (f32[32,640]{1,0:T(8,128)S(1)}, f32[32,640]{1,0:T(8,128)S(1)}, u32[]{:S(2)}, u32[]{:S(2)}) collective-permute-start(f32[32,640]{1,0:T(8,128)S(1)} %add.202), channel_id=1, source_target_pairs={{0,16},{1,17},{2,18},{3,19},{4,20},{5,21},{6,22},{7,23},{8,24},{9,... | collective-permute-start | bytes 245768 | tf_op jit(solution)/shard_map/ppermute | solution.py:290
  96.8 5.4 %collective-permute-start.30 = (f32[32,640]{1,0:T(8,128)S(1)}, f32[32,640]{1,0:T(8,128)S(1)}, u32[]{:S(2)}, u32[]{:S(2)}) collective-permute-start(f32[32,640]{1,0:T(8,128)S(1)} %add.203.refs_0_), channel_id=1, source_target_pairs={{0,5},{1,4},{2,7},{3,6},{4,1},{5,0},{6,3},{7,2},{8,13},{9,12},{10,... | collective-permute-start | bytes 245768 | tf_op jit(solution)/shard_map/ppermute | solution.py:290
  98.3 4.4 %collective-permute-start.29 = (f32[32,640]{1,0:T(8,128)S(1)}, f32[32,640]{1,0:T(8,128)S(1)}, u32[]{:S(2)}, u32[]{:S(2)}) collective-permute-start(f32[32,640]{1,0:T(8,128)S(1)} %add.203.refs_0_), channel_id=1, source_target_pairs={{0,1},{1,0},{2,3},{3,2},{4,5},{5,4},{6,7},{7,6},{8,9},{9,8},{10,11... | collective-permute-start | bytes 245768 | tf_op jit(solution)/shard_map/ppermute | solution.py:290
  99.2 4.4 %collective-permute-start.28 = (f32[32,640]{1,0:T(8,128)S(1)}, f32[32,640]{1,0:T(8,128)S(1)}, u32[]{:S(2)}, u32[]{:S(2)}) collective-permute-start(f32[32,640]{1,0:T(8,128)S(1)} %add.203.refs_0_), channel_id=1, source_target_pairs={{0,4},{1,5},{2,6},{3,7},{4,0},{5,1},{6,2},{7,3},{8,12},{9,13},{10,... | collective-permute-start | bytes 245768 | tf_op jit(solution)/shard_map/ppermute | solution.py:290
  100.3 3.3 %collective-permute-start.31 = (f32[32,640]{1,0:T(8,128)S(1)}, f32[32,640]{1,0:T(8,128)S(1)}, u32[]{:S(2)}, u32[]{:S(2)}) collective-permute-start(f32[32,640]{1,0:T(8,128)S(1)} %add.203.refs_0_), channel_id=1, source_target_pairs={{0,2},{1,3},{2,0},{3,1},{4,6},{5,7},{6,4},{7,5},{8,10},{9,11},{10,... | collective-permute-start | bytes 245768 | tf_op jit(solution)/shard_map/ppermute | solution.py:290
  102.2 1.5 %collective-permute-start.34 = (f32[32,640]{1,0:T(8,128)S(1)}, f32[32,640]{1,0:T(8,128)S(1)}, u32[]{:S(2)}, u32[]{:S(2)}) collective-permute-start(f32[32,640]{1,0:T(8,128)S(1)} %collective-permute-done.30.refs_3_), channel_id=1, source_target_pairs={{0,2},{1,3},{2,0},{3,1},{4,6},{5,7},{6,4},{7,5},{8,10},{9,11},{10,... | collective-permute-start | bytes 245768 | tf_op jit(solution)/shard_map/ppermute | solution.py:290
  102.8 1.3 collective-permute-start.33
  103.6 1.3 collective-permute-start.32
  114.5 1.8 %copy-start.4 = (f32[8,640]{1,0:T(8,128)}, f32[8,640]{1,0:T(8,128)S(1)}, u32[]{:S(2)}) copy-start(f32[8,640]{1,0:T(8,128)S(1)} %get-tuple-element.33.old_answer) | copy-start | bytes 61444
  114.5 18.5 %copy-start.6 = (f32[8,128]{1,0:T(8,128)}, f32[8,128]{1,0:T(8,128)S(1)}, u32[]{:S(2)}) copy-start(f32[8,128]{1,0:T(8,128)S(1)} %get-tuple-element.32.energy) | copy-start | bytes 12292
  114.6 1.7 %collective-permute-start.35 = (f32[128,640]{1,0:T(8,128)S(1)}, f32[128,640]{1,0:T(8,128)S(1)}, u32[]{:S(2)}, u32[]{:S(2)}) collective-permute-start(f32[128,640]{1,0:T(8,128)S(1)} %slice.73), channel_id=1, source_target_pairs={{0,2},{1,3},{2,0},{3,1},{4,6},{5,7},{6,4},{7,5},{8,10},{9,11},{10,... | collective-permute-start | bytes 983048 | tf_op jit(solution)/shard_map/ppermute | solution.py:290
  116.3 4.6 %collective-permute-start.36 = (f32[32,640]{1,0:T(8,128)S(1)}, f32[32,640]{1,0:T(8,128)S(1)}, u32[]{:S(2)}, u32[]{:S(2)}) collective-permute-start(f32[32,640]{1,0:T(8,128)S(1)} %get-tuple-element.34), channel_id=1, source_target_pairs={{0,4},{1,5},{2,6},{3,7},{4,0},{5,1},{6,2},{7,3},{8,12},{9,13},{10,... | collective-permute-start | bytes 245768 | tf_op jit(solution)/shard_map/ppermute | solution.py:290
  117.5 6.0 %collective-permute-start.38 = (f32[32,640]{1,0:T(8,128)S(1)}, f32[32,640]{1,0:T(8,128)S(1)}, u32[]{:S(2)}, u32[]{:S(2)}) collective-permute-start(f32[32,640]{1,0:T(8,128)S(1)} %get-tuple-element.35), channel_id=1, source_target_pairs={{0,5},{1,4},{2,7},{3,6},{4,1},{5,0},{6,3},{7,2},{8,13},{9,12},{10,... | collective-permute-start | bytes 245768 | tf_op jit(solution)/shard_map/ppermute | solution.py:290
  119.0 4.8 %collective-permute-start.37 = (f32[32,640]{1,0:T(8,128)S(1)}, f32[32,640]{1,0:T(8,128)S(1)}, u32[]{:S(2)}, u32[]{:S(2)}) collective-permute-start(f32[32,640]{1,0:T(8,128)S(1)} %get-tuple-element.36), channel_id=1, source_target_pairs={{0,1},{1,0},{2,3},{3,2},{4,5},{5,4},{6,7},{7,6},{8,9},{9,8},{10,11... | collective-permute-start | bytes 245768 | tf_op jit(solution)/shard_map/ppermute | solution.py:290
  123.9 4.5 %collective-permute-start.39 = (f32[32,640]{1,0:T(8,128)S(1)}, f32[32,640]{1,0:T(8,128)S(1)}, u32[]{:S(2)}, u32[]{:S(2)}) collective-permute-start(f32[32,640]{1,0:T(8,128)S(1)} %fusion.3), channel_id=1, source_target_pairs={{0,8},{1,9},{2,10},{3,11},{4,12},{5,13},{6,14},{7,15},{8,0},{9,1},... | collective-permute-start | bytes 245768 | tf_op jit(solution)/shard_map/ppermute | solution.py:290
  128.4 5.7 %collective-permute-start.40 = (f32[32,640]{1,0:T(8,128)S(1)}, f32[32,640]{1,0:T(8,128)S(1)}, u32[]{:S(2)}, u32[]{:S(2)}) collective-permute-start(f32[32,640]{1,0:T(8,128)S(1)} %add.208), channel_id=1, source_target_pairs={{0,16},{1,17},{2,18},{3,19},{4,20},{5,21},{6,22},{7,23},{8,24},{9,... | collective-permute-start | bytes 245768 | tf_op jit(solution)/shard_map/ppermute | solution.py:290

commit v2 on v1

v2 whole, which is shorter than its diff:
```python
import functools
import math

import jax
import jax.numpy as jnp
from jax import lax
from jax.experimental import pallas as pl
from jax.experimental.pallas import tpu as pltpu
from jax.sharding import PartitionSpec as P

ITERS = 3
CPAR = 9
CAMERAS = 64
SLOTS = 8
POINTS = 128
TILE = CPAR * CAMERAS
PAIRS = 5
WIDTH = PAIRS * 128
BATCH = 96
AXES = ("pts", "cam")


def split_two(value):
    high = value.astype(jnp.bfloat16)
    low = (value - high.astype(jnp.float32)).astype(jnp.bfloat16)
    return high, low


def all_slots(value):
    for by in (4, 2, 1):
        value = value + pltpu.roll(value, by, 0)
    return value


def invert(gram):
    a, b, c, d, e, f = gram
    aa = d * f - e * e
    bb = c * e - b * f
    cc = b * e - c * d
    dd = a * f - c * c
    ee = b * c - a * e
    ff = a * d - b * b
    scale = 1.0 / (a * aa + b * bb + c * cc)
    return [entry * scale for entry in (aa, bb, cc, dd, ee, ff)]


def setup_kernel(counts, cam, point, index, damp, cam_out, point_out, index_out, inverse_out, selector_out):
    step = pl.program_id(0)
    block = cam.shape[0]
    slot = lax.broadcasted_iota(jnp.int32, (SLOTS, POINTS), 0)
    camera = lax.broadcasted_iota(jnp.int32, (CAMERAS, POINTS), 0).astype(jnp.bfloat16)
    one = jnp.ones((CAMERAS, POINTS), jnp.bfloat16)
    zero = jnp.zeros((CAMERAS, POINTS), jnp.bfloat16)

    def advance(i, carry):
        live = (slot < counts[step * block + i]).astype(jnp.float32)
        for r in range(2 * CPAR):
            cam_out[i, r] = cam[i, r] * live
        rows = [point[i, r] for r in range(6)]
        for r in range(6):
            point_out[i, r] = rows[r]
        seen = index[i]
        index_out[i] = seen
        rows = [row * live for row in rows]
        entries = [(0, 0), (0, 1), (0, 2), (1, 1), (1, 2), (2, 2)]
        gram = [all_slots(rows[a] * rows[b] + rows[3 + a] * rows[3 + b]) for a, b in entries]
        for a, entry in enumerate((0, 3, 5)):
            gram[entry] = gram[entry] + damp[a, pl.ds(i, 1), :]
        for a, entry in enumerate(invert(gram)):
            inverse_out[i, a] = entry
        wide = seen.astype(jnp.float32)
        for k in range(SLOTS):
            row = wide[k : k + 1, :].astype(jnp.bfloat16)
            down, right = k // 2 * CAMERAS, k % 2 * POINTS
            selector_out[i, down : down + CAMERAS, right : right + POINTS] = jnp.where(camera == row, one, zero)
        return carry

    lax.fori_loop(0, block, advance, 0, unroll=4)


def tile_product(cam, point, index, inverse, selector, picked_from, row, put_to):
    slot = lax.broadcasted_iota(jnp.int32, (SLOTS, POINTS), 0)
    lane = lax.broadcasted_iota(jnp.int32, (SLOTS, POINTS), 1)
    other = index + CAMERAS
    pairs = [picked_from[pl.ds(row, SLOTS), p * 128 : (p + 1) * 128] for p in range(PAIRS)]
    picked = [
        jnp.take_along_axis(
            pairs[j // 2], other if j % 2 else index, axis=1, mode="promise_in_bounds"
        )
        for j in range(CPAR)
    ]
    rows = [point(r) for r in range(6)]
    q = []
    for r in range(2):
        total = cam(9 * r) * picked[0]
        for j in range(1, CPAR):
            total = total + cam(9 * r + j) * picked[j]
        q.append(total)
    y = [all_slots(rows[a] * q[0] + rows[3 + a] * q[1]) for a in range(3)]
    i0, i1, i2, i3, i4, i5 = [inverse(a) for a in range(6)]
    z = [
        i0 * y[0] + i1 * y[1] + i2 * y[2],
        i1 * y[0] + i3 * y[1] + i4 * y[2],
        i2 * y[0] + i4 * y[1] + i5 * y[2],
    ]
    e = [
        q[r] - (rows[3 * r] * z[0] + rows[3 * r + 1] * z[1] + rows[3 * r + 2] * z[2])
        for r in range(2)
    ]
    slot_twice = lax.broadcasted_iota(jnp.int32, (2 * SLOTS, POINTS), 0) & 1
    odd = slot_twice.astype(jnp.bfloat16)
    even = (1 - slot_twice).astype(jnp.bfloat16)
    left = []
    for j in range(CPAR):
        returned = cam(j) * e[0] + cam(9 + j) * e[1]
        high = returned.astype(jnp.bfloat16).astype(jnp.float32)
        both = jnp.concatenate([high, returned - high], axis=0).astype(jnp.bfloat16)
        left.append(jnp.concatenate([both * even, both * odd], axis=1))
    left = jnp.concatenate(left, axis=0)
    spread = lax.dot_general(
        left, selector, (((1,), (1,)), ((), ())), preferred_element_type=jnp.float32
    )
    side = (slot >> 1) & 1
    first_side = side == 0
    keep = (lane >> 6) == side
    sums = []
    for j in range(CPAR):
        both = spread[16 * j : 16 * j + 8] + spread[16 * j + 8 : 16 * j + 16]
        sums.append(jnp.where(slot < 4, both[:, :128], both[:, 128:]))
    sums.append(jnp.zeros_like(sums[0]))
    for p in range(PAIRS):
        one, two = sums[2 * p], sums[2 * p + 1]
        stay = jnp.where(first_side, one, two)
        move = pltpu.roll(jnp.where(first_side, two, one), CAMERAS, 1)
        put_to[pl.ds(row, SLOTS), p * 128 : (p + 1) * 128] = jnp.where(keep, stay, move)
    return q[0] * e[0] + q[1] * e[1]


def product_steps(problem, pick, put, vector, out, picked_from, put_to):
    cam, point, index, inverse, selector = problem
    tiles = cam.shape[0]
    batch = math.gcd(tiles, BATCH)
    high, low = split_two(vector[...])
    picked_from[...] = jnp.dot(
        pick[...], high, preferred_element_type=jnp.float32
    ) + jnp.dot(pick[...], low, preferred_element_type=jnp.float32)

    def advance(step, total):
        for turn in range(batch):
            i = step * batch + turn
            total = total + tile_product(
                lambda r: cam[i, r],
                lambda r: point[i, r],
                index[i],
                lambda a: inverse[i, a],
                selector[i],
                picked_from,
                pl.multiple_of(i * SLOTS, SLOTS),
                put_to,
            )
        return total

    dot = lax.fori_loop(0, tiles // batch, advance, jnp.zeros((SLOTS, POINTS), jnp.float32))
    high, low = split_two(put_to[...])
    out[...] = jnp.dot(put[...], high, preferred_element_type=jnp.float32) + jnp.dot(
        put[...], low, preferred_element_type=jnp.float32
    )
    return dot


def total_of(value):
    return jnp.sum(value, keepdims=True).reshape(1, 1)


def finish(place, damp, vector, out, dot):
    rows = damp.shape[0]
    own = pl.ds(pl.multiple_of(place[0] * rows, rows), rows)
    damped = damp[...] * vector[own, :]
    out[own, :] += damped
    part = total_of(dot) + total_of(damped * vector[own, :])
    lane = lax.broadcasted_iota(jnp.int32, (out.shape[0], 128), 1)
    out[:, WIDTH - 128 :] += jnp.where(lane >= TILE - (WIDTH - 128), part, 0.0)


def first_kernel(ranks, place, *refs):
    problem, (pick, put, damp), refs = refs[:5], refs[5:8], refs[8:]
    pieces, refs = refs[:ranks], refs[ranks:]
    out, residual, scaling, vector, energy, picked_from, put_to = refs
    ring, _, rows, _ = pieces[0].shape
    for r in range(ranks):
        for away in range(ring):
            at = pl.multiple_of((r * ring + (away ^ place[0])) * rows, rows)
            residual[pl.ds(at, rows), :] = pieces[r][away, 0]
            scaling[pl.ds(at, rows), :] = pieces[r][away, 1]
    scaled = residual[...] * scaling[...]
    vector[...] = scaled
    energy[...] = jnp.broadcast_to(total_of(scaled * residual[...]), energy.shape)
    dot = product_steps(problem, pick, put, vector, out, picked_from, put_to)
    finish(place, damp, vector, out, dot)


def next_kernel(ranks, place, *refs):
    problem, (pick, put, damp), refs = refs[:5], refs[5:8], refs[8:]
    pieces, refs = refs[:ranks], refs[ranks:]
    old_residual, scaling, old_vector, old_energy, old_answer = refs[:5]
    out, residual, vector, energy, answer, picked_from, put_to = refs[5:]
    many = pieces[0].shape[0]
    rows = damp.shape[0]
    step_size = old_energy[0:1, 0:1] / pieces[0][0:1, TILE : TILE + 1]
    own = pl.ds(pl.multiple_of(place[0] * rows, rows), rows)
    answer[...] = old_answer[...] + step_size * old_vector[own, :]
    power = jnp.zeros((1, 1), jnp.float32)
    for r in range(ranks):
        part = slice(r * many, (r + 1) * many)
        left = old_residual[part, :] - step_size * pieces[r][...]
        residual[part, :] = left
        scaled = scaling[part, :] * left
        vector[part, :] = scaled
        power = power + total_of(scaled * left)
    vector[...] += (power / old_energy[0:1, 0:1]) * old_vector[...]
    energy[...] = jnp.broadcast_to(power, energy.shape)
    dot = product_steps(problem, pick, put, vector, out, picked_from, put_to)
    finish(place, damp, vector, out, dot)


def plain_kernel(*refs):
    problem, (pick, put, vector), (out, picked_from, put_to) = refs[:5], refs[5:8], refs[8:]
    product_steps(problem, pick, put, vector, out, picked_from, put_to)


def last_kernel(place, piece, old_residual, old_vector, energy, old_answer, answer, residual):
    rows = old_answer.shape[0]
    step_size = energy[0:1, 0:1] / piece[0:1, TILE : TILE + 1]
    own = pl.ds(pl.multiple_of(place[0] * rows, rows), rows)
    answer[0] = (old_answer[...] + step_size * old_vector[own, :])[:, :TILE]
    residual[0] = (old_residual[own, :] - step_size * piece[own, :])[:, :TILE]


def whole(shape):
    return pl.BlockSpec(shape, lambda s, *refs: (0,) * len(shape))


def by_tiles(block, shape):
    return pl.BlockSpec((block,) + shape[1:], lambda s, *refs: (s,) + (0,) * (len(shape) - 1))


def call_setup(counts, cam, point, index, damp):
    tiles = cam.shape[0]
    block = math.gcd(tiles, 16)
    shapes = [cam.shape, point.shape, index.shape, (tiles, 6, SLOTS, POINTS)]
    shapes += [(tiles, SLOTS // 2 * CAMERAS, 2 * POINTS)]
    kinds = [jnp.float32, jnp.float32, jnp.int32, jnp.float32, jnp.bfloat16]
    return pl.pallas_call(
        setup_kernel,
        out_shape=[pltpu.VMEM(shape, kind) for shape, kind in zip(shapes, kinds)],
        grid_spec=pltpu.PrefetchScalarGridSpec(
            num_scalar_prefetch=1,
            grid=(tiles // block,),
            in_specs=[by_tiles(block, shape) for shape in shapes[:3]]
            + [pl.BlockSpec((3, block, POINTS), lambda s, *refs: (0, s, 0))],
            out_specs=[by_tiles(block, shape) for shape in shapes],
        ),
        compiler_params=pltpu.CompilerParams(
            vmem_limit_bytes=14 * 2**20, dimension_semantics=("arbitrary",)
        ),
        cost_estimate=pl.CostEstimate(flops=10**8, bytes_accessed=3 * 10**7, transcendentals=0),
    )(counts, *[pltpu.with_memory_space_constraint(x, pltpu.HBM) for x in (cam, point, index, damp)])


def call_product(kernel, scalars, problem, others, outs):
    tiles = problem[0].shape[0]
    scratch = pltpu.VMEM((tiles * SLOTS, WIDTH), jnp.float32)
    held = [pltpu.with_memory_space_constraint(array, pltpu.VMEM) for array in problem]
    return pl.pallas_call(
        kernel,
        out_shape=[jax.ShapeDtypeStruct(shape, jnp.float32) for shape in outs],
        in_specs=[pl.BlockSpec(memory_space=pltpu.SMEM)] * len(scalars)
        + [pl.BlockSpec(memory_space=pltpu.VMEM)] * (len(held) + len(others)),
        out_specs=[pl.BlockSpec(memory_space=pltpu.VMEM)] * len(outs),
        scratch_shapes=[scratch, scratch],
        compiler_params=pltpu.CompilerParams(vmem_limit_bytes=20 * 2**20),
    )(*scalars, *held, *others)


def tables_of(rows, window):
    listed = rows.reshape(-1)
    places = lax.iota(jnp.int32, window)
    pick = (listed[:, None] == places[None, :]).astype(jnp.bfloat16)
    put = (places[:, None] == listed[None, :]).astype(jnp.bfloat16)
    return [pick, put]


def widen(array):
    return jnp.pad(array, [(0, 0)] * (array.ndim - 1) + [(0, WIDTH - TILE)])


def exchange(array, mask):
    devices = lax.axis_size("pts") * lax.axis_size("cam")
    return lax.ppermute(array, AXES, [(i, i ^ mask) for i in range(devices)])


def two_groups(rhs, damp_cam, precond, problem, tile_ids):
    CAM, CORE, Y, Z = 1, 2, 4, 8
    shards = lax.axis_size("pts")
    tiles = rhs.shape[0]
    ring = shards // 4
    group, shard = lax.axis_index("cam"), lax.axis_index("pts")
    group_tiles = shards * tiles
    window = 2 * group_tiles
    place = (shard >> 2).reshape(1)
    where = (group * group_tiles + tile_ids - group_tiles // 2) % window
    owner_group, owner = where // group_tiles, where % group_tiles // tiles
    apart = owner ^ shard
    rank = (apart & 1) * 4 + (owner_group ^ group) * 2 + ((apart >> 1) & 1)
    tables = tables_of((rank * ring + (owner >> 2)) * tiles + where % tiles, window)
    steady = tables + [widen(damp_cam)]

    def gather(own):
        near = [own, exchange(own, Y), exchange(own, CAM), exchange(own, CAM | Y)]
        return near + [exchange(piece, CORE) for piece in near]

    def reduce(partial):
        half = window // 2
        mine = partial[:half] + exchange(partial[half:], CORE)
        part = half // 4
        mine = (
            mine[:part]
            + exchange(mine[part : 2 * part], Y)
            + exchange(mine[2 * part : 3 * part], CAM)
            + exchange(mine[3 * part :], CAM | Y)
        )
        return sum([exchange(mine, Z * away) for away in range(1, ring)], mine)

    both = widen(jnp.stack([rhs, precond]))
    pieces = gather(jnp.stack([both] + [exchange(both, Z * away) for away in range(1, ring)]))
    full, small, own = (window, WIDTH), (8, 128), (tiles, WIDTH)
    partial, residual, scaling, vector, energy = call_product(
        functools.partial(first_kernel, 8), [place], problem, steady + pieces,
        [full, full, full, full, small],
    )
    answer = jnp.zeros(own, jnp.float32)
    for iteration in range(1, ITERS):
        pieces = gather(reduce(partial))
        partial, residual, vector, energy, answer = call_product(
            functools.partial(next_kernel, 8), [place], problem,
            steady + pieces + [residual, scaling, vector, energy, answer],
            [full, full, full, small, own],
        )
    mine = reduce(partial)
    return pl.pallas_call(
        last_kernel,
        out_shape=[jax.ShapeDtypeStruct((1, tiles, TILE), jnp.float32)] * 2,
        grid=(1,),
        in_specs=[pl.BlockSpec(memory_space=pltpu.SMEM)]
        + [whole(shape) for shape in (mine.shape, mine.shape, mine.shape, small, own)],
        out_specs=[whole((1, tiles, TILE))] * 2,
    )(place, mine, residual, vector, energy, answer)


def from_behind(shard, axis, by):
    devices = lax.axis_size(axis)
    return lax.ppermute(shard, axis, [(i, (i + by) % devices) for i in range(devices)])


def many_groups(rhs, damp_cam, precond, problem, tile_ids):
    group_tiles = lax.axis_size("pts") * rhs.shape[0]
    halfway = group_tiles // 2
    window = 2 * group_tiles
    tables = tables_of(tile_ids, window)

    def product(vector):
        panel = lax.all_gather(widen(vector), "pts", axis=0, tiled=True)
        lower = from_behind(panel[halfway:], "cam", 1)
        upper = from_behind(panel[:halfway], "cam", -1)
        whole_window = jnp.concatenate([lower, panel, upper], axis=0)
        partial = call_product(
            plain_kernel, [], problem, tables + [whole_window], [(window, WIDTH)]
        )[0]
        from_above = from_behind(partial[:halfway], "cam", -1)
        from_below = from_behind(partial[halfway + group_tiles :], "cam", 1)
        summed = partial[halfway : halfway + group_tiles] + jnp.concatenate(
            [from_below, from_above], axis=0
        )
        return lax.psum_scatter(summed, "pts", scatter_dimension=0, tiled=True)[:, :TILE] + damp_cam * vector

    def inner(one, two):
        return lax.psum(jnp.sum(one * two), AXES)

    answer, residual = jnp.zeros(rhs.shape, jnp.float32), rhs
    scaled = precond * residual
    direction = scaled
    energy = inner(residual, scaled)
    for iteration in range(ITERS):
        mapped = product(direction)
        step_size = energy / inner(direction, mapped)
        answer = answer + step_size * direction
        residual = residual - step_size * mapped
        scaled = precond * residual
        energy_next = inner(residual, scaled)
        direction = scaled + energy_next / energy * direction
        energy = energy_next
    return answer[None], residual[None]


def on_device(rhs, damp_cam, precond, cam_jac, pt_jac, damp_pt, cam_index, tile_ids, counts):
    problem = call_setup(
        counts[0],
        jnp.transpose(cam_jac[0], (0, 2, 1, 3)),
        jnp.transpose(pt_jac[0], (0, 2, 1, 3)),
        cam_index[0],
        jnp.transpose(damp_pt[0], (1, 0, 2)),
    )
    groups, shards = lax.axis_size("cam"), lax.axis_size("pts")
    plan = two_groups if groups == 2 and shards in (4, 8, 16, 32) else many_groups
    return tuple(plan(rhs[0], damp_cam[0], precond[0], problem, tile_ids[0]))


def solution(mesh):
    return jax.shard_map(
        on_device,
        mesh=mesh,
        in_specs=(
            P("cam", "pts", None),
            P("cam", "pts", None),
            P("cam", "pts", None),
            P("cam", "pts", None, None, None),
            P("cam", "pts", None, None, None),
            P("cam", "pts", None, None),
            P("cam", "pts", None, None),
            P("cam", "pts", None),
            P("cam", "pts"),
        ),
        out_specs=(P("cam", "pts", None), P("cam", "pts", None)),
        check_vma=False,
    )
```

time: 137 us -> 126 us (0.920)
  local copies, waits for them, and re-layouts: 9.59 us -> 3.39 us
  starting transfers between devices: 44.2 us -> 41.8 us
  Pallas kernels: 31.1 us -> 29.1 us
    pallas_call x3, Pallas kernels: 29.5 us -> 19.8 us  [call_product(): pl.pallas_call(kernel, out_shape=[jax.ShapeDtypeStruct(shape, jnp.float32...]
    pallas_call x0 -> x1, Pallas kernels: none -> 7.51 us  [call_setup(): pl.pallas_call(setup_kernel, out_shape=[pltpu.VMEM(shape, kind) for shape...]
    unnamed x14 -> x10, local copies, waits for them, and re-layouts: 7.24 us -> 2.35 us
    ppermute x41 -> x45, starting transfers between devices: 44.2 us -> 41.8 us  [exchange(): return lax.ppermute(array, AXES, [(i, i ^ mask) for i in range(devices)])]
    ppermute x41 -> x45, waiting for transfers between devices: 48.1 us -> 48.3 us  [exchange(): return lax.ppermute(array, AXES, [(i, i ^ mask) for i in range(devices)])]
  transfers between devices with their start and end apart: 41 -> 45, of which waited for: 35 -> 32; matrix products, arithmetic and copies ran while one was open for 2% -> 1% of each run, Pallas kernels for 0% -> 6%
where the time goes in v2:
time: 126 us
  waiting for transfers between devices  48.3 us (38%)
  starting transfers between devices  41.8 us (33%)
  Pallas kernels  29.1 us (23%)
  local copies, waits for them, and re-layouts  3.39 us (3%)
  other arithmetic  2.61 us (2%)
    ppermute x45, waiting for transfers between devices, exchange(): return lax.ppermute(array, AXES, [(i, i ^ mask) for i in range(devices)])  48.3 us
    ppermute x45, starting transfers between devices, exchange(): return lax.ppermute(array, AXES, [(i, i ^ mask) for i in range(devices)])  41.8 us
    pallas_call x3, Pallas kernels, call_product(): pl.pallas_call(kernel, out_shape=[jax.ShapeDtypeStruct(shape, jnp.float32...  19.8 us
    pallas_call x1, Pallas kernels, call_setup(): pl.pallas_call(setup_kernel, out_shape=[pltpu.VMEM(shape, kind) for shape...  7.51 us
  transfers between devices with their start and end apart: 45, of which 32 were waited for; matrix products, arithmetic and copies ran while one was open for 1% of the time, Pallas kernels for 6%

profile of v2, /device:TPU:0, one launch (start us, length us, event | category | flops | bytes accessed | tf_op | source)
XLA Modules:
  0.0 126.1 jit_solution(11297052455085962444)
XLA Ops:
  0.6 0.8 fusion.22
  1.4 3.0 %collective-permute-start = (f32[2,8,640]{2,1,0:T(8,128)S(1)}, f32[2,8,640]{2,1,0:T(8,128)S(1)}, u32[]{:S(2)}, u32[]{:S(2)}) collective-permute-start(f32[2,8,640]{2,1,0:T(8,128)S(1)} %get-tuple-element.52), channel_id=1, source_target_pairs={{0,8},{1,9},{2,10},{3,11},{4,12},{5,13},{6,14},{7,15},{8,0},{9,1},... | collective-permute-start | bytes 122888 | tf_op jit(solution)/shard_map/ppermute | solution.py:299
  4.4 2.6 %collective-permute-start.1 = (f32[2,8,640]{2,1,0:T(8,128)S(1)}, f32[2,8,640]{2,1,0:T(8,128)S(1)}, u32[]{:S(2)}, u32[]{:S(2)}) collective-permute-start(f32[2,8,640]{2,1,0:T(8,128)S(1)} %get-tuple-element.52), channel_id=1, source_target_pairs={{0,16},{1,17},{2,18},{3,19},{4,20},{5,21},{6,22},{7,23},{8,24},{9,... | collective-permute-start | bytes 122888 | tf_op jit(solution)/shard_map/ppermute | solution.py:299
  7.0 0.7 add_add_fusion.3
  7.9 0.7 pad.8.refs_7_
  8.7 0.7 copy-done.4
  9.3 7.5 %shard_map.104 = (f32[96,18,8,128]{3,2,1,0:T(8,128)S(1)}, f32[96,6,8,128]{3,2,1,0:T(8,128)S(1)}, s32[96,8,128]{2,1,0:T(8,128)S(1)}, f32[96,6,8,128]{3,2,1,0:T(8,128)S(1)}, bf16[96,256,256]{2,1,0:T(8,128)(2,1)S(1)}) custom-call(s32[96]{0:T(128)S(1)} %bitcast.18, f32[96,18,8,128]{3,2,1,0:T(8,128)} %bitcast.19, f32[96,6,8,128]{3,2,1,0:T(8,128)} %bitcast.20, ...), custom_call_target="tpu_custom_call" | custom-call | flops 100000000 | bytes 30000000 | tf_op jit(solution)/shard_map/pallas_call | solution.py:253
  16.9 2.7 %collective-permute-start.5 = (f32[4,2,8,640]{3,2,1,0:T(8,128)S(1)}, f32[4,2,8,640]{3,2,1,0:T(8,128)S(1)}, u32[]{:S(2)}, u32[]{:S(2)}) collective-permute-start(f32[4,2,8,640]{3,2,1,0:T(8,128)S(1)} %pad_maximum_fusion.refs_8_), channel_id=1, source_target_pairs={{0,5},{1,4},{2,7},{3,6},{4,1},{5,0},{6,3},{7,2},{8,13},{9,12},{10,... | collective-permute-start | bytes 491528 | tf_op jit(solution)/shard_map/ppermute | solution.py:299
  19.6 0.5 collective-permute-start.4
  20.6 4.4 %collective-permute-done.5.refs_11_ = f32[4,2,8,640]{3,2,1,0:T(8,128)S(1)} collective-permute-done((f32[4,2,8,640]{3,2,1,0:T(8,128)S(1)}, f32[4,2,8,640]{3,2,1,0:T(8,128)S(1)}, u32[]{:S(2)}, u32[]{:S(2)}) %collective-permute-start.5) | collective-permute-done | bytes 163872 | tf_op jit(solution)/shard_map/ppermute | solution.py:299
  25.0 1.8 %collective-permute-done.4.refs_10_ = f32[4,2,8,640]{3,2,1,0:T(8,128)S(1)} collective-permute-done((f32[4,2,8,640]{3,2,1,0:T(8,128)S(1)}, f32[4,2,8,640]{3,2,1,0:T(8,128)S(1)}, u32[]{:S(2)}, u32[]{:S(2)}) %collective-permute-start.4) | collective-permute-done | bytes 163872 | tf_op jit(solution)/shard_map/ppermute | solution.py:299
  26.8 0.5 collective-permute-start.7
  27.5 0.7 collective-permute-done.8.refs_14_
  28.4 6.3 %shard_map.105 = (f32[256,640]{1,0:T(8,128)S(1)}, f32[256,640]{1,0:T(8,128)S(1)}, f32[256,640]{1,0:T(8,128)S(1)}, f32[256,640]{1,0:T(8,128)S(1)}, f32[8,128]{1,0:T(8,128)S(1)}) custom-call(s32[1]{0:T(128)} %bitcast.place, f32[96,18,8,128]{3,2,1,0:T(8,128)S(1)} %get-tuple-element.22.refs_0_, f32[96,6,8,128]{3,2,1,0:T(8,128)S(1)} %get-tuple-element.23.refs_1_, ...), custom_call_target="tpu_custom_call" | custom-call | tf_op jit(solution)/shard_map/pallas_call | solution.py:274
  35.1 1.4 %collective-permute-done.10 = f32[128,640]{1,0:T(8,128)S(1)} collective-permute-done((f32[128,640]{1,0:T(8,128)S(1)}, f32[128,640]{1,0:T(8,128)S(1)}, u32[]{:S(2)}, u32[]{:S(2)}) %collective-permute-start.10) | collective-permute-done | bytes 327712 | tf_op jit(solution)/shard_map/ppermute | solution.py:299
  36.5 1.3 %collective-permute-start.11 = (f32[32,640]{1,0:T(8,128)S(1)}, f32[32,640]{1,0:T(8,128)S(1)}, u32[]{:S(2)}, u32[]{:S(2)}) collective-permute-start(f32[32,640]{1,0:T(8,128)S(1)} %get-tuple-element.48), channel_id=1, source_target_pairs={{0,4},{1,5},{2,6},{3,7},{4,0},{5,1},{6,2},{7,3},{8,12},{9,13},{10,... | collective-permute-start | bytes 245768 | tf_op jit(solution)/shard_map/ppermute | solution.py:299
  37.8 1.7 %collective-permute-start.13 = (f32[32,640]{1,0:T(8,128)S(1)}, f32[32,640]{1,0:T(8,128)S(1)}, u32[]{:S(2)}, u32[]{:S(2)}) collective-permute-start(f32[32,640]{1,0:T(8,128)S(1)} %get-tuple-element.49), channel_id=1, source_target_pairs={{0,5},{1,4},{2,7},{3,6},{4,1},{5,0},{6,3},{7,2},{8,13},{9,12},{10,... | collective-permute-start | bytes 245768 | tf_op jit(solution)/shard_map/ppermute | solution.py:299
  39.6 0.5 collective-permute-start.12
  40.1 1.1 collective-permute-done.11
  41.2 2.7 %collective-permute-done.13 = f32[32,640]{1,0:T(8,128)S(1)} collective-permute-done((f32[32,640]{1,0:T(8,128)S(1)}, f32[32,640]{1,0:T(8,128)S(1)}, u32[]{:S(2)}, u32[]{:S(2)}) %collective-permute-start.13) | collective-permute-done | bytes 81952 | tf_op jit(solution)/shard_map/ppermute | solution.py:299
  44.3 3.6 %collective-permute-start.16 = (f32[32,640]{1,0:T(8,128)S(1)}, f32[32,640]{1,0:T(8,128)S(1)}, u32[]{:S(2)}, u32[]{:S(2)}) collective-permute-start(f32[32,640]{1,0:T(8,128)S(1)} %fusion.7), channel_id=1, source_target_pairs={{0,24},{1,25},{2,26},{3,27},{4,28},{5,29},{6,30},{7,31},{8,16},{9,... | collective-permute-start | bytes 245768 | tf_op jit(solution)/shard_map/ppermute | solution.py:299
  47.9 0.8 collective-permute-start.14
  48.7 2.3 %collective-permute-done.16 = f32[32,640]{1,0:T(8,128)S(1)} collective-permute-done((f32[32,640]{1,0:T(8,128)S(1)}, f32[32,640]{1,0:T(8,128)S(1)}, u32[]{:S(2)}, u32[]{:S(2)}) %collective-permute-start.16) | collective-permute-done | bytes 81952 | tf_op jit(solution)/shard_map/ppermute | solution.py:299
  51.1 3.0 %collective-permute-done.15 = f32[32,640]{1,0:T(8,128)S(1)} collective-permute-done((f32[32,640]{1,0:T(8,128)S(1)}, f32[32,640]{1,0:T(8,128)S(1)}, u32[]{:S(2)}, u32[]{:S(2)}) %collective-permute-start.15) | collective-permute-done | bytes 81952 | tf_op jit(solution)/shard_map/ppermute | solution.py:299
  54.1 2.0 %collective-permute-start.19 = (f32[32,640]{1,0:T(8,128)S(1)}, f32[32,640]{1,0:T(8,128)S(1)}, u32[]{:S(2)}, u32[]{:S(2)}) collective-permute-start(f32[32,640]{1,0:T(8,128)S(1)} %add_add_fusion.2.refs_8_), channel_id=1, source_target_pairs={{0,5},{1,4},{2,7},{3,6},{4,1},{5,0},{6,3},{7,2},{8,13},{9,12},{10,... | collective-permute-start | bytes 245768 | tf_op jit(solution)/shard_map/ppermute | solution.py:299
  56.1 0.8 collective-permute-start.18
  56.9 0.8 collective-permute-start.17
  57.7 2.4 %collective-permute-done.19.refs_11_ = f32[32,640]{1,0:T(8,128)S(1)} collective-permute-done((f32[32,640]{1,0:T(8,128)S(1)}, f32[32,640]{1,0:T(8,128)S(1)}, u32[]{:S(2)}, u32[]{:S(2)}) %collective-permute-start.19) | collective-permute-done | bytes 81952 | tf_op jit(solution)/shard_map/ppermute | solution.py:299
  60.6 0.7 collective-permute-done.17.refs_9_
  61.8 0.8 collective-permute-done.21.refs_13_
  62.6 6.9 %shard_map.106 = (f32[256,640]{1,0:T(8,128)S(1)}, f32[256,640]{1,0:T(8,128)S(1)}, f32[256,640]{1,0:T(8,128)S(1)}, f32[8,128]{1,0:T(8,128)S(1)}, f32[8,640]{1,0:T(8,128)S(1)}) custom-call(s32[1]{0:T(128)} %bitcast.place, f32[96,18,8,128]{3,2,1,0:T(8,128)S(1)} %get-tuple-element.22.refs_0_, f32[96,6,8,128]{3,2,1,0:T(8,128)S(1)} %get-tuple-element.23.refs_1_, ...), custom_call_target="tpu_custom_call" | custom-call | tf_op jit(solution)/shard_map/pallas_call | solution.py:274
  69.7 1.5 %collective-permute-done.24 = f32[128,640]{1,0:T(8,128)S(1)} collective-permute-done((f32[128,640]{1,0:T(8,128)S(1)}, f32[128,640]{1,0:T(8,128)S(1)}, u32[]{:S(2)}, u32[]{:S(2)}) %collective-permute-start.24) | collective-permute-done | bytes 327712 | tf_op jit(solution)/shard_map/ppermute | solution.py:299
  71.3 0.9 collective-permute-start.25
  72.1 1.9 %collective-permute-start.27 = (f32[32,640]{1,0:T(8,128)S(1)}, f32[32,640]{1,0:T(8,128)S(1)}, u32[]{:S(2)}, u32[]{:S(2)}) collective-permute-start(f32[32,640]{1,0:T(8,128)S(1)} %get-tuple-element.46), channel_id=1, source_target_pairs={{0,5},{1,4},{2,7},{3,6},{4,1},{5,0},{6,3},{7,2},{8,13},{9,12},{10,... | collective-permute-start | bytes 245768 | tf_op jit(solution)/shard_map/ppermute | solution.py:299
  74.0 0.8 collective-permute-start.26
  74.8 2.0 %collective-permute-done.25 = f32[32,640]{1,0:T(8,128)S(1)} collective-permute-done((f32[32,640]{1,0:T(8,128)S(1)}, f32[32,640]{1,0:T(8,128)S(1)}, u32[]{:S(2)}, u32[]{:S(2)}) %collective-permute-start.25) | collective-permute-done | bytes 81952 | tf_op jit(solution)/shard_map/ppermute | solution.py:299
  76.8 1.5 %collective-permute-done.27 = f32[32,640]{1,0:T(8,128)S(1)} collective-permute-done((f32[32,640]{1,0:T(8,128)S(1)}, f32[32,640]{1,0:T(8,128)S(1)}, u32[]{:S(2)}, u32[]{:S(2)}) %collective-permute-start.27) | collective-permute-done | bytes 81952 | tf_op jit(solution)/shard_map/ppermute | solution.py:299
  78.3 0.5 collective-permute-done.26
  78.9 2.6 %collective-permute-start.30 = (f32[32,640]{1,0:T(8,128)S(1)}, f32[32,640]{1,0:T(8,128)S(1)}, u32[]{:S(2)}, u32[]{:S(2)}) collective-permute-start(f32[32,640]{1,0:T(8,128)S(1)} %fusion.5), channel_id=1, source_target_pairs={{0,24},{1,25},{2,26},{3,27},{4,28},{5,29},{6,30},{7,31},{8,16},{9,... | collective-permute-start | bytes 245768 | tf_op jit(solution)/shard_map/ppermute | solution.py:299
  81.4 1.9 %collective-permute-start.28 = (f32[32,640]{1,0:T(8,128)S(1)}, f32[32,640]{1,0:T(8,128)S(1)}, u32[]{:S(2)}, u32[]{:S(2)}) collective-permute-start(f32[32,640]{1,0:T(8,128)S(1)} %fusion.5), channel_id=1, source_target_pairs={{0,8},{1,9},{2,10},{3,11},{4,12},{5,13},{6,14},{7,15},{8,0},{9,1},... | collective-permute-start | bytes 245768 | tf_op jit(solution)/shard_map/ppermute | solution.py:299
  83.3 2.1 %collective-permute-done.30 = f32[32,640]{1,0:T(8,128)S(1)} collective-permute-done((f32[32,640]{1,0:T(8,128)S(1)}, f32[32,640]{1,0:T(8,128)S(1)}, u32[]{:S(2)}, u32[]{:S(2)}) %collective-permute-start.30) | collective-permute-done | bytes 81952 | tf_op jit(solution)/shard_map/ppermute | solution.py:299
  85.5 3.1 %collective-permute-done.29 = f32[32,640]{1,0:T(8,128)S(1)} collective-permute-done((f32[32,640]{1,0:T(8,128)S(1)}, f32[32,640]{1,0:T(8,128)S(1)}, u32[]{:S(2)}, u32[]{:S(2)}) %collective-permute-start.29) | collective-permute-done | bytes 81952 | tf_op jit(solution)/shard_map/ppermute | solution.py:299
  88.6 1.5 %collective-permute-start.33 = (f32[32,640]{1,0:T(8,128)S(1)}, f32[32,640]{1,0:T(8,128)S(1)}, u32[]{:S(2)}, u32[]{:S(2)}) collective-permute-start(f32[32,640]{1,0:T(8,128)S(1)} %add_add_fusion.1.refs_8_), channel_id=1, source_target_pairs={{0,5},{1,4},{2,7},{3,6},{4,1},{5,0},{6,3},{7,2},{8,13},{9,12},{10,... | collective-permute-start | bytes 245768 | tf_op jit(solution)/shard_map/ppermute | solution.py:299
  90.1 1.1 collective-permute-start.32
  91.2 0.9 collective-permute-start.31
  92.1 2.1 %collective-permute-done.33.refs_11_ = f32[32,640]{1,0:T(8,128)S(1)} collective-permute-done((f32[32,640]{1,0:T(8,128)S(1)}, f32[32,640]{1,0:T(8,128)S(1)}, u32[]{:S(2)}, u32[]{:S(2)}) %collective-permute-start.33) | collective-permute-done | bytes 81952 | tf_op jit(solution)/shard_map/ppermute | solution.py:299
  94.7 0.9 collective-permute-done.31.refs_9_
  95.9 1.0 collective-permute-done.35.refs_13_
  96.9 6.7 %shard_map.107 = (f32[256,640]{1,0:T(8,128)S(1)}, f32[256,640]{1,0:T(8,128)S(1)}, f32[256,640]{1,0:T(8,128)S(1)}, f32[8,128]{1,0:T(8,128)S(1)}, f32[8,640]{1,0:T(8,128)S(1)}) custom-call(s32[1]{0:T(128)} %bitcast.place, f32[96,18,8,128]{3,2,1,0:T(8,128)S(1)} %get-tuple-element.22.refs_0_, f32[96,6,8,128]{3,2,1,0:T(8,128)S(1)} %get-tuple-element.23.refs_1_, ...), custom_call_target="tpu_custom_call" | custom-call | tf_op jit(solution)/shard_map/pallas_call | solution.py:274
  103.6 0.8 copy-done
  104.5 0.8 copy-done.1
  105.6 1.5 %collective-permute-done.38 = f32[128,640]{1,0:T(8,128)S(1)} collective-permute-done((f32[128,640]{1,0:T(8,128)S(1)}, f32[128,640]{1,0:T(8,128)S(1)}, u32[]{:S(2)}, u32[]{:S(2)}) %collective-permute-start.38) | collective-permute-done | bytes 327712 | tf_op jit(solution)/shard_map/ppermute | solution.py:299
  107.1 1.0 collective-permute-start.39
  108.1 1.5 %collective-permute-start.41 = (f32[32,640]{1,0:T(8,128)S(1)}, f32[32,640]{1,0:T(8,128)S(1)}, u32[]{:S(2)}, u32[]{:S(2)}) collective-permute-start(f32[32,640]{1,0:T(8,128)S(1)} %get-tuple-element.43), channel_id=1, source_target_pairs={{0,5},{1,4},{2,7},{3,6},{4,1},{5,0},{6,3},{7,2},{8,13},{9,12},{10,... | collective-permute-start | bytes 245768 | tf_op jit(solution)/shard_map/ppermute | solution.py:299
  109.6 1.1 collective-permute-start.40
  110.7 1.9 %collective-permute-done.39 = f32[32,640]{1,0:T(8,128)S(1)} collective-permute-done((f32[32,640]{1,0:T(8,128)S(1)}, f32[32,640]{1,0:T(8,128)S(1)}, u32[]{:S(2)}, u32[]{:S(2)}) %collective-permute-start.39) | collective-permute-done | bytes 81952 | tf_op jit(solution)/shard_map/ppermute | solution.py:299
  112.6 1.5 %collective-permute-done.41 = f32[32,640]{1,0:T(8,128)S(1)} collective-permute-done((f32[32,640]{1,0:T(8,128)S(1)}, f32[32,640]{1,0:T(8,128)S(1)}, u32[]{:S(2)}, u32[]{:S(2)}) %collective-permute-start.41) | collective-permute-done | bytes 81952 | tf_op jit(solution)/shard_map/ppermute | solution.py:299
  114.1 0.5 collective-permute-done.40
  114.7 2.1 %collective-permute-start.44 = (f32[32,640]{1,0:T(8,128)S(1)}, f32[32,640]{1,0:T(8,128)S(1)}, u32[]{:S(2)}, u32[]{:S(2)}) collective-permute-start(f32[32,640]{1,0:T(8,128)S(1)} %fusion.3), channel_id=1, source_target_pairs={{0,24},{1,25},{2,26},{3,27},{4,28},{5,29},{6,30},{7,31},{8,16},{9,... | collective-permute-start | bytes 245768 | tf_op jit(solution)/shard_map/ppermute | solution.py:299
  116.7 2.4 %collective-permute-start.42 = (f32[32,640]{1,0:T(8,128)S(1)}, f32[32,640]{1,0:T(8,128)S(1)}, u32[]{:S(2)}, u32[]{:S(2)}) collective-permute-start(f32[32,640]{1,0:T(8,128)S(1)} %fusion.3), channel_id=1, source_target_pairs={{0,8},{1,9},{2,10},{3,11},{4,12},{5,13},{6,14},{7,15},{8,0},{9,1},... | collective-permute-start | bytes 245768 | tf_op jit(solution)/shard_map/ppermute | solution.py:299
  119.1 2.7 %collective-permute-done.44 = f32[32,640]{1,0:T(8,128)S(1)} collective-permute-done((f32[32,640]{1,0:T(8,128)S(1)}, f32[32,640]{1,0:T(8,128)S(1)}, u32[]{:S(2)}, u32[]{:S(2)}) %collective-permute-start.44) | collective-permute-done | bytes 81952 | tf_op jit(solution)/shard_map/ppermute | solution.py:299
  121.8 1.9 %collective-permute-done.43 = f32[32,640]{1,0:T(8,128)S(1)} collective-permute-done((f32[32,640]{1,0:T(8,128)S(1)}, f32[32,640]{1,0:T(8,128)S(1)}, u32[]{:S(2)}, u32[]{:S(2)}) %collective-permute-start.43) | collective-permute-done | bytes 81952 | tf_op jit(solution)/shard_map/ppermute | solution.py:299
  123.7 0.7 add_add_fusion.piece
  124.4 1.7 %shard_map.108 = (f32[1,8,576]{2,1,0:T(8,128)}, f32[1,8,576]{2,1,0:T(8,128)}) custom-call(s32[1]{0:T(128)} %bitcast.place, f32[32,640]{1,0:T(8,128)} %add_add_fusion.piece, f32[256,640]{1,0:T(8,128)} %copy-done, f32[256,640]{1,0:T(8,128)} %copy-done.1, f32[8,128]{1,0:T(8,128)} %copy-done.3, f32[8,640]{1,0:T(8,128)} %copy-done.2), custom_call_target="tpu_custom_call" | custom-call | tf_op jit(solution)/shard_map/pallas_call | solution.py:350
  (66 shorter events, 4.3 us)
Async XLA Ops:
  1.4 15.4 %collective-permute-start = (f32[2,8,640]{2,1,0:T(8,128)S(1)}, f32[2,8,640]{2,1,0:T(8,128)S(1)}, u32[]{:S(2)}, u32[]{:S(2)}) collective-permute-start(f32[2,8,640]{2,1,0:T(8,128)S(1)} %get-tuple-element.52), channel_id=1, source_target_pairs={{0,8},{1,9},{2,10},{3,11},{4,12},{5,13},{6,14},{7,15},{8,0},{9,1},... | collective-permute-start | bytes 122888 | tf_op jit(solution)/shard_map/ppermute | solution.py:299
  4.4 12.4 %collective-permute-start.1 = (f32[2,8,640]{2,1,0:T(8,128)S(1)}, f32[2,8,640]{2,1,0:T(8,128)S(1)}, u32[]{:S(2)}, u32[]{:S(2)}) collective-permute-start(f32[2,8,640]{2,1,0:T(8,128)S(1)} %get-tuple-element.52), channel_id=1, source_target_pairs={{0,16},{1,17},{2,18},{3,19},{4,20},{5,21},{6,22},{7,23},{8,24},{9,... | collective-permute-start | bytes 122888 | tf_op jit(solution)/shard_map/ppermute | solution.py:299
  7.0 9.8 %collective-permute-start.2 = (f32[2,8,640]{2,1,0:T(8,128)S(1)}, f32[2,8,640]{2,1,0:T(8,128)S(1)}, u32[]{:S(2)}, u32[]{:S(2)}) collective-permute-start(f32[2,8,640]{2,1,0:T(8,128)S(1)} %get-tuple-element.52), channel_id=1, source_target_pairs={{0,24},{1,25},{2,26},{3,27},{4,28},{5,29},{6,30},{7,31},{8,16},{9,... | collective-permute-start | bytes 122888 | tf_op jit(solution)/shard_map/ppermute | solution.py:299
  8.7 0.7 copy-start.4
  16.9 8.1 %collective-permute-start.5 = (f32[4,2,8,640]{3,2,1,0:T(8,128)S(1)}, f32[4,2,8,640]{3,2,1,0:T(8,128)S(1)}, u32[]{:S(2)}, u32[]{:S(2)}) collective-permute-start(f32[4,2,8,640]{3,2,1,0:T(8,128)S(1)} %pad_maximum_fusion.refs_8_), channel_id=1, source_target_pairs={{0,5},{1,4},{2,7},{3,6},{4,1},{5,0},{6,3},{7,2},{8,13},{9,12},{10,... | collective-permute-start | bytes 491528 | tf_op jit(solution)/shard_map/ppermute | solution.py:299
  19.6 7.2 %collective-permute-start.4 = (f32[4,2,8,640]{3,2,1,0:T(8,128)S(1)}, f32[4,2,8,640]{3,2,1,0:T(8,128)S(1)}, u32[]{:S(2)}, u32[]{:S(2)}) collective-permute-start(f32[4,2,8,640]{3,2,1,0:T(8,128)S(1)} %pad_maximum_fusion.refs_8_), channel_id=1, source_target_pairs={{0,1},{1,0},{2,3},{3,2},{4,5},{5,4},{6,7},{7,6},{8,9},{9,8},{10,11... | collective-permute-start | bytes 491528 | tf_op jit(solution)/shard_map/ppermute | solution.py:299
  20.1 6.7 %collective-permute-start.3 = (f32[4,2,8,640]{3,2,1,0:T(8,128)S(1)}, f32[4,2,8,640]{3,2,1,0:T(8,128)S(1)}, u32[]{:S(2)}, u32[]{:S(2)}) collective-permute-start(f32[4,2,8,640]{3,2,1,0:T(8,128)S(1)} %pad_maximum_fusion.refs_8_), channel_id=1, source_target_pairs={{0,4},{1,5},{2,6},{3,7},{4,0},{5,1},{6,2},{7,3},{8,12},{9,13},{10,... | collective-permute-start | bytes 491528 | tf_op jit(solution)/shard_map/ppermute | solution.py:299
  20.5 7.0 %collective-permute-start.6 = (f32[4,2,8,640]{3,2,1,0:T(8,128)S(1)}, f32[4,2,8,640]{3,2,1,0:T(8,128)S(1)}, u32[]{:S(2)}, u32[]{:S(2)}) collective-permute-start(f32[4,2,8,640]{3,2,1,0:T(8,128)S(1)} %pad_maximum_fusion.refs_8_), channel_id=1, source_target_pairs={{0,2},{1,3},{2,0},{3,1},{4,6},{5,7},{6,4},{7,5},{8,10},{9,11},{10,... | collective-permute-start | bytes 491528 | tf_op jit(solution)/shard_map/ppermute | solution.py:299
  25.0 2.5 %collective-permute-start.9 = (f32[4,2,8,640]{3,2,1,0:T(8,128)S(1)}, f32[4,2,8,640]{3,2,1,0:T(8,128)S(1)}, u32[]{:S(2)}, u32[]{:S(2)}) collective-permute-start(f32[4,2,8,640]{3,2,1,0:T(8,128)S(1)} %collective-permute-done.5.refs_11_), channel_id=1, source_target_pairs={{0,2},{1,3},{2,0},{3,1},{4,6},{5,7},{6,4},{7,5},{8,10},{9,11},{10,... | collective-permute-start | bytes 491528 | tf_op jit(solution)/shard_map/ppermute | solution.py:299
  26.8 1.4 %collective-permute-start.8 = (f32[4,2,8,640]{3,2,1,0:T(8,128)S(1)}, f32[4,2,8,640]{3,2,1,0:T(8,128)S(1)}, u32[]{:S(2)}, u32[]{:S(2)}) collective-permute-start(f32[4,2,8,640]{3,2,1,0:T(8,128)S(1)} %collective-permute-done.4.refs_10_), channel_id=1, source_target_pairs={{0,2},{1,3},{2,0},{3,1},{4,6},{5,7},{6,4},{7,5},{8,10},{9,11},{10,... | collective-permute-start | bytes 491528 | tf_op jit(solution)/shard_map/ppermute | solution.py:299
  26.8 1.6 %collective-permute-start.7 = (f32[4,2,8,640]{3,2,1,0:T(8,128)S(1)}, f32[4,2,8,640]{3,2,1,0:T(8,128)S(1)}, u32[]{:S(2)}, u32[]{:S(2)}) collective-permute-start(f32[4,2,8,640]{3,2,1,0:T(8,128)S(1)} %collective-permute-done.3.refs_9_), channel_id=1, source_target_pairs={{0,2},{1,3},{2,0},{3,1},{4,6},{5,7},{6,4},{7,5},{8,10},{9,11},{10,... | collective-permute-start | bytes 491528 | tf_op jit(solution)/shard_map/ppermute | solution.py:299
  34.8 1.7 %collective-permute-start.10 = (f32[128,640]{1,0:T(8,128)S(1)}, f32[128,640]{1,0:T(8,128)S(1)}, u32[]{:S(2)}, u32[]{:S(2)}) collective-permute-start(f32[128,640]{1,0:T(8,128)S(1)} %slice.55), channel_id=1, source_target_pairs={{0,2},{1,3},{2,0},{3,1},{4,6},{5,7},{6,4},{7,5},{8,10},{9,11},{10,... | collective-permute-start | bytes 983048 | tf_op jit(solution)/shard_map/ppermute | solution.py:299
  36.5 4.7 %collective-permute-start.11 = (f32[32,640]{1,0:T(8,128)S(1)}, f32[32,640]{1,0:T(8,128)S(1)}, u32[]{:S(2)}, u32[]{:S(2)}) collective-permute-start(f32[32,640]{1,0:T(8,128)S(1)} %get-tuple-element.48), channel_id=1, source_target_pairs={{0,4},{1,5},{2,6},{3,7},{4,0},{5,1},{6,2},{7,3},{8,12},{9,13},{10,... | collective-permute-start | bytes 245768 | tf_op jit(solution)/shard_map/ppermute | solution.py:299
  37.8 6.1 %collective-permute-start.13 = (f32[32,640]{1,0:T(8,128)S(1)}, f32[32,640]{1,0:T(8,128)S(1)}, u32[]{:S(2)}, u32[]{:S(2)}) collective-permute-start(f32[32,640]{1,0:T(8,128)S(1)} %get-tuple-element.49), channel_id=1, source_target_pairs={{0,5},{1,4},{2,7},{3,6},{4,1},{5,0},{6,3},{7,2},{8,13},{9,12},{10,... | collective-permute-start | bytes 245768 | tf_op jit(solution)/shard_map/ppermute | solution.py:299
  39.6 4.7 %collective-permute-start.12 = (f32[32,640]{1,0:T(8,128)S(1)}, f32[32,640]{1,0:T(8,128)S(1)}, u32[]{:S(2)}, u32[]{:S(2)}) collective-permute-start(f32[32,640]{1,0:T(8,128)S(1)} %get-tuple-element.50), channel_id=1, source_target_pairs={{0,1},{1,0},{2,3},{3,2},{4,5},{5,4},{6,7},{7,6},{8,9},{9,8},{10,11... | collective-permute-start | bytes 245768 | tf_op jit(solution)/shard_map/ppermute | solution.py:299
  44.3 6.8 %collective-permute-start.16 = (f32[32,640]{1,0:T(8,128)S(1)}, f32[32,640]{1,0:T(8,128)S(1)}, u32[]{:S(2)}, u32[]{:S(2)}) collective-permute-start(f32[32,640]{1,0:T(8,128)S(1)} %fusion.7), channel_id=1, source_target_pairs={{0,24},{1,25},{2,26},{3,27},{4,28},{5,29},{6,30},{7,31},{8,16},{9,... | collective-permute-start | bytes 245768 | tf_op jit(solution)/shard_map/ppermute | solution.py:299
  47.9 6.2 %collective-permute-start.15 = (f32[32,640]{1,0:T(8,128)S(1)}, f32[32,640]{1,0:T(8,128)S(1)}, u32[]{:S(2)}, u32[]{:S(2)}) collective-permute-start(f32[32,640]{1,0:T(8,128)S(1)} %fusion.7), channel_id=1, source_target_pairs={{0,16},{1,17},{2,18},{3,19},{4,20},{5,21},{6,22},{7,23},{8,24},{9,... | collective-permute-start | bytes 245768 | tf_op jit(solution)/shard_map/ppermute | solution.py:299
  47.9 6.2 %collective-permute-start.14 = (f32[32,640]{1,0:T(8,128)S(1)}, f32[32,640]{1,0:T(8,128)S(1)}, u32[]{:S(2)}, u32[]{:S(2)}) collective-permute-start(f32[32,640]{1,0:T(8,128)S(1)} %fusion.7), channel_id=1, source_target_pairs={{0,8},{1,9},{2,10},{3,11},{4,12},{5,13},{6,14},{7,15},{8,0},{9,1},... | collective-permute-start | bytes 245768 | tf_op jit(solution)/shard_map/ppermute | solution.py:299
  54.1 6.0 %collective-permute-start.19 = (f32[32,640]{1,0:T(8,128)S(1)}, f32[32,640]{1,0:T(8,128)S(1)}, u32[]{:S(2)}, u32[]{:S(2)}) collective-permute-start(f32[32,640]{1,0:T(8,128)S(1)} %add_add_fusion.2.refs_8_), channel_id=1, source_target_pairs={{0,5},{1,4},{2,7},{3,6},{4,1},{5,0},{6,3},{7,2},{8,13},{9,12},{10,... | collective-permute-start | bytes 245768 | tf_op jit(solution)/shard_map/ppermute | solution.py:299
  56.1 4.4 %collective-permute-start.18 = (f32[32,640]{1,0:T(8,128)S(1)}, f32[32,640]{1,0:T(8,128)S(1)}, u32[]{:S(2)}, u32[]{:S(2)}) collective-permute-start(f32[32,640]{1,0:T(8,128)S(1)} %add_add_fusion.2.refs_8_), channel_id=1, source_target_pairs={{0,1},{1,0},{2,3},{3,2},{4,5},{5,4},{6,7},{7,6},{8,9},{9,8},{10,11... | collective-permute-start | bytes 245768 | tf_op jit(solution)/shard_map/ppermute | solution.py:299
  56.9 4.4 %collective-permute-start.17 = (f32[32,640]{1,0:T(8,128)S(1)}, f32[32,640]{1,0:T(8,128)S(1)}, u32[]{:S(2)}, u32[]{:S(2)}) collective-permute-start(f32[32,640]{1,0:T(8,128)S(1)} %add_add_fusion.2.refs_8_), channel_id=1, source_target_pairs={{0,4},{1,5},{2,6},{3,7},{4,0},{5,1},{6,2},{7,3},{8,12},{9,13},{10,... | collective-permute-start | bytes 245768 | tf_op jit(solution)/shard_map/ppermute | solution.py:299
  57.7 3.7 %collective-permute-start.20 = (f32[32,640]{1,0:T(8,128)S(1)}, f32[32,640]{1,0:T(8,128)S(1)}, u32[]{:S(2)}, u32[]{:S(2)}) collective-permute-start(f32[32,640]{1,0:T(8,128)S(1)} %add_add_fusion.2.refs_8_), channel_id=1, source_target_pairs={{0,2},{1,3},{2,0},{3,1},{4,6},{5,7},{6,4},{7,5},{8,10},{9,11},{10,... | collective-permute-start | bytes 245768 | tf_op jit(solution)/shard_map/ppermute | solution.py:299
  60.1 1.3 %collective-permute-start.23 = (f32[32,640]{1,0:T(8,128)S(1)}, f32[32,640]{1,0:T(8,128)S(1)}, u32[]{:S(2)}, u32[]{:S(2)}) collective-permute-start(f32[32,640]{1,0:T(8,128)S(1)} %collective-permute-done.19.refs_11_), channel_id=1, source_target_pairs={{0,2},{1,3},{2,0},{3,1},{4,6},{5,7},{6,4},{7,5},{8,10},{9,11},{10,... | collective-permute-start | bytes 245768 | tf_op jit(solution)/shard_map/ppermute | solution.py:299
  60.5 1.3 %collective-permute-start.22 = (f32[32,640]{1,0:T(8,128)S(1)}, f32[32,640]{1,0:T(8,128)S(1)}, u32[]{:S(2)}, u32[]{:S(2)}) collective-permute-start(f32[32,640]{1,0:T(8,128)S(1)} %collective-permute-done.18.refs_10_), channel_id=1, source_target_pairs={{0,2},{1,3},{2,0},{3,1},{4,6},{5,7},{6,4},{7,5},{8,10},{9,11},{10,... | collective-permute-start | bytes 245768 | tf_op jit(solution)/shard_map/ppermute | solution.py:299
  61.3 1.3 %collective-permute-start.21 = (f32[32,640]{1,0:T(8,128)S(1)}, f32[32,640]{1,0:T(8,128)S(1)}, u32[]{:S(2)}, u32[]{:S(2)}) collective-permute-start(f32[32,640]{1,0:T(8,128)S(1)} %collective-permute-done.17.refs_9_), channel_id=1, source_target_pairs={{0,2},{1,3},{2,0},{3,1},{4,6},{5,7},{6,4},{7,5},{8,10},{9,11},{10,... | collective-permute-start | bytes 245768 | tf_op jit(solution)/shard_map/ppermute | solution.py:299
  69.5 1.7 %collective-permute-start.24 = (f32[128,640]{1,0:T(8,128)S(1)}, f32[128,640]{1,0:T(8,128)S(1)}, u32[]{:S(2)}, u32[]{:S(2)}) collective-permute-start(f32[128,640]{1,0:T(8,128)S(1)} %slice.61), channel_id=1, source_target_pairs={{0,2},{1,3},{2,0},{3,1},{4,6},{5,7},{6,4},{7,5},{8,10},{9,11},{10,... | collective-permute-start | bytes 983048 | tf_op jit(solution)/shard_map/ppermute | solution.py:299
  71.3 5.6 %collective-permute-start.25 = (f32[32,640]{1,0:T(8,128)S(1)}, f32[32,640]{1,0:T(8,128)S(1)}, u32[]{:S(2)}, u32[]{:S(2)}) collective-permute-start(f32[32,640]{1,0:T(8,128)S(1)} %get-tuple-element.45), channel_id=1, source_target_pairs={{0,4},{1,5},{2,6},{3,7},{4,0},{5,1},{6,2},{7,3},{8,12},{9,13},{10,... | collective-permute-start | bytes 245768 | tf_op jit(solution)/shard_map/ppermute | solution.py:299
  72.1 6.2 %collective-permute-start.27 = (f32[32,640]{1,0:T(8,128)S(1)}, f32[32,640]{1,0:T(8,128)S(1)}, u32[]{:S(2)}, u32[]{:S(2)}) collective-permute-start(f32[32,640]{1,0:T(8,128)S(1)} %get-tuple-element.46), channel_id=1, source_target_pairs={{0,5},{1,4},{2,7},{3,6},{4,1},{5,0},{6,3},{7,2},{8,13},{9,12},{10,... | collective-permute-start | bytes 245768 | tf_op jit(solution)/shard_map/ppermute | solution.py:299
  74.0 4.8 %collective-permute-start.26 = (f32[32,640]{1,0:T(8,128)S(1)}, f32[32,640]{1,0:T(8,128)S(1)}, u32[]{:S(2)}, u32[]{:S(2)}) collective-permute-start(f32[32,640]{1,0:T(8,128)S(1)} %get-tuple-element.47), channel_id=1, source_target_pairs={{0,1},{1,0},{2,3},{3,2},{4,5},{5,4},{6,7},{7,6},{8,9},{9,8},{10,11... | collective-permute-start | bytes 245768 | tf_op jit(solution)/shard_map/ppermute | solution.py:299
  78.9 6.6 %collective-permute-start.30 = (f32[32,640]{1,0:T(8,128)S(1)}, f32[32,640]{1,0:T(8,128)S(1)}, u32[]{:S(2)}, u32[]{:S(2)}) collective-permute-start(f32[32,640]{1,0:T(8,128)S(1)} %fusion.5), channel_id=1, source_target_pairs={{0,24},{1,25},{2,26},{3,27},{4,28},{5,29},{6,30},{7,31},{8,16},{9,... | collective-permute-start | bytes 245768 | tf_op jit(solution)/shard_map/ppermute | solution.py:299
  81.4 7.1 %collective-permute-start.29 = (f32[32,640]{1,0:T(8,128)S(1)}, f32[32,640]{1,0:T(8,128)S(1)}, u32[]{:S(2)}, u32[]{:S(2)}) collective-permute-start(f32[32,640]{1,0:T(8,128)S(1)} %fusion.5), channel_id=1, source_target_pairs={{0,16},{1,17},{2,18},{3,19},{4,20},{5,21},{6,22},{7,23},{8,24},{9,... | collective-permute-start | bytes 245768 | tf_op jit(solution)/shard_map/ppermute | solution.py:299
  81.4 7.1 %collective-permute-start.28 = (f32[32,640]{1,0:T(8,128)S(1)}, f32[32,640]{1,0:T(8,128)S(1)}, u32[]{:S(2)}, u32[]{:S(2)}) collective-permute-start(f32[32,640]{1,0:T(8,128)S(1)} %fusion.5), channel_id=1, source_target_pairs={{0,8},{1,9},{2,10},{3,11},{4,12},{5,13},{6,14},{7,15},{8,0},{9,1},... | collective-permute-start | bytes 245768 | tf_op jit(solution)/shard_map/ppermute | solution.py:299
  88.6 5.6 %collective-permute-start.33 = (f32[32,640]{1,0:T(8,128)S(1)}, f32[32,640]{1,0:T(8,128)S(1)}, u32[]{:S(2)}, u32[]{:S(2)}) collective-permute-start(f32[32,640]{1,0:T(8,128)S(1)} %add_add_fusion.1.refs_8_), channel_id=1, source_target_pairs={{0,5},{1,4},{2,7},{3,6},{4,1},{5,0},{6,3},{7,2},{8,13},{9,12},{10,... | collective-permute-start | bytes 245768 | tf_op jit(solution)/shard_map/ppermute | solution.py:299
  90.1 4.5 %collective-permute-start.32 = (f32[32,640]{1,0:T(8,128)S(1)}, f32[32,640]{1,0:T(8,128)S(1)}, u32[]{:S(2)}, u32[]{:S(2)}) collective-permute-start(f32[32,640]{1,0:T(8,128)S(1)} %add_add_fusion.1.refs_8_), channel_id=1, source_target_pairs={{0,1},{1,0},{2,3},{3,2},{4,5},{5,4},{6,7},{7,6},{8,9},{9,8},{10,11... | collective-permute-start | bytes 245768 | tf_op jit(solution)/shard_map/ppermute | solution.py:299
  91.2 4.4 %collective-permute-start.31 = (f32[32,640]{1,0:T(8,128)S(1)}, f32[32,640]{1,0:T(8,128)S(1)}, u32[]{:S(2)}, u32[]{:S(2)}) collective-permute-start(f32[32,640]{1,0:T(8,128)S(1)} %add_add_fusion.1.refs_8_), channel_id=1, source_target_pairs={{0,4},{1,5},{2,6},{3,7},{4,0},{5,1},{6,2},{7,3},{8,12},{9,13},{10,... | collective-permute-start | bytes 245768 | tf_op jit(solution)/shard_map/ppermute | solution.py:299
  92.1 3.5 %collective-permute-start.34 = (f32[32,640]{1,0:T(8,128)S(1)}, f32[32,640]{1,0:T(8,128)S(1)}, u32[]{:S(2)}, u32[]{:S(2)}) collective-permute-start(f32[32,640]{1,0:T(8,128)S(1)} %add_add_fusion.1.refs_8_), channel_id=1, source_target_pairs={{0,2},{1,3},{2,0},{3,1},{4,6},{5,7},{6,4},{7,5},{8,10},{9,11},{10,... | collective-permute-start | bytes 245768 | tf_op jit(solution)/shard_map/ppermute | solution.py:299
  94.2 1.5 %collective-permute-start.37 = (f32[32,640]{1,0:T(8,128)S(1)}, f32[32,640]{1,0:T(8,128)S(1)}, u32[]{:S(2)}, u32[]{:S(2)}) collective-permute-start(f32[32,640]{1,0:T(8,128)S(1)} %collective-permute-done.33.refs_11_), channel_id=1, source_target_pairs={{0,2},{1,3},{2,0},{3,1},{4,6},{5,7},{6,4},{7,5},{8,10},{9,11},{10,... | collective-permute-start | bytes 245768 | tf_op jit(solution)/shard_map/ppermute | solution.py:299
  94.6 1.3 %collective-permute-start.36 = (f32[32,640]{1,0:T(8,128)S(1)}, f32[32,640]{1,0:T(8,128)S(1)}, u32[]{:S(2)}, u32[]{:S(2)}) collective-permute-start(f32[32,640]{1,0:T(8,128)S(1)} %collective-permute-done.32.refs_10_), channel_id=1, source_target_pairs={{0,2},{1,3},{2,0},{3,1},{4,6},{5,7},{6,4},{7,5},{8,10},{9,11},{10,... | collective-permute-start | bytes 245768 | tf_op jit(solution)/shard_map/ppermute | solution.py:299
  95.7 1.3 %collective-permute-start.35 = (f32[32,640]{1,0:T(8,128)S(1)}, f32[32,640]{1,0:T(8,128)S(1)}, u32[]{:S(2)}, u32[]{:S(2)}) collective-permute-start(f32[32,640]{1,0:T(8,128)S(1)} %collective-permute-done.31.refs_9_), channel_id=1, source_target_pairs={{0,2},{1,3},{2,0},{3,1},{4,6},{5,7},{6,4},{7,5},{8,10},{9,11},{10,... | collective-permute-start | bytes 245768 | tf_op jit(solution)/shard_map/ppermute | solution.py:299
  103.6 0.9 copy-start
  104.5 0.8 copy-start.1
  105.3 1.8 %copy-start.2 = (f32[8,640]{1,0:T(8,128)}, f32[8,640]{1,0:T(8,128)S(1)}, u32[]{:S(2)}) copy-start(f32[8,640]{1,0:T(8,128)S(1)} %get-tuple-element.41.old_answer) | copy-start | bytes 61444
  105.3 1.8 %copy-start.3 = (f32[8,128]{1,0:T(8,128)}, f32[8,128]{1,0:T(8,128)S(1)}, u32[]{:S(2)}) copy-start(f32[8,128]{1,0:T(8,128)S(1)} %get-tuple-element.40.energy) | copy-start | bytes 12292
  105.3 1.7 %collective-permute-start.38 = (f32[128,640]{1,0:T(8,128)S(1)}, f32[128,640]{1,0:T(8,128)S(1)}, u32[]{:S(2)}, u32[]{:S(2)}) collective-permute-start(f32[128,640]{1,0:T(8,128)S(1)} %slice.67), channel_id=1, source_target_pairs={{0,2},{1,3},{2,0},{3,1},{4,6},{5,7},{6,4},{7,5},{8,10},{9,11},{10,... | collective-permute-start | bytes 983048 | tf_op jit(solution)/shard_map/ppermute | solution.py:299
  107.1 5.4 %collective-permute-start.39 = (f32[32,640]{1,0:T(8,128)S(1)}, f32[32,640]{1,0:T(8,128)S(1)}, u32[]{:S(2)}, u32[]{:S(2)}) collective-permute-start(f32[32,640]{1,0:T(8,128)S(1)} %get-tuple-element.42), channel_id=1, source_target_pairs={{0,4},{1,5},{2,6},{3,7},{4,0},{5,1},{6,2},{7,3},{8,12},{9,13},{10,... | collective-permute-start | bytes 245768 | tf_op jit(solution)/shard_map/ppermute | solution.py:299
  108.1 6.0 %collective-permute-start.41 = (f32[32,640]{1,0:T(8,128)S(1)}, f32[32,640]{1,0:T(8,128)S(1)}, u32[]{:S(2)}, u32[]{:S(2)}) collective-permute-start(f32[32,640]{1,0:T(8,128)S(1)} %get-tuple-element.43), channel_id=1, source_target_pairs={{0,5},{1,4},{2,7},{3,6},{4,1},{5,0},{6,3},{7,2},{8,13},{9,12},{10,... | collective-permute-start | bytes 245768 | tf_op jit(solution)/shard_map/ppermute | solution.py:299
  109.6 5.1 %collective-permute-start.40 = (f32[32,640]{1,0:T(8,128)S(1)}, f32[32,640]{1,0:T(8,128)S(1)}, u32[]{:S(2)}, u32[]{:S(2)}) collective-permute-start(f32[32,640]{1,0:T(8,128)S(1)} %get-tuple-element.44), channel_id=1, source_target_pairs={{0,1},{1,0},{2,3},{3,2},{4,5},{5,4},{6,7},{7,6},{8,9},{9,8},{10,11... | collective-permute-start | bytes 245768 | tf_op jit(solution)/shard_map/ppermute | solution.py:299
  114.7 7.2 %collective-permute-start.44 = (f32[32,640]{1,0:T(8,128)S(1)}, f32[32,640]{1,0:T(8,128)S(1)}, u32[]{:S(2)}, u32[]{:S(2)}) collective-permute-start(f32[32,640]{1,0:T(8,128)S(1)} %fusion.3), channel_id=1, source_target_pairs={{0,24},{1,25},{2,26},{3,27},{4,28},{5,29},{6,30},{7,31},{8,16},{9,... | collective-permute-start | bytes 245768 | tf_op jit(solution)/shard_map/ppermute | solution.py:299
  116.7 7.0 %collective-permute-start.43 = (f32[32,640]{1,0:T(8,128)S(1)}, f32[32,640]{1,0:T(8,128)S(1)}, u32[]{:S(2)}, u32[]{:S(2)}) collective-permute-start(f32[32,640]{1,0:T(8,128)S(1)} %fusion.3), channel_id=1, source_target_pairs={{0,16},{1,17},{2,18},{3,19},{4,20},{5,21},{6,22},{7,23},{8,24},{9,... | collective-permute-start | bytes 245768 | tf_op jit(solution)/shard_map/ppermute | solution.py:299
  116.7 7.0 %collective-permute-start.42 = (f32[32,640]{1,0:T(8,128)S(1)}, f32[32,640]{1,0:T(8,128)S(1)}, u32[]{:S(2)}, u32[]{:S(2)}) collective-permute-start(f32[32,640]{1,0:T(8,128)S(1)} %fusion.3), channel_id=1, source_target_pairs={{0,8},{1,9},{2,10},{3,11},{4,12},{5,13},{6,14},{7,15},{8,0},{9,1},... | collective-permute-start | bytes 245768 | tf_op jit(solution)/shard_map/ppermute | solution.py:299

commit v3 on v2

v3 whole, which is shorter than its diff:
```python
import functools
import math

import jax
import jax.numpy as jnp
from jax import lax
from jax.experimental import pallas as pl
from jax.experimental.pallas import tpu as pltpu
from jax.sharding import PartitionSpec as P

ITERS = 3
CPAR = 9
CAMERAS = 64
SLOTS = 8
POINTS = 128
TILE = CPAR * CAMERAS
PAIRS = 5
WIDTH = PAIRS * 128
CHUNKS = 2
AXES = ("pts", "cam")


def split_two(value):
    high = value.astype(jnp.bfloat16)
    low = (value - high.astype(jnp.float32)).astype(jnp.bfloat16)
    return high, low


def all_slots(value):
    for by in (4, 2, 1):
        value = value + pltpu.roll(value, by, 0)
    return value


def invert(gram):
    a, b, c, d, e, f = gram
    aa = d * f - e * e
    bb = c * e - b * f
    cc = b * e - c * d
    dd = a * f - c * c
    ee = b * c - a * e
    ff = a * d - b * b
    scale = 1.0 / (a * aa + b * bb + c * cc)
    return [entry * scale for entry in (aa, bb, cc, dd, ee, ff)]


def setup_kernel(
    skip, group, counts, cam, point, index, damp,
    cam_out, point_out, index_out, inverse_out, selector_out, damping, arrived,
):
    tiles = cam_out.shape[0]
    turns = tiles // group

    def copy(array, out, turn, kind):
        here = pl.ds(turn * group, group)
        there = pl.ds(skip + turn * group, group)
        return pltpu.make_async_copy(array.at[there], out.at[here], arrived.at[kind, turn])

    damping_copy = pltpu.make_async_copy(damp.at[:, pl.ds(skip, tiles)], damping, arrived.at[3, 0])
    damping_copy.start()
    for kind, (array, out) in enumerate(((point, point_out), (index, index_out), (cam, cam_out))):
        for turn in range(turns):
            copy(array, out, turn, kind).start()
    slot = lax.broadcasted_iota(jnp.int32, (SLOTS, POINTS), 0)
    camera = lax.broadcasted_iota(jnp.int32, (CAMERAS, POINTS), 0).astype(jnp.bfloat16)
    one = jnp.ones((CAMERAS, POINTS), jnp.bfloat16)
    zero = jnp.zeros((CAMERAS, POINTS), jnp.bfloat16)
    damping_copy.wait()
    for turn in range(turns):
        copy(point, point_out, turn, 0).wait()
        copy(index, index_out, turn, 1).wait()
        for i in range(turn * group, (turn + 1) * group):
            live = (slot < counts[skip + i]).astype(jnp.float32)
            rows = [point_out[i, r] * live for r in range(6)]
            entries = [(0, 0), (0, 1), (0, 2), (1, 1), (1, 2), (2, 2)]
            gram = [all_slots(rows[a] * rows[b] + rows[3 + a] * rows[3 + b]) for a, b in entries]
            for a, entry in enumerate((0, 3, 5)):
                gram[entry] = gram[entry] + damping[a, i : i + 1, :]
            for a, entry in enumerate(invert(gram)):
                inverse_out[i, a] = entry
            wide = index_out[i].astype(jnp.float32)
            for k in range(SLOTS):
                row = wide[k : k + 1, :].astype(jnp.bfloat16)
                down, right = k // 2 * CAMERAS, k % 2 * POINTS
                selector_out[i, down : down + CAMERAS, right : right + POINTS] = jnp.where(
                    camera == row, one, zero
                )
    for turn in range(turns):
        copy(cam, cam_out, turn, 2).wait()


def tile_product(cam, point, index, inverse, selector, picked_from, row, put_to):
    slot = lax.broadcasted_iota(jnp.int32, (SLOTS, POINTS), 0)
    lane = lax.broadcasted_iota(jnp.int32, (SLOTS, POINTS), 1)
    other = index + CAMERAS
    pairs = [picked_from[pl.ds(row, SLOTS), p * 128 : (p + 1) * 128] for p in range(PAIRS)]
    picked = [
        jnp.take_along_axis(
            pairs[j // 2], other if j % 2 else index, axis=1, mode="promise_in_bounds"
        )
        for j in range(CPAR)
    ]
    rows = [point(r) for r in range(6)]
    q = []
    for r in range(2):
        total = cam(9 * r) * picked[0]
        for j in range(1, CPAR):
            total = total + cam(9 * r + j) * picked[j]
        q.append(total)
    y = [all_slots(rows[a] * q[0] + rows[3 + a] * q[1]) for a in range(3)]
    i0, i1, i2, i3, i4, i5 = [inverse(a) for a in range(6)]
    z = [
        i0 * y[0] + i1 * y[1] + i2 * y[2],
        i1 * y[0] + i3 * y[1] + i4 * y[2],
        i2 * y[0] + i4 * y[1] + i5 * y[2],
    ]
    e = [
        q[r] - (rows[3 * r] * z[0] + rows[3 * r + 1] * z[1] + rows[3 * r + 2] * z[2])
        for r in range(2)
    ]
    slot_twice = lax.broadcasted_iota(jnp.int32, (2 * SLOTS, POINTS), 0) & 1
    odd = slot_twice.astype(jnp.bfloat16)
    even = (1 - slot_twice).astype(jnp.bfloat16)
    returned = [cam(j) * e[0] + cam(9 + j) * e[1] for j in range(CPAR)]
    left = []
    for p in range(PAIRS - 1):
        left += split_two(jnp.concatenate(returned[2 * p : 2 * p + 2], axis=0))
    high = returned[-1].astype(jnp.bfloat16).astype(jnp.float32)
    left.append(jnp.concatenate([high, returned[-1] - high], axis=0).astype(jnp.bfloat16))
    left = jnp.concatenate(
        [jnp.concatenate([rows * even, rows * odd], axis=1) for rows in left], axis=0
    )
    spread = lax.dot_general(
        left, selector, (((1,), (1,)), ((), ())), preferred_element_type=jnp.float32
    )
    side = (slot >> 1) & 1
    first_side = side == 0
    keep = (lane >> 6) == side
    sums = []
    for j in range(CPAR):
        first = 32 * (j // 2) + 8 * (j % 2)
        second = first + (16 if j < CPAR - 1 else 8)
        both = spread[first : first + 8] + spread[second : second + 8]
        sums.append(jnp.where(slot < 4, both[:, :128], both[:, 128:]))
    sums.append(jnp.zeros_like(sums[0]))
    for p in range(PAIRS):
        one, two = sums[2 * p], sums[2 * p + 1]
        stay = jnp.where(first_side, one, two)
        move = pltpu.roll(jnp.where(first_side, two, one), CAMERAS, 1)
        put_to[pl.ds(row, SLOTS), p * 128 : (p + 1) * 128] = jnp.where(keep, stay, move)
    return q[0] * e[0] + q[1] * e[1]


def wide_dot(table, value):
    both = jnp.dot(
        table, jnp.concatenate(split_two(value), axis=1), preferred_element_type=jnp.float32
    )
    return both[:, :WIDTH] + both[:, WIDTH:]


def product_steps(problem, pick, put, vector, out, picked_from, put_to):
    picked_from[...] = wide_dot(pick[...], vector[...])
    total = jnp.zeros((SLOTS, POINTS), jnp.float32)
    row = 0
    for cam, point, index, inverse, selector in problem:
        for i in range(cam.shape[0]):
            total = total + tile_product(
                lambda r: cam[i, r],
                lambda r: point[i, r],
                index[i],
                lambda a: inverse[i, a],
                selector[i],
                picked_from,
                row,
                put_to,
            )
            row += SLOTS
    out[...] = wide_dot(put[...], put_to[...])
    return total


def total_of(value):
    return jnp.sum(value, keepdims=True).reshape(1, 1)


def in_spare(rows, value):
    lane = lax.broadcasted_iota(jnp.int32, (rows, 128), 1)
    return jnp.where(lane >= TILE - (WIDTH - 128), value, 0.0)


def spare_of(ref):
    return ref[0:1, TILE : TILE + 1]


def offer(residual, scaling, scaled):
    value = scaling[...] * residual[...]
    scaled[...] = value
    part = total_of(value * residual[...])
    scaled[:, WIDTH - 128 :] += in_spare(scaled.shape[0], part)


def start_kernel(*refs):
    pieces, (residual, scaling, scaled) = refs[:-4], refs[-3:]
    rows = pieces[0].shape[1]
    for away, piece in enumerate(pieces):
        residual[away * rows : (away + 1) * rows, :] = piece[0]
        scaling[away * rows : (away + 1) * rows, :] = piece[1]
    offer(residual, scaling, scaled)


def turn_kernel(ring, *refs):
    pieces, refs = refs[:ring], refs[ring:]
    energy, vector, old_answer, old_residual, scaling, answer, residual, scaled = refs
    rows = answer.shape[0]
    step_size = energy[0:1, 0:1] / sum([spare_of(piece) for piece in pieces])
    for b in range(ring):
        here = slice(b * rows, (b + 1) * rows)
        mapped = pieces[0][here, :]
        for a in range(1, ring):
            mapped = mapped + pieces[a][(a ^ b) * rows : ((a ^ b) + 1) * rows, :]
        residual[here, :] = old_residual[here, :] - step_size * mapped
    answer[...] = old_answer[...] + step_size * vector[:rows, :]
    offer(residual, scaling, scaled)


def last_kernel(ring, *refs):
    pieces, (energy, vector, old_answer, old_residual, answer, residual) = refs[:ring], refs[ring:]
    rows = old_answer.shape[0]
    mapped = sum([piece[...] for piece in pieces[1:]], pieces[0][...])
    step_size = energy[0:1, 0:1] / mapped[0:1, TILE : TILE + 1]
    answer[0] = (old_answer[...] + step_size * vector[:rows, :])[:, :TILE]
    residual[0] = (old_residual[:rows, :] - step_size * mapped)[:, :TILE]


def step_kernel(chunks, ranks, first, *refs):
    problem = [refs[5 * c : 5 * c + 5] for c in range(chunks)]
    (pick, put, damp), refs = refs[5 * chunks : 5 * chunks + 3], refs[5 * chunks + 3 :]
    pieces, refs = refs[:ranks], refs[ranks:]
    if not first:
        (old_vector, old_energy), refs = refs[:2], refs[2:]
    out, vector, energy, picked_from, put_to = refs
    power = sum([spare_of(piece) for piece in pieces])
    energy[...] = jnp.broadcast_to(power, energy.shape)
    many = pieces[0].shape[0]
    for r in range(ranks):
        part = slice(r * many, (r + 1) * many)
        if first:
            vector[part, :] = pieces[r][...]
        else:
            vector[part, :] = pieces[r][...] + (power / old_energy[0:1, 0:1]) * old_vector[part, :]
    dot = product_steps(problem, pick, put, vector, out, picked_from, put_to)
    rows = damp.shape[0]
    damped = damp[...] * vector[:rows, :]
    out[:rows, :] += damped
    out[:, WIDTH - 128 :] += in_spare(out.shape[0], total_of(dot) + total_of(damped * vector[:rows, :]))


def plain_kernel(chunks, *refs):
    problem = [refs[5 * c : 5 * c + 5] for c in range(chunks)]
    pick, put, vector, out, picked_from, put_to = refs[5 * chunks :]
    product_steps(problem, pick, put, vector, out, picked_from, put_to)


def in_vmem(kernel, operands, outs, scratch=()):
    spec = pl.BlockSpec(memory_space=pltpu.VMEM)
    return pl.pallas_call(
        kernel,
        out_shape=[jax.ShapeDtypeStruct(shape, jnp.float32) for shape in outs],
        in_specs=[spec] * len(operands),
        out_specs=[spec] * len(outs),
        scratch_shapes=list(scratch),
        compiler_params=pltpu.CompilerParams(vmem_limit_bytes=20 * 2**20),
    )(*operands)


def call_setup(skip, tiles, counts, cam, point, index, damp):
    group = math.gcd(tiles, 8)
    shapes = [(tiles,) + array.shape[1:] for array in (cam, point, index)]
    shapes += [(tiles, 6, SLOTS, POINTS), (tiles, SLOTS // 2 * CAMERAS, 2 * POINTS)]
    kinds = [jnp.float32, jnp.float32, jnp.int32, jnp.float32, jnp.bfloat16]
    return pl.pallas_call(
        functools.partial(setup_kernel, skip, group),
        out_shape=[pltpu.VMEM(shape, kind) for shape, kind in zip(shapes, kinds)],
        in_specs=[pl.BlockSpec(memory_space=pltpu.SMEM)] + [pl.BlockSpec(memory_space=pltpu.HBM)] * 4,
        out_specs=[pl.BlockSpec(memory_space=pltpu.VMEM)] * 5,
        scratch_shapes=[
            pltpu.VMEM((3, tiles, POINTS), jnp.float32),
            pltpu.SemaphoreType.DMA((4, tiles // group)),
        ],
        compiler_params=pltpu.CompilerParams(vmem_limit_bytes=4 * 2**20),
        cost_estimate=pl.CostEstimate(flops=3 * 10**7, bytes_accessed=10**7, transcendentals=0),
    )(counts, *[pltpu.with_memory_space_constraint(x, pltpu.HBM) for x in (cam, point, index, damp)])


def call_product(kernel, problem, others, outs):
    tiles = sum(chunk[0].shape[0] for chunk in problem)
    scratch = pltpu.VMEM((tiles * SLOTS, WIDTH), jnp.float32)
    held = [pltpu.with_memory_space_constraint(array, pltpu.VMEM) for chunk in problem for array in chunk]
    return in_vmem(kernel, held + others, outs, [scratch, scratch])


def tables_of(rows, counts, window):
    live = lax.iota(jnp.int32, SLOTS)[None, :] < counts[:, None]
    listed = jnp.where(live, rows, -1).reshape(-1)
    places = lax.iota(jnp.int32, window)
    pick = (listed[:, None] == places[None, :]).astype(jnp.bfloat16)
    put = (places[:, None] == listed[None, :]).astype(jnp.bfloat16)
    return [pick, put]


def widen(array):
    return jnp.pad(array, [(0, 0)] * (array.ndim - 1) + [(0, WIDTH - TILE)])


def exchange(array, mask):
    devices = lax.axis_size("pts") * lax.axis_size("cam")
    return lax.ppermute(array, AXES, [(i, i ^ mask) for i in range(devices)])


def two_groups(rhs, damp_cam, precond, problem, tile_ids, counts):
    CAM, CORE, Y, Z = 1, 2, 4, 8
    shards = lax.axis_size("pts")
    tiles = rhs.shape[0]
    ring = shards // 4
    group, shard = lax.axis_index("cam"), lax.axis_index("pts")
    group_tiles = shards * tiles
    window = 2 * group_tiles
    where = (group * group_tiles + tile_ids - group_tiles // 2) % window
    owner_group, owner = where // group_tiles, where % group_tiles // tiles
    apart = owner ^ shard
    rank = (apart & 1) * 4 + (owner_group ^ group) * 2 + ((apart >> 1) & 1)
    tables = tables_of((rank * ring + (apart >> 2)) * tiles + where % tiles, counts, window)
    steady = tables + [widen(damp_cam)]

    def gather(own, ahead=None):
        near = [own, exchange(own, Y), exchange(own, CAM), exchange(own, CAM | Y)]
        if ahead is not None:
            near = list(lax.optimization_barrier((*near, ahead)))[:4]
        return near + [exchange(piece, CORE) for piece in near]

    def reduce(partial):
        half = window // 2
        mine = partial[:half] + exchange(partial[half:], CORE)
        part = half // 4
        return (
            mine[:part]
            + exchange(mine[part : 2 * part], Y)
            + exchange(mine[2 * part : 3 * part], CAM)
            + exchange(mine[3 * part :], CAM | Y)
        )

    full, line, small, own = (window, WIDTH), (ring * tiles, WIDTH), (8, 128), (tiles, WIDTH)
    both = widen(jnp.stack([rhs, precond]))
    both = [both] + [exchange(both, Z * away) for away in range(1, ring)]
    residual, scaling, scaled = in_vmem(start_kernel, both + [problem[0][2]], [line, line, line])
    answer = jnp.zeros(own, jnp.float32)
    known = []
    for iteration in range(ITERS):
        partial, vector, energy = call_product(
            functools.partial(step_kernel, len(problem), 8, iteration == 0),
            problem, steady + gather(scaled, problem[-1][2] if iteration == 0 else None) + known, [full, full, small],
        )
        known = [vector, energy]
        mine = reduce(partial)
        if iteration + 1 < ITERS:
            parts = [mine] + [exchange(mine, Z * away) for away in range(1, ring)]
            answer, residual, scaled = in_vmem(
                functools.partial(turn_kernel, ring),
                parts + [energy, vector, answer, residual, scaling],
                [own, line, line],
            )
    parts = [mine[:tiles]] + [
        exchange(mine[away * tiles : (away + 1) * tiles], Z * away) for away in range(1, ring)
    ]
    return in_vmem(
        functools.partial(last_kernel, ring),
        parts + [energy, vector, answer, residual],
        [(1, tiles, TILE)] * 2,
    )


def from_behind(shard, axis, by):
    devices = lax.axis_size(axis)
    return lax.ppermute(shard, axis, [(i, (i + by) % devices) for i in range(devices)])


def many_groups(rhs, damp_cam, precond, problem, tile_ids, counts):
    group_tiles = lax.axis_size("pts") * rhs.shape[0]
    halfway = group_tiles // 2
    window = 2 * group_tiles
    tables = tables_of(tile_ids, counts, window)

    def product(vector):
        panel = lax.all_gather(widen(vector), "pts", axis=0, tiled=True)
        lower = from_behind(panel[halfway:], "cam", 1)
        upper = from_behind(panel[:halfway], "cam", -1)
        whole_window = jnp.concatenate([lower, panel, upper], axis=0)
        partial = call_product(
            functools.partial(plain_kernel, len(problem)), problem, tables + [whole_window], [(window, WIDTH)]
        )[0]
        from_above = from_behind(partial[:halfway], "cam", -1)
        from_below = from_behind(partial[halfway + group_tiles :], "cam", 1)
        summed = partial[halfway : halfway + group_tiles] + jnp.concatenate(
            [from_below, from_above], axis=0
        )
        return lax.psum_scatter(summed, "pts", scatter_dimension=0, tiled=True)[:, :TILE] + damp_cam * vector

    def inner(one, two):
        return lax.psum(jnp.sum(one * two), AXES)

    answer, residual = jnp.zeros(rhs.shape, jnp.float32), rhs
    scaled = precond * residual
    direction = scaled
    energy = inner(residual, scaled)
    for iteration in range(ITERS):
        mapped = product(direction)
        step_size = energy / inner(direction, mapped)
        answer = answer + step_size * direction
        residual = residual - step_size * mapped
        scaled = precond * residual
        energy_next = inner(residual, scaled)
        direction = scaled + energy_next / energy * direction
        energy = energy_next
    return answer[None], residual[None]


def on_device(rhs, damp_cam, precond, cam_jac, pt_jac, damp_pt, cam_index, tile_ids, counts):
    arrays = (
        counts[0],
        jnp.transpose(cam_jac[0], (0, 2, 1, 3)),
        jnp.transpose(pt_jac[0], (0, 2, 1, 3)),
        cam_index[0],
        jnp.transpose(damp_pt[0], (1, 0, 2)),
    )
    chunks = math.gcd(cam_jac.shape[1], CHUNKS)
    tiles = cam_jac.shape[1] // chunks
    problem = [call_setup(chunk * tiles, tiles, *arrays) for chunk in range(chunks)]
    groups, shards = lax.axis_size("cam"), lax.axis_size("pts")
    plan = two_groups if groups == 2 and shards in (4, 8, 16, 32) else many_groups
    return tuple(plan(rhs[0], damp_cam[0], precond[0], problem, tile_ids[0], counts[0]))


def solution(mesh):
    return jax.shard_map(
        on_device,
        mesh=mesh,
        in_specs=(
            P("cam", "pts", None),
            P("cam", "pts", None),
            P("cam", "pts", None),
            P("cam", "pts", None, None, None),
            P("cam", "pts", None, None, None),
            P("cam", "pts", None, None),
            P("cam", "pts", None, None),
            P("cam", "pts", None),
            P("cam", "pts"),
        ),
        out_specs=(P("cam", "pts", None), P("cam", "pts", None)),
        check_vma=False,
    )
```

time: 126 us -> 114 us (0.905)
  waiting for transfers between devices: 48.3 us -> 39.9 us
  local copies, waits for them, and re-layouts: 3.39 us -> 1.08 us
  Pallas kernels: 29.1 us -> 27 us
    ppermute x45, waiting for transfers between devices: 48.3 us -> 39.9 us  [exchange(): return lax.ppermute(array, AXES, [(i, i ^ mask) for i in range(devices)])]
    pallas_call x5 -> x9, Pallas kernels: 29.1 us -> 27 us  [the longest x7 19.8 us: in_vmem(): pl.pallas_call(kernel, out_shape=[jax.ShapeDtypeStruct(shape, jnp.float32...]
    unnamed x10 -> x6, local copies, waits for them, and re-layouts: 2.35 us -> 0.66 us
  transfers between devices with their start and end apart: 45 -> 45, of which waited for: 32 -> 33; matrix products, arithmetic and copies ran while one was open for 1% -> 2% of each run, Pallas kernels for 6% -> 6%
where the time goes in v3:
time: 114 us
  starting transfers between devices  42.6 us (37%)
  waiting for transfers between devices  39.9 us (35%)
  Pallas kernels  27 us (24%)
  other arithmetic  2.65 us (2%)
    ppermute x45, starting transfers between devices, exchange(): return lax.ppermute(array, AXES, [(i, i ^ mask) for i in range(devices)])  42.6 us
    ppermute x45, waiting for transfers between devices, exchange(): return lax.ppermute(array, AXES, [(i, i ^ mask) for i in range(devices)])  39.9 us
    pallas_call x7, Pallas kernels, in_vmem(): pl.pallas_call(kernel, out_shape=[jax.ShapeDtypeStruct(shape, jnp.float32...  19.8 us
    pallas_call x2, Pallas kernels, call_setup(): pl.pallas_call(functools.partial(setup_kernel, skip, group), out_shape=[p...  7.2 us
  transfers between devices with their start and end apart: 45, of which 33 were waited for; matrix products, arithmetic and copies ran while one was open for 2% of the time, Pallas kernels for 6%

profile of v3, /device:TPU:0, one launch (start us, length us, event | category | flops | bytes accessed | tf_op | source)
XLA Modules:
  0.0 114.2 jit_solution(7115132000255687699)
XLA Ops:
  0.6 0.8 select_maximum_fusion.refs_0_
  1.4 5.0 %collective-permute-start.2 = (f32[2,8,640]{2,1,0:T(8,128)S(1)}, f32[2,8,640]{2,1,0:T(8,128)S(1)}, u32[]{:S(2)}, u32[]{:S(2)}) collective-permute-start(f32[2,8,640]{2,1,0:T(8,128)S(1)} %select_maximum_fusion.refs_0_), channel_id=1, source_target_pairs={{0,24},{1,25},{2,26},{3,27},{4,28},{5,29},{6,30},{7,31},{8,16},{9,... | collective-permute-start | bytes 122888 | tf_op jit(solution)/shard_map/ppermute | solution.py:317
  6.4 0.6 collective-permute-start
  7.1 0.7 iota_compare_fusion.2
  7.9 0.7 add_add_fusion
  8.8 0.6 copy-done
  9.5 3.6 %shard_map.104 = (f32[48,18,8,128]{3,2,1,0:T(8,128)S(1)}, f32[48,6,8,128]{3,2,1,0:T(8,128)S(1)}, s32[48,8,128]{2,1,0:T(8,128)S(1)}, f32[48,6,8,128]{3,2,1,0:T(8,128)S(1)}, bf16[48,256,256]{2,1,0:T(8,128)(2,1)S(1)}) custom-call(s32[96]{0:T(128)S(1)} %bitcast.13, f32[96,18,8,128]{3,2,1,0:T(8,128)} %bitcast.15, f32[96,6,8,128]{3,2,1,0:T(8,128)} %bitcast.17, ...), custom_call_target="tpu_custom_call" | custom-call | flops 30000000 | bytes 10000000 | tf_op jit(solution)/shard_map/pallas_call | solution.py:281
  13.3 2.7 %collective-permute-start.5 = (f32[32,640]{1,0:T(8,128)S(1)}, f32[32,640]{1,0:T(8,128)S(1)}, u32[]{:S(2)}, u32[]{:S(2)}) collective-permute-start(f32[32,640]{1,0:T(8,128)S(1)} %get-tuple-element.45.refs_13_), channel_id=1, source_target_pairs={{0,5},{1,4},{2,7},{3,6},{4,1},{5,0},{6,3},{7,2},{8,13},{9,12},{10,... | collective-permute-start | bytes 245768 | tf_op jit(solution)/shard_map/ppermute | solution.py:317
  15.9 0.5 collective-permute-start.4
  16.9 3.6 %shard_map.105 = (f32[48,18,8,128]{3,2,1,0:T(8,128)S(1)}, f32[48,6,8,128]{3,2,1,0:T(8,128)S(1)}, s32[48,8,128]{2,1,0:T(8,128)S(1)}, f32[48,6,8,128]{3,2,1,0:T(8,128)S(1)}, bf16[48,256,256]{2,1,0:T(8,128)(2,1)S(1)}) custom-call(s32[96]{0:T(128)S(1)} %bitcast.14, f32[96,18,8,128]{3,2,1,0:T(8,128)} %bitcast.16, f32[96,6,8,128]{3,2,1,0:T(8,128)} %bitcast.18, ...), custom_call_target="tpu_custom_call" | custom-call | flops 30000000 | bytes 10000000 | tf_op jit(solution)/shard_map/pallas_call | solution.py:281
  20.9 0.5 collective-permute-start.7
  21.4 0.5 collective-permute-start.9
  22.9 5.9 %shard_map.107 = (f32[256,640]{1,0:T(8,128)S(1)}, f32[256,640]{1,0:T(8,128)S(1)}, f32[8,128]{1,0:T(8,128)S(1)}) custom-call(f32[48,18,8,128]{3,2,1,0:T(8,128)S(1)} %get-tuple-element.34.refs_0_, f32[48,6,8,128]{3,2,1,0:T(8,128)S(1)} %get-tuple-element.35.refs_1_, s32[48,8,128]{2,1,0:T(8,128)S(1)} %get-tuple-element.36.refs_4_.refs_2_, ...), custom_call_target="tpu_custom_call" | custom-call | tf_op jit(solution)/shard_map/pallas_call | solution.py:266
  28.8 0.4 collective-permute-start.10
  29.3 1.3 %collective-permute-done.10 = f32[128,640]{1,0:T(8,128)S(1)} collective-permute-done((f32[128,640]{1,0:T(8,128)S(1)}, f32[128,640]{1,0:T(8,128)S(1)}, u32[]{:S(2)}, u32[]{:S(2)}) %collective-permute-start.10) | collective-permute-done | bytes 327712 | tf_op jit(solution)/shard_map/ppermute | solution.py:317
  30.6 1.5 %collective-permute-start.11 = (f32[32,640]{1,0:T(8,128)S(1)}, f32[32,640]{1,0:T(8,128)S(1)}, u32[]{:S(2)}, u32[]{:S(2)}) collective-permute-start(f32[32,640]{1,0:T(8,128)S(1)} %get-tuple-element.72), channel_id=1, source_target_pairs={{0,4},{1,5},{2,6},{3,7},{4,0},{5,1},{6,2},{7,3},{8,12},{9,13},{10,... | collective-permute-start | bytes 245768 | tf_op jit(solution)/shard_map/ppermute | solution.py:317
  32.1 1.6 %collective-permute-start.13 = (f32[32,640]{1,0:T(8,128)S(1)}, f32[32,640]{1,0:T(8,128)S(1)}, u32[]{:S(2)}, u32[]{:S(2)}) collective-permute-start(f32[32,640]{1,0:T(8,128)S(1)} %get-tuple-element.73), channel_id=1, source_target_pairs={{0,5},{1,4},{2,7},{3,6},{4,1},{5,0},{6,3},{7,2},{8,13},{9,12},{10,... | collective-permute-start | bytes 245768 | tf_op jit(solution)/shard_map/ppermute | solution.py:317
  33.6 0.5 collective-permute-start.12
  34.2 1.6 %collective-permute-done.11 = f32[32,640]{1,0:T(8,128)S(1)} collective-permute-done((f32[32,640]{1,0:T(8,128)S(1)}, f32[32,640]{1,0:T(8,128)S(1)}, u32[]{:S(2)}, u32[]{:S(2)}) %collective-permute-start.11) | collective-permute-done | bytes 81952 | tf_op jit(solution)/shard_map/ppermute | solution.py:317
  35.8 2.2 %collective-permute-done.13 = f32[32,640]{1,0:T(8,128)S(1)} collective-permute-done((f32[32,640]{1,0:T(8,128)S(1)}, f32[32,640]{1,0:T(8,128)S(1)}, u32[]{:S(2)}, u32[]{:S(2)}) %collective-permute-start.13) | collective-permute-done | bytes 81952 | tf_op jit(solution)/shard_map/ppermute | solution.py:317
  38.0 0.4 collective-permute-done.12
  38.4 3.7 %collective-permute-start.16 = (f32[32,640]{1,0:T(8,128)S(1)}, f32[32,640]{1,0:T(8,128)S(1)}, u32[]{:S(2)}, u32[]{:S(2)}) collective-permute-start(f32[32,640]{1,0:T(8,128)S(1)} %fusion.7.refs_0_), channel_id=1, source_target_pairs={{0,24},{1,25},{2,26},{3,27},{4,28},{5,29},{6,30},{7,31},{8,16},{9,... | collective-permute-start | bytes 245768 | tf_op jit(solution)/shard_map/ppermute | solution.py:317
  42.1 0.8 collective-permute-start.14
  42.8 2.4 %collective-permute-done.16.refs_3_ = f32[32,640]{1,0:T(8,128)S(1)} collective-permute-done((f32[32,640]{1,0:T(8,128)S(1)}, f32[32,640]{1,0:T(8,128)S(1)}, u32[]{:S(2)}, u32[]{:S(2)}) %collective-permute-start.16) | collective-permute-done | bytes 81952 | tf_op jit(solution)/shard_map/ppermute | solution.py:317
  45.2 3.4 %collective-permute-done.15.refs_2_ = f32[32,640]{1,0:T(8,128)S(1)} collective-permute-done((f32[32,640]{1,0:T(8,128)S(1)}, f32[32,640]{1,0:T(8,128)S(1)}, u32[]{:S(2)}, u32[]{:S(2)}) %collective-permute-start.15) | collective-permute-done | bytes 81952 | tf_op jit(solution)/shard_map/ppermute | solution.py:317
  48.8 2.0 %collective-permute-start.19 = (f32[32,640]{1,0:T(8,128)S(1)}, f32[32,640]{1,0:T(8,128)S(1)}, u32[]{:S(2)}, u32[]{:S(2)}) collective-permute-start(f32[32,640]{1,0:T(8,128)S(1)} %get-tuple-element.54.refs_13_), channel_id=1, source_target_pairs={{0,5},{1,4},{2,7},{3,6},{4,1},{5,0},{6,3},{7,2},{8,13},{9,12},{10,... | collective-permute-start | bytes 245768 | tf_op jit(solution)/shard_map/ppermute | solution.py:317
  50.9 0.8 collective-permute-start.18
  51.7 0.7 collective-permute-start.17
  52.4 2.1 %collective-permute-done.19.refs_16_ = f32[32,640]{1,0:T(8,128)S(1)} collective-permute-done((f32[32,640]{1,0:T(8,128)S(1)}, f32[32,640]{1,0:T(8,128)S(1)}, u32[]{:S(2)}, u32[]{:S(2)}) %collective-permute-start.19) | collective-permute-done | bytes 81952 | tf_op jit(solution)/shard_map/ppermute | solution.py:317
  54.5 0.9 collective-permute-done.18.refs_15_
  55.3 0.8 collective-permute-done.17.refs_14_
  56.2 0.4 collective-permute-done.22.refs_19_
  56.6 0.8 collective-permute-done.21.refs_18_
  57.4 6.3 %shard_map.109 = (f32[256,640]{1,0:T(8,128)S(1)}, f32[256,640]{1,0:T(8,128)S(1)}, f32[8,128]{1,0:T(8,128)S(1)}) custom-call(f32[48,18,8,128]{3,2,1,0:T(8,128)S(1)} %get-tuple-element.34.refs_0_, f32[48,6,8,128]{3,2,1,0:T(8,128)S(1)} %get-tuple-element.35.refs_1_, s32[48,8,128]{2,1,0:T(8,128)S(1)} %get-tuple-element.36.refs_4_.refs_2_, ...), custom_call_target="tpu_custom_call" | custom-call | tf_op jit(solution)/shard_map/pallas_call | solution.py:266
  64.0 1.5 %collective-permute-done.24 = f32[128,640]{1,0:T(8,128)S(1)} collective-permute-done((f32[128,640]{1,0:T(8,128)S(1)}, f32[128,640]{1,0:T(8,128)S(1)}, u32[]{:S(2)}, u32[]{:S(2)}) %collective-permute-start.24) | collective-permute-done | bytes 327712 | tf_op jit(solution)/shard_map/ppermute | solution.py:317
  65.6 0.8 collective-permute-start.25
  66.3 2.0 %collective-permute-start.27 = (f32[32,640]{1,0:T(8,128)S(1)}, f32[32,640]{1,0:T(8,128)S(1)}, u32[]{:S(2)}, u32[]{:S(2)}) collective-permute-start(f32[32,640]{1,0:T(8,128)S(1)} %get-tuple-element.70), channel_id=1, source_target_pairs={{0,5},{1,4},{2,7},{3,6},{4,1},{5,0},{6,3},{7,2},{8,13},{9,12},{10,... | collective-permute-start | bytes 245768 | tf_op jit(solution)/shard_map/ppermute | solution.py:317
  68.3 0.8 collective-permute-start.26
  69.1 2.1 %collective-permute-done.25 = f32[32,640]{1,0:T(8,128)S(1)} collective-permute-done((f32[32,640]{1,0:T(8,128)S(1)}, f32[32,640]{1,0:T(8,128)S(1)}, u32[]{:S(2)}, u32[]{:S(2)}) %collective-permute-start.25) | collective-permute-done | bytes 81952 | tf_op jit(solution)/shard_map/ppermute | solution.py:317
  71.2 1.1 collective-permute-done.27
  72.3 0.8 collective-permute-done.26
  73.1 2.8 %collective-permute-start.30 = (f32[32,640]{1,0:T(8,128)S(1)}, f32[32,640]{1,0:T(8,128)S(1)}, u32[]{:S(2)}, u32[]{:S(2)}) collective-permute-start(f32[32,640]{1,0:T(8,128)S(1)} %fusion.5.refs_0_), channel_id=1, source_target_pairs={{0,24},{1,25},{2,26},{3,27},{4,28},{5,29},{6,30},{7,31},{8,16},{9,... | collective-permute-start | bytes 245768 | tf_op jit(solution)/shard_map/ppermute | solution.py:317
  75.9 1.7 %collective-permute-start.28 = (f32[32,640]{1,0:T(8,128)S(1)}, f32[32,640]{1,0:T(8,128)S(1)}, u32[]{:S(2)}, u32[]{:S(2)}) collective-permute-start(f32[32,640]{1,0:T(8,128)S(1)} %fusion.5.refs_0_), channel_id=1, source_target_pairs={{0,8},{1,9},{2,10},{3,11},{4,12},{5,13},{6,14},{7,15},{8,0},{9,1},... | collective-permute-start | bytes 245768 | tf_op jit(solution)/shard_map/ppermute | solution.py:317
  77.6 1.9 %collective-permute-done.30.refs_3_ = f32[32,640]{1,0:T(8,128)S(1)} collective-permute-done((f32[32,640]{1,0:T(8,128)S(1)}, f32[32,640]{1,0:T(8,128)S(1)}, u32[]{:S(2)}, u32[]{:S(2)}) %collective-permute-start.30) | collective-permute-done | bytes 81952 | tf_op jit(solution)/shard_map/ppermute | solution.py:317
  79.5 3.3 %collective-permute-done.29.refs_2_ = f32[32,640]{1,0:T(8,128)S(1)} collective-permute-done((f32[32,640]{1,0:T(8,128)S(1)}, f32[32,640]{1,0:T(8,128)S(1)}, u32[]{:S(2)}, u32[]{:S(2)}) %collective-permute-start.29) | collective-permute-done | bytes 81952 | tf_op jit(solution)/shard_map/ppermute | solution.py:317
  83.1 1.2 %collective-permute-start.33 = (f32[32,640]{1,0:T(8,128)S(1)}, f32[32,640]{1,0:T(8,128)S(1)}, u32[]{:S(2)}, u32[]{:S(2)}) collective-permute-start(f32[32,640]{1,0:T(8,128)S(1)} %get-tuple-element.60.refs_13_), channel_id=1, source_target_pairs={{0,5},{1,4},{2,7},{3,6},{4,1},{5,0},{6,3},{7,2},{8,13},{9,12},{10,... | collective-permute-start | bytes 245768 | tf_op jit(solution)/shard_map/ppermute | solution.py:317
  84.3 0.9 collective-permute-start.32
  85.2 1.4 %collective-permute-start.31 = (f32[32,640]{1,0:T(8,128)S(1)}, f32[32,640]{1,0:T(8,128)S(1)}, u32[]{:S(2)}, u32[]{:S(2)}) collective-permute-start(f32[32,640]{1,0:T(8,128)S(1)} %get-tuple-element.60.refs_13_), channel_id=1, source_target_pairs={{0,4},{1,5},{2,6},{3,7},{4,0},{5,1},{6,2},{7,3},{8,12},{9,13},{10,... | collective-permute-start | bytes 245768 | tf_op jit(solution)/shard_map/ppermute | solution.py:317
  86.6 2.0 %collective-permute-done.33.refs_16_ = f32[32,640]{1,0:T(8,128)S(1)} collective-permute-done((f32[32,640]{1,0:T(8,128)S(1)}, f32[32,640]{1,0:T(8,128)S(1)}, u32[]{:S(2)}, u32[]{:S(2)}) %collective-permute-start.33) | collective-permute-done | bytes 81952 | tf_op jit(solution)/shard_map/ppermute | solution.py:317
  88.7 0.4 collective-permute-start.36
  89.1 0.5 collective-permute-done.31.refs_14_
  90.0 0.9 collective-permute-done.35.refs_18_
  90.9 6.1 %shard_map.111 = (f32[256,640]{1,0:T(8,128)S(1)}, f32[256,640]{1,0:T(8,128)S(1)}, f32[8,128]{1,0:T(8,128)S(1)}) custom-call(f32[48,18,8,128]{3,2,1,0:T(8,128)S(1)} %get-tuple-element.34.refs_0_, f32[48,6,8,128]{3,2,1,0:T(8,128)S(1)} %get-tuple-element.35.refs_1_, s32[48,8,128]{2,1,0:T(8,128)S(1)} %get-tuple-element.36.refs_4_.refs_2_, ...), custom_call_target="tpu_custom_call" | custom-call | tf_op jit(solution)/shard_map/pallas_call | solution.py:266
  97.3 1.5 %collective-permute-done.38 = f32[128,640]{1,0:T(8,128)S(1)} collective-permute-done((f32[128,640]{1,0:T(8,128)S(1)}, f32[128,640]{1,0:T(8,128)S(1)}, u32[]{:S(2)}, u32[]{:S(2)}) %collective-permute-start.38) | collective-permute-done | bytes 327712 | tf_op jit(solution)/shard_map/ppermute | solution.py:317
  98.9 1.5 %collective-permute-start.39 = (f32[32,640]{1,0:T(8,128)S(1)}, f32[32,640]{1,0:T(8,128)S(1)}, u32[]{:S(2)}, u32[]{:S(2)}) collective-permute-start(f32[32,640]{1,0:T(8,128)S(1)} %get-tuple-element.66), channel_id=1, source_target_pairs={{0,4},{1,5},{2,6},{3,7},{4,0},{5,1},{6,2},{7,3},{8,12},{9,13},{10,... | collective-permute-start | bytes 245768 | tf_op jit(solution)/shard_map/ppermute | solution.py:317
  100.4 1.2 %collective-permute-start.41 = (f32[32,640]{1,0:T(8,128)S(1)}, f32[32,640]{1,0:T(8,128)S(1)}, u32[]{:S(2)}, u32[]{:S(2)}) collective-permute-start(f32[32,640]{1,0:T(8,128)S(1)} %get-tuple-element.67), channel_id=1, source_target_pairs={{0,5},{1,4},{2,7},{3,6},{4,1},{5,0},{6,3},{7,2},{8,13},{9,12},{10,... | collective-permute-start | bytes 245768 | tf_op jit(solution)/shard_map/ppermute | solution.py:317
  101.5 0.9 collective-permute-start.40
  102.4 1.0 collective-permute-done.39
  103.4 2.9 %collective-permute-done.41 = f32[32,640]{1,0:T(8,128)S(1)} collective-permute-done((f32[32,640]{1,0:T(8,128)S(1)}, f32[32,640]{1,0:T(8,128)S(1)}, u32[]{:S(2)}, u32[]{:S(2)}) %collective-permute-start.41) | collective-permute-done | bytes 81952 | tf_op jit(solution)/shard_map/ppermute | solution.py:317
  106.4 2.4 %collective-permute-start.44 = (f32[8,640]{1,0:T(8,128)S(1)}, f32[8,640]{1,0:T(8,128)S(1)}, u32[]{:S(2)}, u32[]{:S(2)}) collective-permute-start(f32[8,640]{1,0:T(8,128)S(1)} %get-tuple-element.75), channel_id=1, source_target_pairs={{0,24},{1,25},{2,26},{3,27},{4,28},{5,29},{6,30},{7,31},{8,16},{9,... | collective-permute-start | bytes 61448 | tf_op jit(solution)/shard_map/ppermute | solution.py:317
  108.8 2.1 %collective-permute-start.42 = (f32[8,640]{1,0:T(8,128)S(1)}, f32[8,640]{1,0:T(8,128)S(1)}, u32[]{:S(2)}, u32[]{:S(2)}) collective-permute-start(f32[8,640]{1,0:T(8,128)S(1)} %get-tuple-element.77), channel_id=1, source_target_pairs={{0,8},{1,9},{2,10},{3,11},{4,12},{5,13},{6,14},{7,15},{8,0},{9,1},... | collective-permute-start | bytes 61448 | tf_op jit(solution)/shard_map/ppermute | solution.py:317
  110.9 1.2 %collective-permute-done.44.refs_3_ = f32[8,640]{1,0:T(8,128)S(1)} collective-permute-done((f32[8,640]{1,0:T(8,128)S(1)}, f32[8,640]{1,0:T(8,128)S(1)}, u32[]{:S(2)}, u32[]{:S(2)}) %collective-permute-start.44) | collective-permute-done | bytes 20512 | tf_op jit(solution)/shard_map/ppermute | solution.py:317
  112.1 1.4 %collective-permute-done.43.refs_2_ = f32[8,640]{1,0:T(8,128)S(1)} collective-permute-done((f32[8,640]{1,0:T(8,128)S(1)}, f32[8,640]{1,0:T(8,128)S(1)}, u32[]{:S(2)}, u32[]{:S(2)}) %collective-permute-start.43) | collective-permute-done | bytes 20512 | tf_op jit(solution)/shard_map/ppermute | solution.py:317
  113.5 0.7 shard_map.112
  (65 shorter events, 4.1 us)
Async XLA Ops:
  1.4 11.7 %collective-permute-start.2 = (f32[2,8,640]{2,1,0:T(8,128)S(1)}, f32[2,8,640]{2,1,0:T(8,128)S(1)}, u32[]{:S(2)}, u32[]{:S(2)}) collective-permute-start(f32[2,8,640]{2,1,0:T(8,128)S(1)} %select_maximum_fusion.refs_0_), channel_id=1, source_target_pairs={{0,24},{1,25},{2,26},{3,27},{4,28},{5,29},{6,30},{7,31},{8,16},{9,... | collective-permute-start | bytes 122888 | tf_op jit(solution)/shard_map/ppermute | solution.py:317
  6.4 6.7 %collective-permute-start.1 = (f32[2,8,640]{2,1,0:T(8,128)S(1)}, f32[2,8,640]{2,1,0:T(8,128)S(1)}, u32[]{:S(2)}, u32[]{:S(2)}) collective-permute-start(f32[2,8,640]{2,1,0:T(8,128)S(1)} %select_maximum_fusion.refs_0_), channel_id=1, source_target_pairs={{0,16},{1,17},{2,18},{3,19},{4,20},{5,21},{6,22},{7,23},{8,24},{9,... | collective-permute-start | bytes 122888 | tf_op jit(solution)/shard_map/ppermute | solution.py:317
  6.4 6.7 %collective-permute-start = (f32[2,8,640]{2,1,0:T(8,128)S(1)}, f32[2,8,640]{2,1,0:T(8,128)S(1)}, u32[]{:S(2)}, u32[]{:S(2)}) collective-permute-start(f32[2,8,640]{2,1,0:T(8,128)S(1)} %select_maximum_fusion.refs_0_), channel_id=1, source_target_pairs={{0,8},{1,9},{2,10},{3,11},{4,12},{5,13},{6,14},{7,15},{8,0},{9,1},... | collective-permute-start | bytes 122888 | tf_op jit(solution)/shard_map/ppermute | solution.py:317
  8.8 0.7 copy-start
  9.5 7.4 %copy-start.1 = (s32[1,96]{1,0:T(1,128)S(1)}, s32[1,96]{1,0:T(1,128)}, u32[]{:S(2)}) copy-start(s32[1,96]{1,0:T(1,128)} %param.17) | copy-start | bytes 1156
  13.3 7.3 %collective-permute-start.5 = (f32[32,640]{1,0:T(8,128)S(1)}, f32[32,640]{1,0:T(8,128)S(1)}, u32[]{:S(2)}, u32[]{:S(2)}) collective-permute-start(f32[32,640]{1,0:T(8,128)S(1)} %get-tuple-element.45.refs_13_), channel_id=1, source_target_pairs={{0,5},{1,4},{2,7},{3,6},{4,1},{5,0},{6,3},{7,2},{8,13},{9,12},{10,... | collective-permute-start | bytes 245768 | tf_op jit(solution)/shard_map/ppermute | solution.py:317
  15.9 4.6 %collective-permute-start.4 = (f32[32,640]{1,0:T(8,128)S(1)}, f32[32,640]{1,0:T(8,128)S(1)}, u32[]{:S(2)}, u32[]{:S(2)}) collective-permute-start(f32[32,640]{1,0:T(8,128)S(1)} %get-tuple-element.45.refs_13_), channel_id=1, source_target_pairs={{0,1},{1,0},{2,3},{3,2},{4,5},{5,4},{6,7},{7,6},{8,9},{9,8},{10,11... | collective-permute-start | bytes 245768 | tf_op jit(solution)/shard_map/ppermute | solution.py:317
  16.5 4.4 %collective-permute-start.3 = (f32[32,640]{1,0:T(8,128)S(1)}, f32[32,640]{1,0:T(8,128)S(1)}, u32[]{:S(2)}, u32[]{:S(2)}) collective-permute-start(f32[32,640]{1,0:T(8,128)S(1)} %get-tuple-element.45.refs_13_), channel_id=1, source_target_pairs={{0,4},{1,5},{2,6},{3,7},{4,0},{5,1},{6,2},{7,3},{8,12},{9,13},{10,... | collective-permute-start | bytes 245768 | tf_op jit(solution)/shard_map/ppermute | solution.py:317
  16.9 5.2 %copy-start.2 = (f32[1,8,576]{2,1,0:T(8,128)S(1)}, f32[1,8,576]{2,1,0:T(8,128)}, u32[]{:S(2)}) copy-start(f32[1,8,576]{2,1,0:T(8,128)} %param.10) | copy-start | bytes 55300
  20.9 1.3 %collective-permute-start.6 = (f32[32,640]{1,0:T(8,128)S(1)}, f32[32,640]{1,0:T(8,128)S(1)}, u32[]{:S(2)}, u32[]{:S(2)}) collective-permute-start(f32[32,640]{1,0:T(8,128)S(1)} %get-tuple-element.45.refs_13_), channel_id=1, source_target_pairs={{0,2},{1,3},{2,0},{3,1},{4,6},{5,7},{6,4},{7,5},{8,10},{9,11},{10,... | collective-permute-start | bytes 245768 | tf_op jit(solution)/shard_map/ppermute | solution.py:317
  20.9 1.4 %collective-permute-start.7 = (f32[32,640]{1,0:T(8,128)S(1)}, f32[32,640]{1,0:T(8,128)S(1)}, u32[]{:S(2)}, u32[]{:S(2)}) collective-permute-start(f32[32,640]{1,0:T(8,128)S(1)} %collective-permute-done.3.refs_14_), channel_id=1, source_target_pairs={{0,2},{1,3},{2,0},{3,1},{4,6},{5,7},{6,4},{7,5},{8,10},{9,11},{10,... | collective-permute-start | bytes 245768 | tf_op jit(solution)/shard_map/ppermute | solution.py:317
  21.4 1.3 %collective-permute-start.8 = (f32[32,640]{1,0:T(8,128)S(1)}, f32[32,640]{1,0:T(8,128)S(1)}, u32[]{:S(2)}, u32[]{:S(2)}) collective-permute-start(f32[32,640]{1,0:T(8,128)S(1)} %collective-permute-done.4.refs_15_), channel_id=1, source_target_pairs={{0,2},{1,3},{2,0},{3,1},{4,6},{5,7},{6,4},{7,5},{8,10},{9,11},{10,... | collective-permute-start | bytes 245768 | tf_op jit(solution)/shard_map/ppermute | solution.py:317
  21.4 1.4 %collective-permute-start.9 = (f32[32,640]{1,0:T(8,128)S(1)}, f32[32,640]{1,0:T(8,128)S(1)}, u32[]{:S(2)}, u32[]{:S(2)}) collective-permute-start(f32[32,640]{1,0:T(8,128)S(1)} %collective-permute-done.5.refs_16_), channel_id=1, source_target_pairs={{0,2},{1,3},{2,0},{3,1},{4,6},{5,7},{6,4},{7,5},{8,10},{9,11},{10,... | collective-permute-start | bytes 245768 | tf_op jit(solution)/shard_map/ppermute | solution.py:317
  28.8 1.7 %collective-permute-start.10 = (f32[128,640]{1,0:T(8,128)S(1)}, f32[128,640]{1,0:T(8,128)S(1)}, u32[]{:S(2)}, u32[]{:S(2)}) collective-permute-start(f32[128,640]{1,0:T(8,128)S(1)} %slice.67), channel_id=1, source_target_pairs={{0,2},{1,3},{2,0},{3,1},{4,6},{5,7},{6,4},{7,5},{8,10},{9,11},{10,... | collective-permute-start | bytes 983048 | tf_op jit(solution)/shard_map/ppermute | solution.py:317
  30.6 5.2 %collective-permute-start.11 = (f32[32,640]{1,0:T(8,128)S(1)}, f32[32,640]{1,0:T(8,128)S(1)}, u32[]{:S(2)}, u32[]{:S(2)}) collective-permute-start(f32[32,640]{1,0:T(8,128)S(1)} %get-tuple-element.72), channel_id=1, source_target_pairs={{0,4},{1,5},{2,6},{3,7},{4,0},{5,1},{6,2},{7,3},{8,12},{9,13},{10,... | collective-permute-start | bytes 245768 | tf_op jit(solution)/shard_map/ppermute | solution.py:317
  32.1 5.9 %collective-permute-start.13 = (f32[32,640]{1,0:T(8,128)S(1)}, f32[32,640]{1,0:T(8,128)S(1)}, u32[]{:S(2)}, u32[]{:S(2)}) collective-permute-start(f32[32,640]{1,0:T(8,128)S(1)} %get-tuple-element.73), channel_id=1, source_target_pairs={{0,5},{1,4},{2,7},{3,6},{4,1},{5,0},{6,3},{7,2},{8,13},{9,12},{10,... | collective-permute-start | bytes 245768 | tf_op jit(solution)/shard_map/ppermute | solution.py:317
  33.6 4.7 %collective-permute-start.12 = (f32[32,640]{1,0:T(8,128)S(1)}, f32[32,640]{1,0:T(8,128)S(1)}, u32[]{:S(2)}, u32[]{:S(2)}) collective-permute-start(f32[32,640]{1,0:T(8,128)S(1)} %get-tuple-element.74), channel_id=1, source_target_pairs={{0,1},{1,0},{2,3},{3,2},{4,5},{5,4},{6,7},{7,6},{8,9},{9,8},{10,11... | collective-permute-start | bytes 245768 | tf_op jit(solution)/shard_map/ppermute | solution.py:317
  38.4 6.8 %collective-permute-start.16 = (f32[32,640]{1,0:T(8,128)S(1)}, f32[32,640]{1,0:T(8,128)S(1)}, u32[]{:S(2)}, u32[]{:S(2)}) collective-permute-start(f32[32,640]{1,0:T(8,128)S(1)} %fusion.7.refs_0_), channel_id=1, source_target_pairs={{0,24},{1,25},{2,26},{3,27},{4,28},{5,29},{6,30},{7,31},{8,16},{9,... | collective-permute-start | bytes 245768 | tf_op jit(solution)/shard_map/ppermute | solution.py:317
  42.0 6.5 %collective-permute-start.15 = (f32[32,640]{1,0:T(8,128)S(1)}, f32[32,640]{1,0:T(8,128)S(1)}, u32[]{:S(2)}, u32[]{:S(2)}) collective-permute-start(f32[32,640]{1,0:T(8,128)S(1)} %fusion.7.refs_0_), channel_id=1, source_target_pairs={{0,16},{1,17},{2,18},{3,19},{4,20},{5,21},{6,22},{7,23},{8,24},{9,... | collective-permute-start | bytes 245768 | tf_op jit(solution)/shard_map/ppermute | solution.py:317
  42.1 6.5 %collective-permute-start.14 = (f32[32,640]{1,0:T(8,128)S(1)}, f32[32,640]{1,0:T(8,128)S(1)}, u32[]{:S(2)}, u32[]{:S(2)}) collective-permute-start(f32[32,640]{1,0:T(8,128)S(1)} %fusion.7.refs_0_), channel_id=1, source_target_pairs={{0,8},{1,9},{2,10},{3,11},{4,12},{5,13},{6,14},{7,15},{8,0},{9,1},... | collective-permute-start | bytes 245768 | tf_op jit(solution)/shard_map/ppermute | solution.py:317
  48.8 5.6 %collective-permute-start.19 = (f32[32,640]{1,0:T(8,128)S(1)}, f32[32,640]{1,0:T(8,128)S(1)}, u32[]{:S(2)}, u32[]{:S(2)}) collective-permute-start(f32[32,640]{1,0:T(8,128)S(1)} %get-tuple-element.54.refs_13_), channel_id=1, source_target_pairs={{0,5},{1,4},{2,7},{3,6},{4,1},{5,0},{6,3},{7,2},{8,13},{9,12},{10,... | collective-permute-start | bytes 245768 | tf_op jit(solution)/shard_map/ppermute | solution.py:317
  50.9 4.4 %collective-permute-start.18 = (f32[32,640]{1,0:T(8,128)S(1)}, f32[32,640]{1,0:T(8,128)S(1)}, u32[]{:S(2)}, u32[]{:S(2)}) collective-permute-start(f32[32,640]{1,0:T(8,128)S(1)} %get-tuple-element.54.refs_13_), channel_id=1, source_target_pairs={{0,1},{1,0},{2,3},{3,2},{4,5},{5,4},{6,7},{7,6},{8,9},{9,8},{10,11... | collective-permute-start | bytes 245768 | tf_op jit(solution)/shard_map/ppermute | solution.py:317
  51.7 4.4 %collective-permute-start.17 = (f32[32,640]{1,0:T(8,128)S(1)}, f32[32,640]{1,0:T(8,128)S(1)}, u32[]{:S(2)}, u32[]{:S(2)}) collective-permute-start(f32[32,640]{1,0:T(8,128)S(1)} %get-tuple-element.54.refs_13_), channel_id=1, source_target_pairs={{0,4},{1,5},{2,6},{3,7},{4,0},{5,1},{6,2},{7,3},{8,12},{9,13},{10,... | collective-permute-start | bytes 245768 | tf_op jit(solution)/shard_map/ppermute | solution.py:317
  52.4 3.8 %collective-permute-start.20 = (f32[32,640]{1,0:T(8,128)S(1)}, f32[32,640]{1,0:T(8,128)S(1)}, u32[]{:S(2)}, u32[]{:S(2)}) collective-permute-start(f32[32,640]{1,0:T(8,128)S(1)} %get-tuple-element.54.refs_13_), channel_id=1, source_target_pairs={{0,2},{1,3},{2,0},{3,1},{4,6},{5,7},{6,4},{7,5},{8,10},{9,11},{10,... | collective-permute-start | bytes 245768 | tf_op jit(solution)/shard_map/ppermute | solution.py:317
  54.5 1.7 %collective-permute-start.23 = (f32[32,640]{1,0:T(8,128)S(1)}, f32[32,640]{1,0:T(8,128)S(1)}, u32[]{:S(2)}, u32[]{:S(2)}) collective-permute-start(f32[32,640]{1,0:T(8,128)S(1)} %collective-permute-done.19.refs_16_), channel_id=1, source_target_pairs={{0,2},{1,3},{2,0},{3,1},{4,6},{5,7},{6,4},{7,5},{8,10},{9,11},{10,... | collective-permute-start | bytes 245768 | tf_op jit(solution)/shard_map/ppermute | solution.py:317
  55.3 1.3 %collective-permute-start.22 = (f32[32,640]{1,0:T(8,128)S(1)}, f32[32,640]{1,0:T(8,128)S(1)}, u32[]{:S(2)}, u32[]{:S(2)}) collective-permute-start(f32[32,640]{1,0:T(8,128)S(1)} %collective-permute-done.18.refs_15_), channel_id=1, source_target_pairs={{0,2},{1,3},{2,0},{3,1},{4,6},{5,7},{6,4},{7,5},{8,10},{9,11},{10,... | collective-permute-start | bytes 245768 | tf_op jit(solution)/shard_map/ppermute | solution.py:317
  56.1 1.3 %collective-permute-start.21 = (f32[32,640]{1,0:T(8,128)S(1)}, f32[32,640]{1,0:T(8,128)S(1)}, u32[]{:S(2)}, u32[]{:S(2)}) collective-permute-start(f32[32,640]{1,0:T(8,128)S(1)} %collective-permute-done.17.refs_14_), channel_id=1, source_target_pairs={{0,2},{1,3},{2,0},{3,1},{4,6},{5,7},{6,4},{7,5},{8,10},{9,11},{10,... | collective-permute-start | bytes 245768 | tf_op jit(solution)/shard_map/ppermute | solution.py:317
  63.8 1.7 %collective-permute-start.24 = (f32[128,640]{1,0:T(8,128)S(1)}, f32[128,640]{1,0:T(8,128)S(1)}, u32[]{:S(2)}, u32[]{:S(2)}) collective-permute-start(f32[128,640]{1,0:T(8,128)S(1)} %slice.73), channel_id=1, source_target_pairs={{0,2},{1,3},{2,0},{3,1},{4,6},{5,7},{6,4},{7,5},{8,10},{9,11},{10,... | collective-permute-start | bytes 983048 | tf_op jit(solution)/shard_map/ppermute | solution.py:317
  65.6 5.7 %collective-permute-start.25 = (f32[32,640]{1,0:T(8,128)S(1)}, f32[32,640]{1,0:T(8,128)S(1)}, u32[]{:S(2)}, u32[]{:S(2)}) collective-permute-start(f32[32,640]{1,0:T(8,128)S(1)} %get-tuple-element.69), channel_id=1, source_target_pairs={{0,4},{1,5},{2,6},{3,7},{4,0},{5,1},{6,2},{7,3},{8,12},{9,13},{10,... | collective-permute-start | bytes 245768 | tf_op jit(solution)/shard_map/ppermute | solution.py:317
  66.3 6.0 %collective-permute-start.27 = (f32[32,640]{1,0:T(8,128)S(1)}, f32[32,640]{1,0:T(8,128)S(1)}, u32[]{:S(2)}, u32[]{:S(2)}) collective-permute-start(f32[32,640]{1,0:T(8,128)S(1)} %get-tuple-element.70), channel_id=1, source_target_pairs={{0,5},{1,4},{2,7},{3,6},{4,1},{5,0},{6,3},{7,2},{8,13},{9,12},{10,... | collective-permute-start | bytes 245768 | tf_op jit(solution)/shard_map/ppermute | solution.py:317
  68.3 4.8 %collective-permute-start.26 = (f32[32,640]{1,0:T(8,128)S(1)}, f32[32,640]{1,0:T(8,128)S(1)}, u32[]{:S(2)}, u32[]{:S(2)}) collective-permute-start(f32[32,640]{1,0:T(8,128)S(1)} %get-tuple-element.71), channel_id=1, source_target_pairs={{0,1},{1,0},{2,3},{3,2},{4,5},{5,4},{6,7},{7,6},{8,9},{9,8},{10,11... | collective-permute-start | bytes 245768 | tf_op jit(solution)/shard_map/ppermute | solution.py:317
  73.1 6.3 %collective-permute-start.30 = (f32[32,640]{1,0:T(8,128)S(1)}, f32[32,640]{1,0:T(8,128)S(1)}, u32[]{:S(2)}, u32[]{:S(2)}) collective-permute-start(f32[32,640]{1,0:T(8,128)S(1)} %fusion.5.refs_0_), channel_id=1, source_target_pairs={{0,24},{1,25},{2,26},{3,27},{4,28},{5,29},{6,30},{7,31},{8,16},{9,... | collective-permute-start | bytes 245768 | tf_op jit(solution)/shard_map/ppermute | solution.py:317
  75.9 6.9 %collective-permute-start.29 = (f32[32,640]{1,0:T(8,128)S(1)}, f32[32,640]{1,0:T(8,128)S(1)}, u32[]{:S(2)}, u32[]{:S(2)}) collective-permute-start(f32[32,640]{1,0:T(8,128)S(1)} %fusion.5.refs_0_), channel_id=1, source_target_pairs={{0,16},{1,17},{2,18},{3,19},{4,20},{5,21},{6,22},{7,23},{8,24},{9,... | collective-permute-start | bytes 245768 | tf_op jit(solution)/shard_map/ppermute | solution.py:317
  75.9 6.9 %collective-permute-start.28 = (f32[32,640]{1,0:T(8,128)S(1)}, f32[32,640]{1,0:T(8,128)S(1)}, u32[]{:S(2)}, u32[]{:S(2)}) collective-permute-start(f32[32,640]{1,0:T(8,128)S(1)} %fusion.5.refs_0_), channel_id=1, source_target_pairs={{0,8},{1,9},{2,10},{3,11},{4,12},{5,13},{6,14},{7,15},{8,0},{9,1},... | collective-permute-start | bytes 245768 | tf_op jit(solution)/shard_map/ppermute | solution.py:317
  83.1 5.5 %collective-permute-start.33 = (f32[32,640]{1,0:T(8,128)S(1)}, f32[32,640]{1,0:T(8,128)S(1)}, u32[]{:S(2)}, u32[]{:S(2)}) collective-permute-start(f32[32,640]{1,0:T(8,128)S(1)} %get-tuple-element.60.refs_13_), channel_id=1, source_target_pairs={{0,5},{1,4},{2,7},{3,6},{4,1},{5,0},{6,3},{7,2},{8,13},{9,12},{10,... | collective-permute-start | bytes 245768 | tf_op jit(solution)/shard_map/ppermute | solution.py:317
  84.3 4.4 %collective-permute-start.32 = (f32[32,640]{1,0:T(8,128)S(1)}, f32[32,640]{1,0:T(8,128)S(1)}, u32[]{:S(2)}, u32[]{:S(2)}) collective-permute-start(f32[32,640]{1,0:T(8,128)S(1)} %get-tuple-element.60.refs_13_), channel_id=1, source_target_pairs={{0,1},{1,0},{2,3},{3,2},{4,5},{5,4},{6,7},{7,6},{8,9},{9,8},{10,11... | collective-permute-start | bytes 245768 | tf_op jit(solution)/shard_map/ppermute | solution.py:317
  85.2 4.4 %collective-permute-start.31 = (f32[32,640]{1,0:T(8,128)S(1)}, f32[32,640]{1,0:T(8,128)S(1)}, u32[]{:S(2)}, u32[]{:S(2)}) collective-permute-start(f32[32,640]{1,0:T(8,128)S(1)} %get-tuple-element.60.refs_13_), channel_id=1, source_target_pairs={{0,4},{1,5},{2,6},{3,7},{4,0},{5,1},{6,2},{7,3},{8,12},{9,13},{10,... | collective-permute-start | bytes 245768 | tf_op jit(solution)/shard_map/ppermute | solution.py:317
  86.6 3.0 %collective-permute-start.34 = (f32[32,640]{1,0:T(8,128)S(1)}, f32[32,640]{1,0:T(8,128)S(1)}, u32[]{:S(2)}, u32[]{:S(2)}) collective-permute-start(f32[32,640]{1,0:T(8,128)S(1)} %get-tuple-element.60.refs_13_), channel_id=1, source_target_pairs={{0,2},{1,3},{2,0},{3,1},{4,6},{5,7},{6,4},{7,5},{8,10},{9,11},{10,... | collective-permute-start | bytes 245768 | tf_op jit(solution)/shard_map/ppermute | solution.py:317
  88.6 1.3 %collective-permute-start.37 = (f32[32,640]{1,0:T(8,128)S(1)}, f32[32,640]{1,0:T(8,128)S(1)}, u32[]{:S(2)}, u32[]{:S(2)}) collective-permute-start(f32[32,640]{1,0:T(8,128)S(1)} %collective-permute-done.33.refs_16_), channel_id=1, source_target_pairs={{0,2},{1,3},{2,0},{3,1},{4,6},{5,7},{6,4},{7,5},{8,10},{9,11},{10,... | collective-permute-start | bytes 245768 | tf_op jit(solution)/shard_map/ppermute | solution.py:317
  88.7 1.3 %collective-permute-start.36 = (f32[32,640]{1,0:T(8,128)S(1)}, f32[32,640]{1,0:T(8,128)S(1)}, u32[]{:S(2)}, u32[]{:S(2)}) collective-permute-start(f32[32,640]{1,0:T(8,128)S(1)} %collective-permute-done.32.refs_15_), channel_id=1, source_target_pairs={{0,2},{1,3},{2,0},{3,1},{4,6},{5,7},{6,4},{7,5},{8,10},{9,11},{10,... | collective-permute-start | bytes 245768 | tf_op jit(solution)/shard_map/ppermute | solution.py:317
  89.6 1.3 %collective-permute-start.35 = (f32[32,640]{1,0:T(8,128)S(1)}, f32[32,640]{1,0:T(8,128)S(1)}, u32[]{:S(2)}, u32[]{:S(2)}) collective-permute-start(f32[32,640]{1,0:T(8,128)S(1)} %collective-permute-done.31.refs_14_), channel_id=1, source_target_pairs={{0,2},{1,3},{2,0},{3,1},{4,6},{5,7},{6,4},{7,5},{8,10},{9,11},{10,... | collective-permute-start | bytes 245768 | tf_op jit(solution)/shard_map/ppermute | solution.py:317
  97.1 1.7 %collective-permute-start.38 = (f32[128,640]{1,0:T(8,128)S(1)}, f32[128,640]{1,0:T(8,128)S(1)}, u32[]{:S(2)}, u32[]{:S(2)}) collective-permute-start(f32[128,640]{1,0:T(8,128)S(1)} %slice.79), channel_id=1, source_target_pairs={{0,2},{1,3},{2,0},{3,1},{4,6},{5,7},{6,4},{7,5},{8,10},{9,11},{10,... | collective-permute-start | bytes 983048 | tf_op jit(solution)/shard_map/ppermute | solution.py:317
  98.9 4.6 %collective-permute-start.39 = (f32[32,640]{1,0:T(8,128)S(1)}, f32[32,640]{1,0:T(8,128)S(1)}, u32[]{:S(2)}, u32[]{:S(2)}) collective-permute-start(f32[32,640]{1,0:T(8,128)S(1)} %get-tuple-element.66), channel_id=1, source_target_pairs={{0,4},{1,5},{2,6},{3,7},{4,0},{5,1},{6,2},{7,3},{8,12},{9,13},{10,... | collective-permute-start | bytes 245768 | tf_op jit(solution)/shard_map/ppermute | solution.py:317
  100.4 6.0 %collective-permute-start.41 = (f32[32,640]{1,0:T(8,128)S(1)}, f32[32,640]{1,0:T(8,128)S(1)}, u32[]{:S(2)}, u32[]{:S(2)}) collective-permute-start(f32[32,640]{1,0:T(8,128)S(1)} %get-tuple-element.67), channel_id=1, source_target_pairs={{0,5},{1,4},{2,7},{3,6},{4,1},{5,0},{6,3},{7,2},{8,13},{9,12},{10,... | collective-permute-start | bytes 245768 | tf_op jit(solution)/shard_map/ppermute | solution.py:317
  101.5 4.8 %collective-permute-start.40 = (f32[32,640]{1,0:T(8,128)S(1)}, f32[32,640]{1,0:T(8,128)S(1)}, u32[]{:S(2)}, u32[]{:S(2)}) collective-permute-start(f32[32,640]{1,0:T(8,128)S(1)} %get-tuple-element.68), channel_id=1, source_target_pairs={{0,1},{1,0},{2,3},{3,2},{4,5},{5,4},{6,7},{7,6},{8,9},{9,8},{10,11... | collective-permute-start | bytes 245768 | tf_op jit(solution)/shard_map/ppermute | solution.py:317
  106.4 5.6 %collective-permute-start.44 = (f32[8,640]{1,0:T(8,128)S(1)}, f32[8,640]{1,0:T(8,128)S(1)}, u32[]{:S(2)}, u32[]{:S(2)}) collective-permute-start(f32[8,640]{1,0:T(8,128)S(1)} %get-tuple-element.75), channel_id=1, source_target_pairs={{0,24},{1,25},{2,26},{3,27},{4,28},{5,29},{6,30},{7,31},{8,16},{9,... | collective-permute-start | bytes 61448 | tf_op jit(solution)/shard_map/ppermute | solution.py:317
  108.8 4.7 %collective-permute-start.43 = (f32[8,640]{1,0:T(8,128)S(1)}, f32[8,640]{1,0:T(8,128)S(1)}, u32[]{:S(2)}, u32[]{:S(2)}) collective-permute-start(f32[8,640]{1,0:T(8,128)S(1)} %get-tuple-element.76), channel_id=1, source_target_pairs={{0,16},{1,17},{2,18},{3,19},{4,20},{5,21},{6,22},{7,23},{8,24},{9,... | collective-permute-start | bytes 61448 | tf_op jit(solution)/shard_map/ppermute | solution.py:317
  108.8 4.7 %collective-permute-start.42 = (f32[8,640]{1,0:T(8,128)S(1)}, f32[8,640]{1,0:T(8,128)S(1)}, u32[]{:S(2)}, u32[]{:S(2)}) collective-permute-start(f32[8,640]{1,0:T(8,128)S(1)} %get-tuple-element.77), channel_id=1, source_target_pairs={{0,8},{1,9},{2,10},{3,11},{4,12},{5,13},{6,14},{7,15},{8,0},{9,1},... | collective-permute-start | bytes 61448 | tf_op jit(solution)/shard_map/ppermute | solution.py:317

commit v4 on v3

--- a/solution.py
+++ b/solution.py
@@ -17,6 +17,7 @@
 PAIRS = 5
 WIDTH = PAIRS * 128
 CHUNKS = 2
+PARTS = 3
 AXES = ("pts", "cam")
 
 
@@ -30,6 +31,23 @@
     for by in (4, 2, 1):
         value = value + pltpu.roll(value, by, 0)
     return value
+
+
+def stack_sums(values):
+    row = lax.broadcasted_iota(jnp.int32, values[0].shape, 0)
+    upper = row < 4
+    values = [
+        jnp.where(upper, one, two) + pltpu.roll(jnp.where(upper, two, one), 4, 0)
+        for one, two in zip(values[:4], values[4:])
+    ]
+    for by in (2, 1):
+        first = (row & by) == 0
+        half = len(values) // 2
+        values = [
+            jnp.where(first, one + pltpu.roll(one, 8 - by, 0), two + pltpu.roll(two, by, 0))
+            for one, two in zip(values[:half], values[half:])
+        ]
+    return values[0]
 
 
 def invert(gram):
@@ -69,15 +87,20 @@
     for turn in range(turns):
         copy(point, point_out, turn, 0).wait()
         copy(index, index_out, turn, 1).wait()
-        for i in range(turn * group, (turn + 1) * group):
+        here = range(turn * group, (turn + 1) * group)
+        grams = []
+        for i in here:
             live = (slot < counts[skip + i]).astype(jnp.float32)
             rows = [point_out[i, r] * live for r in range(6)]
             entries = [(0, 0), (0, 1), (0, 2), (1, 1), (1, 2), (2, 2)]
-            gram = [all_slots(rows[a] * rows[b] + rows[3 + a] * rows[3 + b]) for a, b in entries]
-            for a, entry in enumerate((0, 3, 5)):
-                gram[entry] = gram[entry] + damping[a, i : i + 1, :]
-            for a, entry in enumerate(invert(gram)):
-                inverse_out[i, a] = entry
+            grams.append([rows[a] * rows[b] + rows[3 + a] * rows[3 + b] for a, b in entries])
+        gram = [stack_sums([one[a] for one in grams]) for a in range(6)]
+        for a, entry in enumerate((0, 3, 5)):
+            gram[entry] = gram[entry] + damping[a, turn * group : (turn + 1) * group, :]
+        inverse = invert(gram)
+        for turned, i in enumerate(here):
+            for a in range(6):
+                inverse_out[i, a] = jnp.broadcast_to(inverse[a][turned : turned + 1, :], slot.shape)
             wide = index_out[i].astype(jnp.float32)
             for k in range(SLOTS):
                 row = wide[k : k + 1, :].astype(jnp.bfloat16)
@@ -151,31 +174,52 @@
     return q[0] * e[0] + q[1] * e[1]
 
 
-def wide_dot(table, value):
-    both = jnp.dot(
-        table, jnp.concatenate(split_two(value), axis=1), preferred_element_type=jnp.float32
-    )
-    return both[:, :WIDTH] + both[:, WIDTH:]
-
-
 def product_steps(problem, pick, put, vector, out, picked_from, put_to):
-    picked_from[...] = wide_dot(pick[...], vector[...])
+    parts = len(picked_from)
+    share = sum(chunk[0].shape[0] for chunk in problem) // parts
+    rows = share * SLOTS
+    high, low = split_two(vector[...])
+
+    def pick_part(part, p):
+        table = pick[part * rows : (part + 1) * rows, :]
+        here = slice(p * 128, (p + 1) * 128)
+        both = jnp.concatenate([high[:, here], low[:, here]], axis=1)
+        found = jnp.dot(table, both, preferred_element_type=jnp.float32)
+        picked_from[part][:, here] = found[:, :128] + found[:, 128:]
+
+    def put_part(part, p):
+        table = put[:, part * rows : (part + 1) * rows]
+        here = slice(p * 128, (p + 1) * 128)
+        both = jnp.concatenate(split_two(put_to[part][:, here]), axis=1)
+        found = jnp.dot(table, both, preferred_element_type=jnp.float32)
+        found = found[:, :128] + found[:, 128:]
+        out[:, here] = found if part == 0 else out[:, here] + found
+
     total = jnp.zeros((SLOTS, POINTS), jnp.float32)
-    row = 0
-    for cam, point, index, inverse, selector in problem:
-        for i in range(cam.shape[0]):
+    tiles = [(chunk, i) for chunk in problem for i in range(chunk[0].shape[0])]
+    for p in range(PAIRS):
+        pick_part(0, p)
+    for part in range(parts):
+        jobs = [functools.partial(pick_part, part + 1, p) for p in range(PAIRS)] if part + 1 < parts else []
+        jobs += [functools.partial(put_part, part - 1, p) for p in range(PAIRS)] if part else []
+        for turn, ((cam, point, index, inverse, selector), i) in enumerate(tiles[part * share : (part + 1) * share]):
+            due = len(jobs) * turn // share
+            if due > len(jobs) * (turn - 1) // share and turn:
+                jobs[due - 1]()
             total = total + tile_product(
                 lambda r: cam[i, r],
                 lambda r: point[i, r],
                 index[i],
                 lambda a: inverse[i, a],
                 selector[i],
-                picked_from,
-                row,
-                put_to,
+                picked_from[part],
+                turn * SLOTS,
+                put_to[part],
             )
-            row += SLOTS
-    out[...] = wide_dot(put[...], put_to[...])
+        if jobs:
+            jobs[-1]()
+    for p in range(PAIRS):
+        put_part(parts - 1, p)
     return total
 
 
@@ -238,7 +282,8 @@
     pieces, refs = refs[:ranks], refs[ranks:]
     if not first:
         (old_vector, old_energy), refs = refs[:2], refs[2:]
-    out, vector, energy, picked_from, put_to = refs
+    (out, vector, energy), scratch = refs[:3], refs[3:]
+    picked_from, put_to = scratch[: len(scratch) // 2], scratch[len(scratch) // 2 :]
     power = sum([spare_of(piece) for piece in pieces])
     energy[...] = jnp.broadcast_to(power, energy.shape)
     many = pieces[0].shape[0]
@@ -257,7 +302,8 @@
 
 def plain_kernel(chunks, *refs):
     problem = [refs[5 * c : 5 * c + 5] for c in range(chunks)]
-    pick, put, vector, out, picked_from, put_to = refs[5 * chunks :]
+    (pick, put, vector, out), scratch = refs[5 * chunks : 5 * chunks + 4], refs[5 * chunks + 4 :]
+    picked_from, put_to = scratch[: len(scratch) // 2], scratch[len(scratch) // 2 :]
     product_steps(problem, pick, put, vector, out, picked_from, put_to)
 
 
@@ -274,7 +320,7 @@
 
 
 def call_setup(skip, tiles, counts, cam, point, index, damp):
-    group = math.gcd(tiles, 8)
+    group = SLOTS
     shapes = [(tiles,) + array.shape[1:] for array in (cam, point, index)]
     shapes += [(tiles, 6, SLOTS, POINTS), (tiles, SLOTS // 2 * CAMERAS, 2 * POINTS)]
     kinds = [jnp.float32, jnp.float32, jnp.int32, jnp.float32, jnp.bfloat16]
@@ -294,9 +340,10 @@
 
 def call_product(kernel, problem, others, outs):
     tiles = sum(chunk[0].shape[0] for chunk in problem)
-    scratch = pltpu.VMEM((tiles * SLOTS, WIDTH), jnp.float32)
+    parts = math.gcd(tiles, PARTS)
+    scratch = pltpu.VMEM((tiles // parts * SLOTS, WIDTH), jnp.float32)
     held = [pltpu.with_memory_space_constraint(array, pltpu.VMEM) for chunk in problem for array in chunk]
-    return in_vmem(kernel, held + others, outs, [scratch, scratch])
+    return in_vmem(kernel, held + others, outs, [scratch] * (2 * parts))
 
 
 def tables_of(rows, counts, window):

time: 114 us -> 113 us (level)
  Pallas kernels: 27 us -> 25.5 us
  transfers between devices with their start and end apart: 45 -> 45, of which waited for: 33 -> 34; matrix products, arithmetic and copies ran while one was open for 2% -> 2% of each run, Pallas kernels for 6% -> 6%
where the time goes in v4:
time: 113 us
  starting transfers between devices  42.5 us (38%)
  waiting for transfers between devices  40.1 us (35%)
  Pallas kernels  25.5 us (23%)
  other arithmetic  2.65 us (2%)
    ppermute x45, starting transfers between devices, exchange(): return lax.ppermute(array, AXES, [(i, i ^ mask) for i in range(devices)])  42.5 us
    ppermute x45, waiting for transfers between devices, exchange(): return lax.ppermute(array, AXES, [(i, i ^ mask) for i in range(devices)])  40.1 us
    pallas_call x7, Pallas kernels, in_vmem(): pl.pallas_call(kernel, out_shape=[jax.ShapeDtypeStruct(shape, jnp.float32...  18.7 us
    pallas_call x2, Pallas kernels, call_setup(): pl.pallas_call(functools.partial(setup_kernel, skip, group), out_shape=[p...  6.87 us
  transfers between devices with their start and end apart: 45, of which 34 were waited for; matrix products, arithmetic and copies ran while one was open for 2% of the time, Pallas kernels for 6%

profile of v4, /device:TPU:0, one launch (start us, length us, event | category | flops | bytes accessed | tf_op | source)
XLA Modules:
  0.0 112.8 jit_solution(10903006984694638886)
XLA Ops:
  0.6 0.8 select_maximum_fusion.refs_0_
  1.4 5.0 %collective-permute-start.2 = (f32[2,8,640]{2,1,0:T(8,128)S(1)}, f32[2,8,640]{2,1,0:T(8,128)S(1)}, u32[]{:S(2)}, u32[]{:S(2)}) collective-permute-start(f32[2,8,640]{2,1,0:T(8,128)S(1)} %select_maximum_fusion.refs_0_), channel_id=1, source_target_pairs={{0,24},{1,25},{2,26},{3,27},{4,28},{5,29},{6,30},{7,31},{8,16},{9,... | collective-permute-start | bytes 122888 | tf_op jit(solution)/shard_map/ppermute | solution.py:364
  6.4 0.6 collective-permute-start
  7.1 0.7 iota_compare_fusion.2
  7.9 0.7 add_add_fusion
  8.8 0.6 copy-done
  9.5 3.4 %shard_map.104 = (f32[48,18,8,128]{3,2,1,0:T(8,128)S(1)}, f32[48,6,8,128]{3,2,1,0:T(8,128)S(1)}, s32[48,8,128]{2,1,0:T(8,128)S(1)}, f32[48,6,8,128]{3,2,1,0:T(8,128)S(1)}, bf16[48,256,256]{2,1,0:T(8,128)(2,1)S(1)}) custom-call(s32[96]{0:T(128)S(1)} %bitcast.13, f32[96,18,8,128]{3,2,1,0:T(8,128)} %bitcast.15, f32[96,6,8,128]{3,2,1,0:T(8,128)} %bitcast.17, ...), custom_call_target="tpu_custom_call" | custom-call | flops 30000000 | bytes 10000000 | tf_op jit(solution)/shard_map/pallas_call | solution.py:327
  13.1 2.7 %collective-permute-start.5 = (f32[32,640]{1,0:T(8,128)S(1)}, f32[32,640]{1,0:T(8,128)S(1)}, u32[]{:S(2)}, u32[]{:S(2)}) collective-permute-start(f32[32,640]{1,0:T(8,128)S(1)} %get-tuple-element.45.refs_13_), channel_id=1, source_target_pairs={{0,5},{1,4},{2,7},{3,6},{4,1},{5,0},{6,3},{7,2},{8,13},{9,12},{10,... | collective-permute-start | bytes 245768 | tf_op jit(solution)/shard_map/ppermute | solution.py:364
  15.8 0.5 collective-permute-start.4
  16.8 3.4 %shard_map.105 = (f32[48,18,8,128]{3,2,1,0:T(8,128)S(1)}, f32[48,6,8,128]{3,2,1,0:T(8,128)S(1)}, s32[48,8,128]{2,1,0:T(8,128)S(1)}, f32[48,6,8,128]{3,2,1,0:T(8,128)S(1)}, bf16[48,256,256]{2,1,0:T(8,128)(2,1)S(1)}) custom-call(s32[96]{0:T(128)S(1)} %bitcast.14, f32[96,18,8,128]{3,2,1,0:T(8,128)} %bitcast.16, f32[96,6,8,128]{3,2,1,0:T(8,128)} %bitcast.18, ...), custom_call_target="tpu_custom_call" | custom-call | flops 30000000 | bytes 10000000 | tf_op jit(solution)/shard_map/pallas_call | solution.py:327
  20.2 0.5 collective-permute-done.3.refs_14_
  20.8 0.5 collective-permute-start.7
  21.3 0.5 collective-permute-start.9
  22.7 5.6 %shard_map.107 = (f32[256,640]{1,0:T(8,128)S(1)}, f32[256,640]{1,0:T(8,128)S(1)}, f32[8,128]{1,0:T(8,128)S(1)}) custom-call(f32[48,18,8,128]{3,2,1,0:T(8,128)S(1)} %get-tuple-element.34.refs_0_, f32[48,6,8,128]{3,2,1,0:T(8,128)S(1)} %get-tuple-element.35.refs_1_, s32[48,8,128]{2,1,0:T(8,128)S(1)} %get-tuple-element.36.refs_4_.refs_2_, ...), custom_call_target="tpu_custom_call" | custom-call | tf_op jit(solution)/shard_map/pallas_call | solution.py:312
  28.3 0.4 collective-permute-start.10
  28.7 1.3 %collective-permute-done.10 = f32[128,640]{1,0:T(8,128)S(1)} collective-permute-done((f32[128,640]{1,0:T(8,128)S(1)}, f32[128,640]{1,0:T(8,128)S(1)}, u32[]{:S(2)}, u32[]{:S(2)}) %collective-permute-start.10) | collective-permute-done | bytes 327712 | tf_op jit(solution)/shard_map/ppermute | solution.py:364
  30.1 1.3 %collective-permute-start.11 = (f32[32,640]{1,0:T(8,128)S(1)}, f32[32,640]{1,0:T(8,128)S(1)}, u32[]{:S(2)}, u32[]{:S(2)}) collective-permute-start(f32[32,640]{1,0:T(8,128)S(1)} %get-tuple-element.72), channel_id=1, source_target_pairs={{0,4},{1,5},{2,6},{3,7},{4,0},{5,1},{6,2},{7,3},{8,12},{9,13},{10,... | collective-permute-start | bytes 245768 | tf_op jit(solution)/shard_map/ppermute | solution.py:364
  31.4 1.7 %collective-permute-start.13 = (f32[32,640]{1,0:T(8,128)S(1)}, f32[32,640]{1,0:T(8,128)S(1)}, u32[]{:S(2)}, u32[]{:S(2)}) collective-permute-start(f32[32,640]{1,0:T(8,128)S(1)} %get-tuple-element.73), channel_id=1, source_target_pairs={{0,5},{1,4},{2,7},{3,6},{4,1},{5,0},{6,3},{7,2},{8,13},{9,12},{10,... | collective-permute-start | bytes 245768 | tf_op jit(solution)/shard_map/ppermute | solution.py:364
  33.1 0.5 collective-permute-start.12
  33.6 1.3 %collective-permute-done.11 = f32[32,640]{1,0:T(8,128)S(1)} collective-permute-done((f32[32,640]{1,0:T(8,128)S(1)}, f32[32,640]{1,0:T(8,128)S(1)}, u32[]{:S(2)}, u32[]{:S(2)}) %collective-permute-start.11) | collective-permute-done | bytes 81952 | tf_op jit(solution)/shard_map/ppermute | solution.py:364
  34.9 2.4 %collective-permute-done.13 = f32[32,640]{1,0:T(8,128)S(1)} collective-permute-done((f32[32,640]{1,0:T(8,128)S(1)}, f32[32,640]{1,0:T(8,128)S(1)}, u32[]{:S(2)}, u32[]{:S(2)}) %collective-permute-start.13) | collective-permute-done | bytes 81952 | tf_op jit(solution)/shard_map/ppermute | solution.py:364
  37.3 0.5 collective-permute-done.12
  37.9 3.7 %collective-permute-start.16 = (f32[32,640]{1,0:T(8,128)S(1)}, f32[32,640]{1,0:T(8,128)S(1)}, u32[]{:S(2)}, u32[]{:S(2)}) collective-permute-start(f32[32,640]{1,0:T(8,128)S(1)} %fusion.7.refs_0_), channel_id=1, source_target_pairs={{0,24},{1,25},{2,26},{3,27},{4,28},{5,29},{6,30},{7,31},{8,16},{9,... | collective-permute-start | bytes 245768 | tf_op jit(solution)/shard_map/ppermute | solution.py:364
  41.5 0.8 collective-permute-start.14
  42.3 2.4 %collective-permute-done.16.refs_3_ = f32[32,640]{1,0:T(8,128)S(1)} collective-permute-done((f32[32,640]{1,0:T(8,128)S(1)}, f32[32,640]{1,0:T(8,128)S(1)}, u32[]{:S(2)}, u32[]{:S(2)}) %collective-permute-start.16) | collective-permute-done | bytes 81952 | tf_op jit(solution)/shard_map/ppermute | solution.py:364
  44.7 3.4 %collective-permute-done.15.refs_2_ = f32[32,640]{1,0:T(8,128)S(1)} collective-permute-done((f32[32,640]{1,0:T(8,128)S(1)}, f32[32,640]{1,0:T(8,128)S(1)}, u32[]{:S(2)}, u32[]{:S(2)}) %collective-permute-start.15) | collective-permute-done | bytes 81952 | tf_op jit(solution)/shard_map/ppermute | solution.py:364
  48.3 1.9 %collective-permute-start.19 = (f32[32,640]{1,0:T(8,128)S(1)}, f32[32,640]{1,0:T(8,128)S(1)}, u32[]{:S(2)}, u32[]{:S(2)}) collective-permute-start(f32[32,640]{1,0:T(8,128)S(1)} %get-tuple-element.54.refs_13_), channel_id=1, source_target_pairs={{0,5},{1,4},{2,7},{3,6},{4,1},{5,0},{6,3},{7,2},{8,13},{9,12},{10,... | collective-permute-start | bytes 245768 | tf_op jit(solution)/shard_map/ppermute | solution.py:364
  50.2 0.8 collective-permute-start.18
  51.0 0.9 collective-permute-start.17
  51.9 2.1 %collective-permute-done.19.refs_16_ = f32[32,640]{1,0:T(8,128)S(1)} collective-permute-done((f32[32,640]{1,0:T(8,128)S(1)}, f32[32,640]{1,0:T(8,128)S(1)}, u32[]{:S(2)}, u32[]{:S(2)}) %collective-permute-start.19) | collective-permute-done | bytes 81952 | tf_op jit(solution)/shard_map/ppermute | solution.py:364
  54.0 0.7 collective-permute-done.18.refs_15_
  54.6 0.8 collective-permute-done.17.refs_14_
  55.5 0.4 collective-permute-done.22.refs_19_
  55.9 0.8 collective-permute-done.21.refs_18_
  56.7 5.9 %shard_map.109 = (f32[256,640]{1,0:T(8,128)S(1)}, f32[256,640]{1,0:T(8,128)S(1)}, f32[8,128]{1,0:T(8,128)S(1)}) custom-call(f32[48,18,8,128]{3,2,1,0:T(8,128)S(1)} %get-tuple-element.34.refs_0_, f32[48,6,8,128]{3,2,1,0:T(8,128)S(1)} %get-tuple-element.35.refs_1_, s32[48,8,128]{2,1,0:T(8,128)S(1)} %get-tuple-element.36.refs_4_.refs_2_, ...), custom_call_target="tpu_custom_call" | custom-call | tf_op jit(solution)/shard_map/pallas_call | solution.py:312
  62.9 1.5 %collective-permute-done.24 = f32[128,640]{1,0:T(8,128)S(1)} collective-permute-done((f32[128,640]{1,0:T(8,128)S(1)}, f32[128,640]{1,0:T(8,128)S(1)}, u32[]{:S(2)}, u32[]{:S(2)}) %collective-permute-start.24) | collective-permute-done | bytes 327712 | tf_op jit(solution)/shard_map/ppermute | solution.py:364
  64.5 0.9 collective-permute-start.25
  65.4 1.8 %collective-permute-start.27 = (f32[32,640]{1,0:T(8,128)S(1)}, f32[32,640]{1,0:T(8,128)S(1)}, u32[]{:S(2)}, u32[]{:S(2)}) collective-permute-start(f32[32,640]{1,0:T(8,128)S(1)} %get-tuple-element.70), channel_id=1, source_target_pairs={{0,5},{1,4},{2,7},{3,6},{4,1},{5,0},{6,3},{7,2},{8,13},{9,12},{10,... | collective-permute-start | bytes 245768 | tf_op jit(solution)/shard_map/ppermute | solution.py:364
  67.2 0.8 collective-permute-start.26
  68.0 1.9 %collective-permute-done.25 = f32[32,640]{1,0:T(8,128)S(1)} collective-permute-done((f32[32,640]{1,0:T(8,128)S(1)}, f32[32,640]{1,0:T(8,128)S(1)}, u32[]{:S(2)}, u32[]{:S(2)}) %collective-permute-start.25) | collective-permute-done | bytes 81952 | tf_op jit(solution)/shard_map/ppermute | solution.py:364
  69.9 1.5 %collective-permute-done.27 = f32[32,640]{1,0:T(8,128)S(1)} collective-permute-done((f32[32,640]{1,0:T(8,128)S(1)}, f32[32,640]{1,0:T(8,128)S(1)}, u32[]{:S(2)}, u32[]{:S(2)}) %collective-permute-start.27) | collective-permute-done | bytes 81952 | tf_op jit(solution)/shard_map/ppermute | solution.py:364
  71.4 0.6 collective-permute-done.26
  72.0 2.8 %collective-permute-start.30 = (f32[32,640]{1,0:T(8,128)S(1)}, f32[32,640]{1,0:T(8,128)S(1)}, u32[]{:S(2)}, u32[]{:S(2)}) collective-permute-start(f32[32,640]{1,0:T(8,128)S(1)} %fusion.5.refs_0_), channel_id=1, source_target_pairs={{0,24},{1,25},{2,26},{3,27},{4,28},{5,29},{6,30},{7,31},{8,16},{9,... | collective-permute-start | bytes 245768 | tf_op jit(solution)/shard_map/ppermute | solution.py:364
  74.8 1.7 %collective-permute-start.28 = (f32[32,640]{1,0:T(8,128)S(1)}, f32[32,640]{1,0:T(8,128)S(1)}, u32[]{:S(2)}, u32[]{:S(2)}) collective-permute-start(f32[32,640]{1,0:T(8,128)S(1)} %fusion.5.refs_0_), channel_id=1, source_target_pairs={{0,8},{1,9},{2,10},{3,11},{4,12},{5,13},{6,14},{7,15},{8,0},{9,1},... | collective-permute-start | bytes 245768 | tf_op jit(solution)/shard_map/ppermute | solution.py:364
  76.5 1.9 %collective-permute-done.30.refs_3_ = f32[32,640]{1,0:T(8,128)S(1)} collective-permute-done((f32[32,640]{1,0:T(8,128)S(1)}, f32[32,640]{1,0:T(8,128)S(1)}, u32[]{:S(2)}, u32[]{:S(2)}) %collective-permute-start.30) | collective-permute-done | bytes 81952 | tf_op jit(solution)/shard_map/ppermute | solution.py:364
  78.4 3.4 %collective-permute-done.29.refs_2_ = f32[32,640]{1,0:T(8,128)S(1)} collective-permute-done((f32[32,640]{1,0:T(8,128)S(1)}, f32[32,640]{1,0:T(8,128)S(1)}, u32[]{:S(2)}, u32[]{:S(2)}) %collective-permute-start.29) | collective-permute-done | bytes 81952 | tf_op jit(solution)/shard_map/ppermute | solution.py:364
  82.0 1.4 %collective-permute-start.33 = (f32[32,640]{1,0:T(8,128)S(1)}, f32[32,640]{1,0:T(8,128)S(1)}, u32[]{:S(2)}, u32[]{:S(2)}) collective-permute-start(f32[32,640]{1,0:T(8,128)S(1)} %get-tuple-element.60.refs_13_), channel_id=1, source_target_pairs={{0,5},{1,4},{2,7},{3,6},{4,1},{5,0},{6,3},{7,2},{8,13},{9,12},{10,... | collective-permute-start | bytes 245768 | tf_op jit(solution)/shard_map/ppermute | solution.py:364
  83.4 0.9 collective-permute-start.32
  84.3 1.3 %collective-permute-start.31 = (f32[32,640]{1,0:T(8,128)S(1)}, f32[32,640]{1,0:T(8,128)S(1)}, u32[]{:S(2)}, u32[]{:S(2)}) collective-permute-start(f32[32,640]{1,0:T(8,128)S(1)} %get-tuple-element.60.refs_13_), channel_id=1, source_target_pairs={{0,4},{1,5},{2,6},{3,7},{4,0},{5,1},{6,2},{7,3},{8,12},{9,13},{10,... | collective-permute-start | bytes 245768 | tf_op jit(solution)/shard_map/ppermute | solution.py:364
  85.6 2.0 %collective-permute-done.33.refs_16_ = f32[32,640]{1,0:T(8,128)S(1)} collective-permute-done((f32[32,640]{1,0:T(8,128)S(1)}, f32[32,640]{1,0:T(8,128)S(1)}, u32[]{:S(2)}, u32[]{:S(2)}) %collective-permute-start.33) | collective-permute-done | bytes 81952 | tf_op jit(solution)/shard_map/ppermute | solution.py:364
  88.0 0.7 collective-permute-done.31.refs_14_
  89.1 0.9 collective-permute-done.35.refs_18_
  90.0 5.8 %shard_map.111 = (f32[256,640]{1,0:T(8,128)S(1)}, f32[256,640]{1,0:T(8,128)S(1)}, f32[8,128]{1,0:T(8,128)S(1)}) custom-call(f32[48,18,8,128]{3,2,1,0:T(8,128)S(1)} %get-tuple-element.34.refs_0_, f32[48,6,8,128]{3,2,1,0:T(8,128)S(1)} %get-tuple-element.35.refs_1_, s32[48,8,128]{2,1,0:T(8,128)S(1)} %get-tuple-element.36.refs_4_.refs_2_, ...), custom_call_target="tpu_custom_call" | custom-call | tf_op jit(solution)/shard_map/pallas_call | solution.py:312
  96.0 1.5 %collective-permute-done.38 = f32[128,640]{1,0:T(8,128)S(1)} collective-permute-done((f32[128,640]{1,0:T(8,128)S(1)}, f32[128,640]{1,0:T(8,128)S(1)}, u32[]{:S(2)}, u32[]{:S(2)}) %collective-permute-start.38) | collective-permute-done | bytes 327712 | tf_op jit(solution)/shard_map/ppermute | solution.py:364
  97.5 1.3 %collective-permute-start.39 = (f32[32,640]{1,0:T(8,128)S(1)}, f32[32,640]{1,0:T(8,128)S(1)}, u32[]{:S(2)}, u32[]{:S(2)}) collective-permute-start(f32[32,640]{1,0:T(8,128)S(1)} %get-tuple-element.66), channel_id=1, source_target_pairs={{0,4},{1,5},{2,6},{3,7},{4,0},{5,1},{6,2},{7,3},{8,12},{9,13},{10,... | collective-permute-start | bytes 245768 | tf_op jit(solution)/shard_map/ppermute | solution.py:364
  98.9 1.3 %collective-permute-start.41 = (f32[32,640]{1,0:T(8,128)S(1)}, f32[32,640]{1,0:T(8,128)S(1)}, u32[]{:S(2)}, u32[]{:S(2)}) collective-permute-start(f32[32,640]{1,0:T(8,128)S(1)} %get-tuple-element.67), channel_id=1, source_target_pairs={{0,5},{1,4},{2,7},{3,6},{4,1},{5,0},{6,3},{7,2},{8,13},{9,12},{10,... | collective-permute-start | bytes 245768 | tf_op jit(solution)/shard_map/ppermute | solution.py:364
  100.2 0.9 collective-permute-start.40
  101.1 1.0 collective-permute-done.39
  102.1 2.8 %collective-permute-done.41 = f32[32,640]{1,0:T(8,128)S(1)} collective-permute-done((f32[32,640]{1,0:T(8,128)S(1)}, f32[32,640]{1,0:T(8,128)S(1)}, u32[]{:S(2)}, u32[]{:S(2)}) %collective-permute-start.41) | collective-permute-done | bytes 81952 | tf_op jit(solution)/shard_map/ppermute | solution.py:364
  105.1 2.3 %collective-permute-start.44 = (f32[8,640]{1,0:T(8,128)S(1)}, f32[8,640]{1,0:T(8,128)S(1)}, u32[]{:S(2)}, u32[]{:S(2)}) collective-permute-start(f32[8,640]{1,0:T(8,128)S(1)} %get-tuple-element.75), channel_id=1, source_target_pairs={{0,24},{1,25},{2,26},{3,27},{4,28},{5,29},{6,30},{7,31},{8,16},{9,... | collective-permute-start | bytes 61448 | tf_op jit(solution)/shard_map/ppermute | solution.py:364
  107.4 2.2 %collective-permute-start.42 = (f32[8,640]{1,0:T(8,128)S(1)}, f32[8,640]{1,0:T(8,128)S(1)}, u32[]{:S(2)}, u32[]{:S(2)}) collective-permute-start(f32[8,640]{1,0:T(8,128)S(1)} %get-tuple-element.77), channel_id=1, source_target_pairs={{0,8},{1,9},{2,10},{3,11},{4,12},{5,13},{6,14},{7,15},{8,0},{9,1},... | collective-permute-start | bytes 61448 | tf_op jit(solution)/shard_map/ppermute | solution.py:364
  109.6 1.2 %collective-permute-done.44.refs_3_ = f32[8,640]{1,0:T(8,128)S(1)} collective-permute-done((f32[8,640]{1,0:T(8,128)S(1)}, f32[8,640]{1,0:T(8,128)S(1)}, u32[]{:S(2)}, u32[]{:S(2)}) %collective-permute-start.44) | collective-permute-done | bytes 20512 | tf_op jit(solution)/shard_map/ppermute | solution.py:364
  110.7 1.3 %collective-permute-done.43.refs_2_ = f32[8,640]{1,0:T(8,128)S(1)} collective-permute-done((f32[8,640]{1,0:T(8,128)S(1)}, f32[8,640]{1,0:T(8,128)S(1)}, u32[]{:S(2)}, u32[]{:S(2)}) %collective-permute-start.43) | collective-permute-done | bytes 20512 | tf_op jit(solution)/shard_map/ppermute | solution.py:364
  112.1 0.7 shard_map.112
  (65 shorter events, 4.2 us)
Async XLA Ops:
  1.4 11.5 %collective-permute-start.2 = (f32[2,8,640]{2,1,0:T(8,128)S(1)}, f32[2,8,640]{2,1,0:T(8,128)S(1)}, u32[]{:S(2)}, u32[]{:S(2)}) collective-permute-start(f32[2,8,640]{2,1,0:T(8,128)S(1)} %select_maximum_fusion.refs_0_), channel_id=1, source_target_pairs={{0,24},{1,25},{2,26},{3,27},{4,28},{5,29},{6,30},{7,31},{8,16},{9,... | collective-permute-start | bytes 122888 | tf_op jit(solution)/shard_map/ppermute | solution.py:364
  6.4 6.5 %collective-permute-start.1 = (f32[2,8,640]{2,1,0:T(8,128)S(1)}, f32[2,8,640]{2,1,0:T(8,128)S(1)}, u32[]{:S(2)}, u32[]{:S(2)}) collective-permute-start(f32[2,8,640]{2,1,0:T(8,128)S(1)} %select_maximum_fusion.refs_0_), channel_id=1, source_target_pairs={{0,16},{1,17},{2,18},{3,19},{4,20},{5,21},{6,22},{7,23},{8,24},{9,... | collective-permute-start | bytes 122888 | tf_op jit(solution)/shard_map/ppermute | solution.py:364
  6.4 6.5 %collective-permute-start = (f32[2,8,640]{2,1,0:T(8,128)S(1)}, f32[2,8,640]{2,1,0:T(8,128)S(1)}, u32[]{:S(2)}, u32[]{:S(2)}) collective-permute-start(f32[2,8,640]{2,1,0:T(8,128)S(1)} %select_maximum_fusion.refs_0_), channel_id=1, source_target_pairs={{0,8},{1,9},{2,10},{3,11},{4,12},{5,13},{6,14},{7,15},{8,0},{9,1},... | collective-permute-start | bytes 122888 | tf_op jit(solution)/shard_map/ppermute | solution.py:364
  8.8 0.7 copy-start
  9.5 7.3 %copy-start.1 = (s32[1,96]{1,0:T(1,128)S(1)}, s32[1,96]{1,0:T(1,128)}, u32[]{:S(2)}) copy-start(s32[1,96]{1,0:T(1,128)} %param.17) | copy-start | bytes 1156
  13.1 7.1 %collective-permute-start.5 = (f32[32,640]{1,0:T(8,128)S(1)}, f32[32,640]{1,0:T(8,128)S(1)}, u32[]{:S(2)}, u32[]{:S(2)}) collective-permute-start(f32[32,640]{1,0:T(8,128)S(1)} %get-tuple-element.45.refs_13_), channel_id=1, source_target_pairs={{0,5},{1,4},{2,7},{3,6},{4,1},{5,0},{6,3},{7,2},{8,13},{9,12},{10,... | collective-permute-start | bytes 245768 | tf_op jit(solution)/shard_map/ppermute | solution.py:364
  15.8 4.5 %collective-permute-start.4 = (f32[32,640]{1,0:T(8,128)S(1)}, f32[32,640]{1,0:T(8,128)S(1)}, u32[]{:S(2)}, u32[]{:S(2)}) collective-permute-start(f32[32,640]{1,0:T(8,128)S(1)} %get-tuple-element.45.refs_13_), channel_id=1, source_target_pairs={{0,1},{1,0},{2,3},{3,2},{4,5},{5,4},{6,7},{7,6},{8,9},{9,8},{10,11... | collective-permute-start | bytes 245768 | tf_op jit(solution)/shard_map/ppermute | solution.py:364
  16.3 4.4 %collective-permute-start.3 = (f32[32,640]{1,0:T(8,128)S(1)}, f32[32,640]{1,0:T(8,128)S(1)}, u32[]{:S(2)}, u32[]{:S(2)}) collective-permute-start(f32[32,640]{1,0:T(8,128)S(1)} %get-tuple-element.45.refs_13_), channel_id=1, source_target_pairs={{0,4},{1,5},{2,6},{3,7},{4,0},{5,1},{6,2},{7,3},{8,12},{9,13},{10,... | collective-permute-start | bytes 245768 | tf_op jit(solution)/shard_map/ppermute | solution.py:364
  16.8 5.2 %copy-start.2 = (f32[1,8,576]{2,1,0:T(8,128)S(1)}, f32[1,8,576]{2,1,0:T(8,128)}, u32[]{:S(2)}) copy-start(f32[1,8,576]{2,1,0:T(8,128)} %param.10) | copy-start | bytes 55300
  20.8 1.3 %collective-permute-start.6 = (f32[32,640]{1,0:T(8,128)S(1)}, f32[32,640]{1,0:T(8,128)S(1)}, u32[]{:S(2)}, u32[]{:S(2)}) collective-permute-start(f32[32,640]{1,0:T(8,128)S(1)} %get-tuple-element.45.refs_13_), channel_id=1, source_target_pairs={{0,2},{1,3},{2,0},{3,1},{4,6},{5,7},{6,4},{7,5},{8,10},{9,11},{10,... | collective-permute-start | bytes 245768 | tf_op jit(solution)/shard_map/ppermute | solution.py:364
  20.8 1.4 %collective-permute-start.7 = (f32[32,640]{1,0:T(8,128)S(1)}, f32[32,640]{1,0:T(8,128)S(1)}, u32[]{:S(2)}, u32[]{:S(2)}) collective-permute-start(f32[32,640]{1,0:T(8,128)S(1)} %collective-permute-done.3.refs_14_), channel_id=1, source_target_pairs={{0,2},{1,3},{2,0},{3,1},{4,6},{5,7},{6,4},{7,5},{8,10},{9,11},{10,... | collective-permute-start | bytes 245768 | tf_op jit(solution)/shard_map/ppermute | solution.py:364
  21.3 1.3 %collective-permute-start.8 = (f32[32,640]{1,0:T(8,128)S(1)}, f32[32,640]{1,0:T(8,128)S(1)}, u32[]{:S(2)}, u32[]{:S(2)}) collective-permute-start(f32[32,640]{1,0:T(8,128)S(1)} %collective-permute-done.4.refs_15_), channel_id=1, source_target_pairs={{0,2},{1,3},{2,0},{3,1},{4,6},{5,7},{6,4},{7,5},{8,10},{9,11},{10,... | collective-permute-start | bytes 245768 | tf_op jit(solution)/shard_map/ppermute | solution.py:364
  21.3 1.4 %collective-permute-start.9 = (f32[32,640]{1,0:T(8,128)S(1)}, f32[32,640]{1,0:T(8,128)S(1)}, u32[]{:S(2)}, u32[]{:S(2)}) collective-permute-start(f32[32,640]{1,0:T(8,128)S(1)} %collective-permute-done.5.refs_16_), channel_id=1, source_target_pairs={{0,2},{1,3},{2,0},{3,1},{4,6},{5,7},{6,4},{7,5},{8,10},{9,11},{10,... | collective-permute-start | bytes 245768 | tf_op jit(solution)/shard_map/ppermute | solution.py:364
  28.3 1.7 %collective-permute-start.10 = (f32[128,640]{1,0:T(8,128)S(1)}, f32[128,640]{1,0:T(8,128)S(1)}, u32[]{:S(2)}, u32[]{:S(2)}) collective-permute-start(f32[128,640]{1,0:T(8,128)S(1)} %slice.67), channel_id=1, source_target_pairs={{0,2},{1,3},{2,0},{3,1},{4,6},{5,7},{6,4},{7,5},{8,10},{9,11},{10,... | collective-permute-start | bytes 983048 | tf_op jit(solution)/shard_map/ppermute | solution.py:364
  30.1 4.8 %collective-permute-start.11 = (f32[32,640]{1,0:T(8,128)S(1)}, f32[32,640]{1,0:T(8,128)S(1)}, u32[]{:S(2)}, u32[]{:S(2)}) collective-permute-start(f32[32,640]{1,0:T(8,128)S(1)} %get-tuple-element.72), channel_id=1, source_target_pairs={{0,4},{1,5},{2,6},{3,7},{4,0},{5,1},{6,2},{7,3},{8,12},{9,13},{10,... | collective-permute-start | bytes 245768 | tf_op jit(solution)/shard_map/ppermute | solution.py:364
  31.4 5.9 %collective-permute-start.13 = (f32[32,640]{1,0:T(8,128)S(1)}, f32[32,640]{1,0:T(8,128)S(1)}, u32[]{:S(2)}, u32[]{:S(2)}) collective-permute-start(f32[32,640]{1,0:T(8,128)S(1)} %get-tuple-element.73), channel_id=1, source_target_pairs={{0,5},{1,4},{2,7},{3,6},{4,1},{5,0},{6,3},{7,2},{8,13},{9,12},{10,... | collective-permute-start | bytes 245768 | tf_op jit(solution)/shard_map/ppermute | solution.py:364
  33.1 4.7 %collective-permute-start.12 = (f32[32,640]{1,0:T(8,128)S(1)}, f32[32,640]{1,0:T(8,128)S(1)}, u32[]{:S(2)}, u32[]{:S(2)}) collective-permute-start(f32[32,640]{1,0:T(8,128)S(1)} %get-tuple-element.74), channel_id=1, source_target_pairs={{0,1},{1,0},{2,3},{3,2},{4,5},{5,4},{6,7},{7,6},{8,9},{9,8},{10,11... | collective-permute-start | bytes 245768 | tf_op jit(solution)/shard_map/ppermute | solution.py:364
  37.9 6.8 %collective-permute-start.16 = (f32[32,640]{1,0:T(8,128)S(1)}, f32[32,640]{1,0:T(8,128)S(1)}, u32[]{:S(2)}, u32[]{:S(2)}) collective-permute-start(f32[32,640]{1,0:T(8,128)S(1)} %fusion.7.refs_0_), channel_id=1, source_target_pairs={{0,24},{1,25},{2,26},{3,27},{4,28},{5,29},{6,30},{7,31},{8,16},{9,... | collective-permute-start | bytes 245768 | tf_op jit(solution)/shard_map/ppermute | solution.py:364
  41.5 6.5 %collective-permute-start.15 = (f32[32,640]{1,0:T(8,128)S(1)}, f32[32,640]{1,0:T(8,128)S(1)}, u32[]{:S(2)}, u32[]{:S(2)}) collective-permute-start(f32[32,640]{1,0:T(8,128)S(1)} %fusion.7.refs_0_), channel_id=1, source_target_pairs={{0,16},{1,17},{2,18},{3,19},{4,20},{5,21},{6,22},{7,23},{8,24},{9,... | collective-permute-start | bytes 245768 | tf_op jit(solution)/shard_map/ppermute | solution.py:364
  41.5 6.5 %collective-permute-start.14 = (f32[32,640]{1,0:T(8,128)S(1)}, f32[32,640]{1,0:T(8,128)S(1)}, u32[]{:S(2)}, u32[]{:S(2)}) collective-permute-start(f32[32,640]{1,0:T(8,128)S(1)} %fusion.7.refs_0_), channel_id=1, source_target_pairs={{0,8},{1,9},{2,10},{3,11},{4,12},{5,13},{6,14},{7,15},{8,0},{9,1},... | collective-permute-start | bytes 245768 | tf_op jit(solution)/shard_map/ppermute | solution.py:364
  48.3 5.6 %collective-permute-start.19 = (f32[32,640]{1,0:T(8,128)S(1)}, f32[32,640]{1,0:T(8,128)S(1)}, u32[]{:S(2)}, u32[]{:S(2)}) collective-permute-start(f32[32,640]{1,0:T(8,128)S(1)} %get-tuple-element.54.refs_13_), channel_id=1, source_target_pairs={{0,5},{1,4},{2,7},{3,6},{4,1},{5,0},{6,3},{7,2},{8,13},{9,12},{10,... | collective-permute-start | bytes 245768 | tf_op jit(solution)/shard_map/ppermute | solution.py:364
  50.2 4.4 %collective-permute-start.18 = (f32[32,640]{1,0:T(8,128)S(1)}, f32[32,640]{1,0:T(8,128)S(1)}, u32[]{:S(2)}, u32[]{:S(2)}) collective-permute-start(f32[32,640]{1,0:T(8,128)S(1)} %get-tuple-element.54.refs_13_), channel_id=1, source_target_pairs={{0,1},{1,0},{2,3},{3,2},{4,5},{5,4},{6,7},{7,6},{8,9},{9,8},{10,11... | collective-permute-start | bytes 245768 | tf_op jit(solution)/shard_map/ppermute | solution.py:364
  51.0 4.4 %collective-permute-start.17 = (f32[32,640]{1,0:T(8,128)S(1)}, f32[32,640]{1,0:T(8,128)S(1)}, u32[]{:S(2)}, u32[]{:S(2)}) collective-permute-start(f32[32,640]{1,0:T(8,128)S(1)} %get-tuple-element.54.refs_13_), channel_id=1, source_target_pairs={{0,4},{1,5},{2,6},{3,7},{4,0},{5,1},{6,2},{7,3},{8,12},{9,13},{10,... | collective-permute-start | bytes 245768 | tf_op jit(solution)/shard_map/ppermute | solution.py:364
  51.9 3.6 %collective-permute-start.20 = (f32[32,640]{1,0:T(8,128)S(1)}, f32[32,640]{1,0:T(8,128)S(1)}, u32[]{:S(2)}, u32[]{:S(2)}) collective-permute-start(f32[32,640]{1,0:T(8,128)S(1)} %get-tuple-element.54.refs_13_), channel_id=1, source_target_pairs={{0,2},{1,3},{2,0},{3,1},{4,6},{5,7},{6,4},{7,5},{8,10},{9,11},{10,... | collective-permute-start | bytes 245768 | tf_op jit(solution)/shard_map/ppermute | solution.py:364
  53.9 1.5 %collective-permute-start.23 = (f32[32,640]{1,0:T(8,128)S(1)}, f32[32,640]{1,0:T(8,128)S(1)}, u32[]{:S(2)}, u32[]{:S(2)}) collective-permute-start(f32[32,640]{1,0:T(8,128)S(1)} %collective-permute-done.19.refs_16_), channel_id=1, source_target_pairs={{0,2},{1,3},{2,0},{3,1},{4,6},{5,7},{6,4},{7,5},{8,10},{9,11},{10,... | collective-permute-start | bytes 245768 | tf_op jit(solution)/shard_map/ppermute | solution.py:364
  54.6 1.3 %collective-permute-start.22 = (f32[32,640]{1,0:T(8,128)S(1)}, f32[32,640]{1,0:T(8,128)S(1)}, u32[]{:S(2)}, u32[]{:S(2)}) collective-permute-start(f32[32,640]{1,0:T(8,128)S(1)} %collective-permute-done.18.refs_15_), channel_id=1, source_target_pairs={{0,2},{1,3},{2,0},{3,1},{4,6},{5,7},{6,4},{7,5},{8,10},{9,11},{10,... | collective-permute-start | bytes 245768 | tf_op jit(solution)/shard_map/ppermute | solution.py:364
  55.5 1.3 %collective-permute-start.21 = (f32[32,640]{1,0:T(8,128)S(1)}, f32[32,640]{1,0:T(8,128)S(1)}, u32[]{:S(2)}, u32[]{:S(2)}) collective-permute-start(f32[32,640]{1,0:T(8,128)S(1)} %collective-permute-done.17.refs_14_), channel_id=1, source_target_pairs={{0,2},{1,3},{2,0},{3,1},{4,6},{5,7},{6,4},{7,5},{8,10},{9,11},{10,... | collective-permute-start | bytes 245768 | tf_op jit(solution)/shard_map/ppermute | solution.py:364
  62.7 1.7 %collective-permute-start.24 = (f32[128,640]{1,0:T(8,128)S(1)}, f32[128,640]{1,0:T(8,128)S(1)}, u32[]{:S(2)}, u32[]{:S(2)}) collective-permute-start(f32[128,640]{1,0:T(8,128)S(1)} %slice.73), channel_id=1, source_target_pairs={{0,2},{1,3},{2,0},{3,1},{4,6},{5,7},{6,4},{7,5},{8,10},{9,11},{10,... | collective-permute-start | bytes 983048 | tf_op jit(solution)/shard_map/ppermute | solution.py:364
  64.5 5.5 %collective-permute-start.25 = (f32[32,640]{1,0:T(8,128)S(1)}, f32[32,640]{1,0:T(8,128)S(1)}, u32[]{:S(2)}, u32[]{:S(2)}) collective-permute-start(f32[32,640]{1,0:T(8,128)S(1)} %get-tuple-element.69), channel_id=1, source_target_pairs={{0,4},{1,5},{2,6},{3,7},{4,0},{5,1},{6,2},{7,3},{8,12},{9,13},{10,... | collective-permute-start | bytes 245768 | tf_op jit(solution)/shard_map/ppermute | solution.py:364
  65.4 6.0 %collective-permute-start.27 = (f32[32,640]{1,0:T(8,128)S(1)}, f32[32,640]{1,0:T(8,128)S(1)}, u32[]{:S(2)}, u32[]{:S(2)}) collective-permute-start(f32[32,640]{1,0:T(8,128)S(1)} %get-tuple-element.70), channel_id=1, source_target_pairs={{0,5},{1,4},{2,7},{3,6},{4,1},{5,0},{6,3},{7,2},{8,13},{9,12},{10,... | collective-permute-start | bytes 245768 | tf_op jit(solution)/shard_map/ppermute | solution.py:364
  67.2 4.8 %collective-permute-start.26 = (f32[32,640]{1,0:T(8,128)S(1)}, f32[32,640]{1,0:T(8,128)S(1)}, u32[]{:S(2)}, u32[]{:S(2)}) collective-permute-start(f32[32,640]{1,0:T(8,128)S(1)} %get-tuple-element.71), channel_id=1, source_target_pairs={{0,1},{1,0},{2,3},{3,2},{4,5},{5,4},{6,7},{7,6},{8,9},{9,8},{10,11... | collective-permute-start | bytes 245768 | tf_op jit(solution)/shard_map/ppermute | solution.py:364
  72.0 6.3 %collective-permute-start.30 = (f32[32,640]{1,0:T(8,128)S(1)}, f32[32,640]{1,0:T(8,128)S(1)}, u32[]{:S(2)}, u32[]{:S(2)}) collective-permute-start(f32[32,640]{1,0:T(8,128)S(1)} %fusion.5.refs_0_), channel_id=1, source_target_pairs={{0,24},{1,25},{2,26},{3,27},{4,28},{5,29},{6,30},{7,31},{8,16},{9,... | collective-permute-start | bytes 245768 | tf_op jit(solution)/shard_map/ppermute | solution.py:364
  74.8 6.9 %collective-permute-start.29 = (f32[32,640]{1,0:T(8,128)S(1)}, f32[32,640]{1,0:T(8,128)S(1)}, u32[]{:S(2)}, u32[]{:S(2)}) collective-permute-start(f32[32,640]{1,0:T(8,128)S(1)} %fusion.5.refs_0_), channel_id=1, source_target_pairs={{0,16},{1,17},{2,18},{3,19},{4,20},{5,21},{6,22},{7,23},{8,24},{9,... | collective-permute-start | bytes 245768 | tf_op jit(solution)/shard_map/ppermute | solution.py:364
  74.8 6.9 %collective-permute-start.28 = (f32[32,640]{1,0:T(8,128)S(1)}, f32[32,640]{1,0:T(8,128)S(1)}, u32[]{:S(2)}, u32[]{:S(2)}) collective-permute-start(f32[32,640]{1,0:T(8,128)S(1)} %fusion.5.refs_0_), channel_id=1, source_target_pairs={{0,8},{1,9},{2,10},{3,11},{4,12},{5,13},{6,14},{7,15},{8,0},{9,1},... | collective-permute-start | bytes 245768 | tf_op jit(solution)/shard_map/ppermute | solution.py:364
  82.0 5.5 %collective-permute-start.33 = (f32[32,640]{1,0:T(8,128)S(1)}, f32[32,640]{1,0:T(8,128)S(1)}, u32[]{:S(2)}, u32[]{:S(2)}) collective-permute-start(f32[32,640]{1,0:T(8,128)S(1)} %get-tuple-element.60.refs_13_), channel_id=1, source_target_pairs={{0,5},{1,4},{2,7},{3,6},{4,1},{5,0},{6,3},{7,2},{8,13},{9,12},{10,... | collective-permute-start | bytes 245768 | tf_op jit(solution)/shard_map/ppermute | solution.py:364
  83.4 4.4 %collective-permute-start.32 = (f32[32,640]{1,0:T(8,128)S(1)}, f32[32,640]{1,0:T(8,128)S(1)}, u32[]{:S(2)}, u32[]{:S(2)}) collective-permute-start(f32[32,640]{1,0:T(8,128)S(1)} %get-tuple-element.60.refs_13_), channel_id=1, source_target_pairs={{0,1},{1,0},{2,3},{3,2},{4,5},{5,4},{6,7},{7,6},{8,9},{9,8},{10,11... | collective-permute-start | bytes 245768 | tf_op jit(solution)/shard_map/ppermute | solution.py:364
  84.3 4.4 %collective-permute-start.31 = (f32[32,640]{1,0:T(8,128)S(1)}, f32[32,640]{1,0:T(8,128)S(1)}, u32[]{:S(2)}, u32[]{:S(2)}) collective-permute-start(f32[32,640]{1,0:T(8,128)S(1)} %get-tuple-element.60.refs_13_), channel_id=1, source_target_pairs={{0,4},{1,5},{2,6},{3,7},{4,0},{5,1},{6,2},{7,3},{8,12},{9,13},{10,... | collective-permute-start | bytes 245768 | tf_op jit(solution)/shard_map/ppermute | solution.py:364
  85.5 3.2 %collective-permute-start.34 = (f32[32,640]{1,0:T(8,128)S(1)}, f32[32,640]{1,0:T(8,128)S(1)}, u32[]{:S(2)}, u32[]{:S(2)}) collective-permute-start(f32[32,640]{1,0:T(8,128)S(1)} %get-tuple-element.60.refs_13_), channel_id=1, source_target_pairs={{0,2},{1,3},{2,0},{3,1},{4,6},{5,7},{6,4},{7,5},{8,10},{9,11},{10,... | collective-permute-start | bytes 245768 | tf_op jit(solution)/shard_map/ppermute | solution.py:364
  87.5 1.3 %collective-permute-start.37 = (f32[32,640]{1,0:T(8,128)S(1)}, f32[32,640]{1,0:T(8,128)S(1)}, u32[]{:S(2)}, u32[]{:S(2)}) collective-permute-start(f32[32,640]{1,0:T(8,128)S(1)} %collective-permute-done.33.refs_16_), channel_id=1, source_target_pairs={{0,2},{1,3},{2,0},{3,1},{4,6},{5,7},{6,4},{7,5},{8,10},{9,11},{10,... | collective-permute-start | bytes 245768 | tf_op jit(solution)/shard_map/ppermute | solution.py:364
  87.8 1.3 %collective-permute-start.36 = (f32[32,640]{1,0:T(8,128)S(1)}, f32[32,640]{1,0:T(8,128)S(1)}, u32[]{:S(2)}, u32[]{:S(2)}) collective-permute-start(f32[32,640]{1,0:T(8,128)S(1)} %collective-permute-done.32.refs_15_), channel_id=1, source_target_pairs={{0,2},{1,3},{2,0},{3,1},{4,6},{5,7},{6,4},{7,5},{8,10},{9,11},{10,... | collective-permute-start | bytes 245768 | tf_op jit(solution)/shard_map/ppermute | solution.py:364
  88.7 1.3 %collective-permute-start.35 = (f32[32,640]{1,0:T(8,128)S(1)}, f32[32,640]{1,0:T(8,128)S(1)}, u32[]{:S(2)}, u32[]{:S(2)}) collective-permute-start(f32[32,640]{1,0:T(8,128)S(1)} %collective-permute-done.31.refs_14_), channel_id=1, source_target_pairs={{0,2},{1,3},{2,0},{3,1},{4,6},{5,7},{6,4},{7,5},{8,10},{9,11},{10,... | collective-permute-start | bytes 245768 | tf_op jit(solution)/shard_map/ppermute | solution.py:364
  95.8 1.7 %collective-permute-start.38 = (f32[128,640]{1,0:T(8,128)S(1)}, f32[128,640]{1,0:T(8,128)S(1)}, u32[]{:S(2)}, u32[]{:S(2)}) collective-permute-start(f32[128,640]{1,0:T(8,128)S(1)} %slice.79), channel_id=1, source_target_pairs={{0,2},{1,3},{2,0},{3,1},{4,6},{5,7},{6,4},{7,5},{8,10},{9,11},{10,... | collective-permute-start | bytes 983048 | tf_op jit(solution)/shard_map/ppermute | solution.py:364
  97.5 4.6 %collective-permute-start.39 = (f32[32,640]{1,0:T(8,128)S(1)}, f32[32,640]{1,0:T(8,128)S(1)}, u32[]{:S(2)}, u32[]{:S(2)}) collective-permute-start(f32[32,640]{1,0:T(8,128)S(1)} %get-tuple-element.66), channel_id=1, source_target_pairs={{0,4},{1,5},{2,6},{3,7},{4,0},{5,1},{6,2},{7,3},{8,12},{9,13},{10,... | collective-permute-start | bytes 245768 | tf_op jit(solution)/shard_map/ppermute | solution.py:364
  98.9 6.0 %collective-permute-start.41 = (f32[32,640]{1,0:T(8,128)S(1)}, f32[32,640]{1,0:T(8,128)S(1)}, u32[]{:S(2)}, u32[]{:S(2)}) collective-permute-start(f32[32,640]{1,0:T(8,128)S(1)} %get-tuple-element.67), channel_id=1, source_target_pairs={{0,5},{1,4},{2,7},{3,6},{4,1},{5,0},{6,3},{7,2},{8,13},{9,12},{10,... | collective-permute-start | bytes 245768 | tf_op jit(solution)/shard_map/ppermute | solution.py:364
  100.2 4.8 %collective-permute-start.40 = (f32[32,640]{1,0:T(8,128)S(1)}, f32[32,640]{1,0:T(8,128)S(1)}, u32[]{:S(2)}, u32[]{:S(2)}) collective-permute-start(f32[32,640]{1,0:T(8,128)S(1)} %get-tuple-element.68), channel_id=1, source_target_pairs={{0,1},{1,0},{2,3},{3,2},{4,5},{5,4},{6,7},{7,6},{8,9},{9,8},{10,11... | collective-permute-start | bytes 245768 | tf_op jit(solution)/shard_map/ppermute | solution.py:364
  105.1 5.6 %collective-permute-start.44 = (f32[8,640]{1,0:T(8,128)S(1)}, f32[8,640]{1,0:T(8,128)S(1)}, u32[]{:S(2)}, u32[]{:S(2)}) collective-permute-start(f32[8,640]{1,0:T(8,128)S(1)} %get-tuple-element.75), channel_id=1, source_target_pairs={{0,24},{1,25},{2,26},{3,27},{4,28},{5,29},{6,30},{7,31},{8,16},{9,... | collective-permute-start | bytes 61448 | tf_op jit(solution)/shard_map/ppermute | solution.py:364
  107.4 4.7 %collective-permute-start.43 = (f32[8,640]{1,0:T(8,128)S(1)}, f32[8,640]{1,0:T(8,128)S(1)}, u32[]{:S(2)}, u32[]{:S(2)}) collective-permute-start(f32[8,640]{1,0:T(8,128)S(1)} %get-tuple-element.76), channel_id=1, source_target_pairs={{0,16},{1,17},{2,18},{3,19},{4,20},{5,21},{6,22},{7,23},{8,24},{9,... | collective-permute-start | bytes 61448 | tf_op jit(solution)/shard_map/ppermute | solution.py:364
  107.4 4.7 %collective-permute-start.42 = (f32[8,640]{1,0:T(8,128)S(1)}, f32[8,640]{1,0:T(8,128)S(1)}, u32[]{:S(2)}, u32[]{:S(2)}) collective-permute-start(f32[8,640]{1,0:T(8,128)S(1)} %get-tuple-element.77), channel_id=1, source_target_pairs={{0,8},{1,9},{2,10},{3,11},{4,12},{5,13},{6,14},{7,15},{8,0},{9,1},... | collective-permute-start | bytes 61448 | tf_op jit(solution)/shard_map/ppermute | solution.py:364

commit v5 on v4

--- a/solution.py
+++ b/solution.py
@@ -16,7 +16,6 @@
 TILE = CPAR * CAMERAS
 PAIRS = 5
 WIDTH = PAIRS * 128
-CHUNKS = 2
 PARTS = 3
 AXES = ("pts", "cam")
 
@@ -335,7 +334,7 @@
         ],
         compiler_params=pltpu.CompilerParams(vmem_limit_bytes=4 * 2**20),
         cost_estimate=pl.CostEstimate(flops=3 * 10**7, bytes_accessed=10**7, transcendentals=0),
-    )(counts, *[pltpu.with_memory_space_constraint(x, pltpu.HBM) for x in (cam, point, index, damp)])
+    )(*[pltpu.with_memory_space_constraint(x, pltpu.HBM) for x in (counts, cam, point, index, damp)])
 
 
 def call_product(kernel, problem, others, outs):
@@ -479,9 +478,9 @@
         cam_index[0],
         jnp.transpose(damp_pt[0], (1, 0, 2)),
     )
-    chunks = math.gcd(cam_jac.shape[1], CHUNKS)
-    tiles = cam_jac.shape[1] // chunks
-    problem = [call_setup(chunk * tiles, tiles, *arrays) for chunk in range(chunks)]
+    tiles = cam_jac.shape[1]
+    first = tiles * 5 // (12 * SLOTS) * SLOTS
+    problem = [call_setup(0, first, *arrays), call_setup(first, tiles - first, *arrays)]
     groups, shards = lax.axis_size("cam"), lax.axis_size("pts")
     plan = two_groups if groups == 2 and shards in (4, 8, 16, 32) else many_groups
     return tuple(plan(rhs[0], damp_cam[0], precond[0], problem, tile_ids[0], counts[0]))

time: 113 us -> 112 us (level)
  transfers between devices with their start and end apart: 45 -> 45, of which waited for: 34 -> 32; matrix products, arithmetic and copies ran while one was open for 2% -> 2% of each run, Pallas kernels for 6% -> 6%
where the time goes in v5:
time: 112 us
  starting transfers between devices  42.8 us (38%)
  waiting for transfers between devices  39.7 us (35%)
  Pallas kernels  25.4 us (23%)
  other arithmetic  2.63 us (2%)
    ppermute x45, starting transfers between devices, exchange(): return lax.ppermute(array, AXES, [(i, i ^ mask) for i in range(devices)])  42.8 us
    ppermute x45, waiting for transfers between devices, exchange(): return lax.ppermute(array, AXES, [(i, i ^ mask) for i in range(devices)])  39.7 us
    pallas_call x7, Pallas kernels, in_vmem(): pl.pallas_call(kernel, out_shape=[jax.ShapeDtypeStruct(shape, jnp.float32...  18.1 us
    pallas_call x2, Pallas kernels, call_setup(): pl.pallas_call(functools.partial(setup_kernel, skip, group), out_shape=[p...  7.25 us
  transfers between devices with their start and end apart: 45, of which 32 were waited for; matrix products, arithmetic and copies ran while one was open for 2% of the time, Pallas kernels for 6%

profile of v5, /device:TPU:0, one launch (start us, length us, event | category | flops | bytes accessed | tf_op | source)
XLA Modules:
  0.0 111.8 jit_solution(15664965221949044256)
XLA Ops:
  0.6 0.8 select_maximum_fusion.refs_0_
  1.4 5.0 %collective-permute-start.2 = (f32[2,8,640]{2,1,0:T(8,128)S(1)}, f32[2,8,640]{2,1,0:T(8,128)S(1)}, u32[]{:S(2)}, u32[]{:S(2)}) collective-permute-start(f32[2,8,640]{2,1,0:T(8,128)S(1)} %select_maximum_fusion.refs_0_), channel_id=1, source_target_pairs={{0,24},{1,25},{2,26},{3,27},{4,28},{5,29},{6,30},{7,31},{8,16},{9,... | collective-permute-start | bytes 122888 | tf_op jit(solution)/shard_map/ppermute | solution.py:363
  6.4 0.6 collective-permute-start
  7.1 0.7 iota_compare_fusion.2
  7.9 0.7 add_add_fusion
  8.8 3.2 %shard_map.104 = (f32[40,18,8,128]{3,2,1,0:T(8,128)S(1)}, f32[40,6,8,128]{3,2,1,0:T(8,128)S(1)}, s32[40,8,128]{2,1,0:T(8,128)S(1)}, f32[40,6,8,128]{3,2,1,0:T(8,128)S(1)}, bf16[40,256,256]{2,1,0:T(8,128)(2,1)S(1)}) custom-call(s32[96]{0:T(128)} %bitcast.22, f32[96,18,8,128]{3,2,1,0:T(8,128)} %bitcast.12, f32[96,6,8,128]{3,2,1,0:T(8,128)} %bitcast.14, ...), custom_call_target="tpu_custom_call" | custom-call | flops 30000000 | bytes 10000000 | tf_op jit(solution)/shard_map/pallas_call | solution.py:326
  12.2 2.7 %collective-permute-start.5 = (f32[32,640]{1,0:T(8,128)S(1)}, f32[32,640]{1,0:T(8,128)S(1)}, u32[]{:S(2)}, u32[]{:S(2)}) collective-permute-start(f32[32,640]{1,0:T(8,128)S(1)} %get-tuple-element.45.refs_13_), channel_id=1, source_target_pairs={{0,5},{1,4},{2,7},{3,6},{4,1},{5,0},{6,3},{7,2},{8,13},{9,12},{10,... | collective-permute-start | bytes 245768 | tf_op jit(solution)/shard_map/ppermute | solution.py:363
  14.9 0.5 collective-permute-start.4
  15.4 0.4 collective-permute-start.3
  15.9 4.0 %shard_map.105 = (f32[56,18,8,128]{3,2,1,0:T(8,128)S(1)}, f32[56,6,8,128]{3,2,1,0:T(8,128)S(1)}, s32[56,8,128]{2,1,0:T(8,128)S(1)}, f32[56,6,8,128]{3,2,1,0:T(8,128)S(1)}, bf16[56,256,256]{2,1,0:T(8,128)(2,1)S(1)}) custom-call(s32[96]{0:T(128)} %bitcast.23, f32[96,18,8,128]{3,2,1,0:T(8,128)} %bitcast.13, f32[96,6,8,128]{3,2,1,0:T(8,128)} %bitcast.15, ...), custom_call_target="tpu_custom_call" | custom-call | flops 30000000 | bytes 10000000 | tf_op jit(solution)/shard_map/pallas_call | solution.py:326
  20.0 0.5 collective-permute-start.7
  20.6 0.4 collective-permute-start.9
  21.5 0.4 collective-permute-done.8.refs_19_
  22.0 5.4 %shard_map.107 = (f32[256,640]{1,0:T(8,128)S(1)}, f32[256,640]{1,0:T(8,128)S(1)}, f32[8,128]{1,0:T(8,128)S(1)}) custom-call(f32[40,18,8,128]{3,2,1,0:T(8,128)S(1)} %get-tuple-element.34.refs_0_, f32[40,6,8,128]{3,2,1,0:T(8,128)S(1)} %get-tuple-element.35.refs_1_, s32[40,8,128]{2,1,0:T(8,128)S(1)} %get-tuple-element.36.refs_4_.refs_2_, ...), custom_call_target="tpu_custom_call" | custom-call | tf_op jit(solution)/shard_map/pallas_call | solution.py:311
  27.4 0.4 collective-permute-start.10
  27.8 1.3 %collective-permute-done.10 = f32[128,640]{1,0:T(8,128)S(1)} collective-permute-done((f32[128,640]{1,0:T(8,128)S(1)}, f32[128,640]{1,0:T(8,128)S(1)}, u32[]{:S(2)}, u32[]{:S(2)}) %collective-permute-start.10) | collective-permute-done | bytes 327712 | tf_op jit(solution)/shard_map/ppermute | solution.py:363
  29.1 1.8 %collective-permute-start.11 = (f32[32,640]{1,0:T(8,128)S(1)}, f32[32,640]{1,0:T(8,128)S(1)}, u32[]{:S(2)}, u32[]{:S(2)}) collective-permute-start(f32[32,640]{1,0:T(8,128)S(1)} %get-tuple-element.72), channel_id=1, source_target_pairs={{0,4},{1,5},{2,6},{3,7},{4,0},{5,1},{6,2},{7,3},{8,12},{9,13},{10,... | collective-permute-start | bytes 245768 | tf_op jit(solution)/shard_map/ppermute | solution.py:363
  30.9 1.4 %collective-permute-start.13 = (f32[32,640]{1,0:T(8,128)S(1)}, f32[32,640]{1,0:T(8,128)S(1)}, u32[]{:S(2)}, u32[]{:S(2)}) collective-permute-start(f32[32,640]{1,0:T(8,128)S(1)} %get-tuple-element.73), channel_id=1, source_target_pairs={{0,5},{1,4},{2,7},{3,6},{4,1},{5,0},{6,3},{7,2},{8,13},{9,12},{10,... | collective-permute-start | bytes 245768 | tf_op jit(solution)/shard_map/ppermute | solution.py:363
  32.3 0.4 collective-permute-start.12
  32.7 2.2 %collective-permute-done.11 = f32[32,640]{1,0:T(8,128)S(1)} collective-permute-done((f32[32,640]{1,0:T(8,128)S(1)}, f32[32,640]{1,0:T(8,128)S(1)}, u32[]{:S(2)}, u32[]{:S(2)}) %collective-permute-start.11) | collective-permute-done | bytes 81952 | tf_op jit(solution)/shard_map/ppermute | solution.py:363
  34.9 1.9 %collective-permute-done.13 = f32[32,640]{1,0:T(8,128)S(1)} collective-permute-done((f32[32,640]{1,0:T(8,128)S(1)}, f32[32,640]{1,0:T(8,128)S(1)}, u32[]{:S(2)}, u32[]{:S(2)}) %collective-permute-start.13) | collective-permute-done | bytes 81952 | tf_op jit(solution)/shard_map/ppermute | solution.py:363
  36.9 3.8 %collective-permute-start.16 = (f32[32,640]{1,0:T(8,128)S(1)}, f32[32,640]{1,0:T(8,128)S(1)}, u32[]{:S(2)}, u32[]{:S(2)}) collective-permute-start(f32[32,640]{1,0:T(8,128)S(1)} %fusion.7.refs_0_), channel_id=1, source_target_pairs={{0,24},{1,25},{2,26},{3,27},{4,28},{5,29},{6,30},{7,31},{8,16},{9,... | collective-permute-start | bytes 245768 | tf_op jit(solution)/shard_map/ppermute | solution.py:363
  40.7 0.6 collective-permute-start.14
  41.4 2.5 %collective-permute-done.16.refs_3_ = f32[32,640]{1,0:T(8,128)S(1)} collective-permute-done((f32[32,640]{1,0:T(8,128)S(1)}, f32[32,640]{1,0:T(8,128)S(1)}, u32[]{:S(2)}, u32[]{:S(2)}) %collective-permute-start.16) | collective-permute-done | bytes 81952 | tf_op jit(solution)/shard_map/ppermute | solution.py:363
  43.9 3.3 %collective-permute-done.15.refs_2_ = f32[32,640]{1,0:T(8,128)S(1)} collective-permute-done((f32[32,640]{1,0:T(8,128)S(1)}, f32[32,640]{1,0:T(8,128)S(1)}, u32[]{:S(2)}, u32[]{:S(2)}) %collective-permute-start.15) | collective-permute-done | bytes 81952 | tf_op jit(solution)/shard_map/ppermute | solution.py:363
  47.5 2.2 %collective-permute-start.19 = (f32[32,640]{1,0:T(8,128)S(1)}, f32[32,640]{1,0:T(8,128)S(1)}, u32[]{:S(2)}, u32[]{:S(2)}) collective-permute-start(f32[32,640]{1,0:T(8,128)S(1)} %get-tuple-element.54.refs_13_), channel_id=1, source_target_pairs={{0,5},{1,4},{2,7},{3,6},{4,1},{5,0},{6,3},{7,2},{8,13},{9,12},{10,... | collective-permute-start | bytes 245768 | tf_op jit(solution)/shard_map/ppermute | solution.py:363
  49.7 0.8 collective-permute-start.18
  50.5 0.6 collective-permute-start.17
  51.1 2.0 %collective-permute-done.19.refs_16_ = f32[32,640]{1,0:T(8,128)S(1)} collective-permute-done((f32[32,640]{1,0:T(8,128)S(1)}, f32[32,640]{1,0:T(8,128)S(1)}, u32[]{:S(2)}, u32[]{:S(2)}) %collective-permute-start.19) | collective-permute-done | bytes 81952 | tf_op jit(solution)/shard_map/ppermute | solution.py:363
  53.1 1.0 collective-permute-done.18.refs_15_
  54.1 0.8 collective-permute-done.17.refs_14_
  55.0 0.4 collective-permute-done.22.refs_19_
  55.4 0.8 collective-permute-done.21.refs_18_
  56.2 5.8 %shard_map.109 = (f32[256,640]{1,0:T(8,128)S(1)}, f32[256,640]{1,0:T(8,128)S(1)}, f32[8,128]{1,0:T(8,128)S(1)}) custom-call(f32[40,18,8,128]{3,2,1,0:T(8,128)S(1)} %get-tuple-element.34.refs_0_, f32[40,6,8,128]{3,2,1,0:T(8,128)S(1)} %get-tuple-element.35.refs_1_, s32[40,8,128]{2,1,0:T(8,128)S(1)} %get-tuple-element.36.refs_4_.refs_2_, ...), custom_call_target="tpu_custom_call" | custom-call | tf_op jit(solution)/shard_map/pallas_call | solution.py:311
  62.2 1.5 %collective-permute-done.24 = f32[128,640]{1,0:T(8,128)S(1)} collective-permute-done((f32[128,640]{1,0:T(8,128)S(1)}, f32[128,640]{1,0:T(8,128)S(1)}, u32[]{:S(2)}, u32[]{:S(2)}) %collective-permute-start.24) | collective-permute-done | bytes 327712 | tf_op jit(solution)/shard_map/ppermute | solution.py:363
  63.8 0.6 collective-permute-start.25
  64.4 2.1 %collective-permute-start.27 = (f32[32,640]{1,0:T(8,128)S(1)}, f32[32,640]{1,0:T(8,128)S(1)}, u32[]{:S(2)}, u32[]{:S(2)}) collective-permute-start(f32[32,640]{1,0:T(8,128)S(1)} %get-tuple-element.70), channel_id=1, source_target_pairs={{0,5},{1,4},{2,7},{3,6},{4,1},{5,0},{6,3},{7,2},{8,13},{9,12},{10,... | collective-permute-start | bytes 245768 | tf_op jit(solution)/shard_map/ppermute | solution.py:363
  66.5 0.8 collective-permute-start.26
  67.3 2.2 %collective-permute-done.25 = f32[32,640]{1,0:T(8,128)S(1)} collective-permute-done((f32[32,640]{1,0:T(8,128)S(1)}, f32[32,640]{1,0:T(8,128)S(1)}, u32[]{:S(2)}, u32[]{:S(2)}) %collective-permute-start.25) | collective-permute-done | bytes 81952 | tf_op jit(solution)/shard_map/ppermute | solution.py:363
  69.6 0.8 collective-permute-done.27
  70.4 0.9 collective-permute-done.26
  71.3 2.8 %collective-permute-start.30 = (f32[32,640]{1,0:T(8,128)S(1)}, f32[32,640]{1,0:T(8,128)S(1)}, u32[]{:S(2)}, u32[]{:S(2)}) collective-permute-start(f32[32,640]{1,0:T(8,128)S(1)} %fusion.5.refs_0_), channel_id=1, source_target_pairs={{0,24},{1,25},{2,26},{3,27},{4,28},{5,29},{6,30},{7,31},{8,16},{9,... | collective-permute-start | bytes 245768 | tf_op jit(solution)/shard_map/ppermute | solution.py:363
  74.1 1.7 %collective-permute-start.28 = (f32[32,640]{1,0:T(8,128)S(1)}, f32[32,640]{1,0:T(8,128)S(1)}, u32[]{:S(2)}, u32[]{:S(2)}) collective-permute-start(f32[32,640]{1,0:T(8,128)S(1)} %fusion.5.refs_0_), channel_id=1, source_target_pairs={{0,8},{1,9},{2,10},{3,11},{4,12},{5,13},{6,14},{7,15},{8,0},{9,1},... | collective-permute-start | bytes 245768 | tf_op jit(solution)/shard_map/ppermute | solution.py:363
  75.8 1.9 %collective-permute-done.30.refs_3_ = f32[32,640]{1,0:T(8,128)S(1)} collective-permute-done((f32[32,640]{1,0:T(8,128)S(1)}, f32[32,640]{1,0:T(8,128)S(1)}, u32[]{:S(2)}, u32[]{:S(2)}) %collective-permute-start.30) | collective-permute-done | bytes 81952 | tf_op jit(solution)/shard_map/ppermute | solution.py:363
  77.7 3.3 %collective-permute-done.29.refs_2_ = f32[32,640]{1,0:T(8,128)S(1)} collective-permute-done((f32[32,640]{1,0:T(8,128)S(1)}, f32[32,640]{1,0:T(8,128)S(1)}, u32[]{:S(2)}, u32[]{:S(2)}) %collective-permute-start.29) | collective-permute-done | bytes 81952 | tf_op jit(solution)/shard_map/ppermute | solution.py:363
  81.3 1.2 %collective-permute-start.33 = (f32[32,640]{1,0:T(8,128)S(1)}, f32[32,640]{1,0:T(8,128)S(1)}, u32[]{:S(2)}, u32[]{:S(2)}) collective-permute-start(f32[32,640]{1,0:T(8,128)S(1)} %get-tuple-element.60.refs_13_), channel_id=1, source_target_pairs={{0,5},{1,4},{2,7},{3,6},{4,1},{5,0},{6,3},{7,2},{8,13},{9,12},{10,... | collective-permute-start | bytes 245768 | tf_op jit(solution)/shard_map/ppermute | solution.py:363
  82.4 0.9 collective-permute-start.32
  83.3 1.5 %collective-permute-start.31 = (f32[32,640]{1,0:T(8,128)S(1)}, f32[32,640]{1,0:T(8,128)S(1)}, u32[]{:S(2)}, u32[]{:S(2)}) collective-permute-start(f32[32,640]{1,0:T(8,128)S(1)} %get-tuple-element.60.refs_13_), channel_id=1, source_target_pairs={{0,4},{1,5},{2,6},{3,7},{4,0},{5,1},{6,2},{7,3},{8,12},{9,13},{10,... | collective-permute-start | bytes 245768 | tf_op jit(solution)/shard_map/ppermute | solution.py:363
  84.8 2.0 %collective-permute-done.33.refs_16_ = f32[32,640]{1,0:T(8,128)S(1)} collective-permute-done((f32[32,640]{1,0:T(8,128)S(1)}, f32[32,640]{1,0:T(8,128)S(1)}, u32[]{:S(2)}, u32[]{:S(2)}) %collective-permute-start.33) | collective-permute-done | bytes 81952 | tf_op jit(solution)/shard_map/ppermute | solution.py:363
  86.9 0.4 collective-permute-start.36
  87.3 0.5 collective-permute-done.31.refs_14_
  88.2 0.8 collective-permute-done.35.refs_18_
  89.0 5.6 %shard_map.111 = (f32[256,640]{1,0:T(8,128)S(1)}, f32[256,640]{1,0:T(8,128)S(1)}, f32[8,128]{1,0:T(8,128)S(1)}) custom-call(f32[40,18,8,128]{3,2,1,0:T(8,128)S(1)} %get-tuple-element.34.refs_0_, f32[40,6,8,128]{3,2,1,0:T(8,128)S(1)} %get-tuple-element.35.refs_1_, s32[40,8,128]{2,1,0:T(8,128)S(1)} %get-tuple-element.36.refs_4_.refs_2_, ...), custom_call_target="tpu_custom_call" | custom-call | tf_op jit(solution)/shard_map/pallas_call | solution.py:311
  94.9 1.5 %collective-permute-done.38 = f32[128,640]{1,0:T(8,128)S(1)} collective-permute-done((f32[128,640]{1,0:T(8,128)S(1)}, f32[128,640]{1,0:T(8,128)S(1)}, u32[]{:S(2)}, u32[]{:S(2)}) %collective-permute-start.38) | collective-permute-done | bytes 327712 | tf_op jit(solution)/shard_map/ppermute | solution.py:363
  96.4 1.6 %collective-permute-start.39 = (f32[32,640]{1,0:T(8,128)S(1)}, f32[32,640]{1,0:T(8,128)S(1)}, u32[]{:S(2)}, u32[]{:S(2)}) collective-permute-start(f32[32,640]{1,0:T(8,128)S(1)} %get-tuple-element.66), channel_id=1, source_target_pairs={{0,4},{1,5},{2,6},{3,7},{4,0},{5,1},{6,2},{7,3},{8,12},{9,13},{10,... | collective-permute-start | bytes 245768 | tf_op jit(solution)/shard_map/ppermute | solution.py:363
  98.0 1.1 collective-permute-start.41
  99.1 0.9 collective-permute-start.40
  100.0 1.1 %collective-permute-done.39 = f32[32,640]{1,0:T(8,128)S(1)} collective-permute-done((f32[32,640]{1,0:T(8,128)S(1)}, f32[32,640]{1,0:T(8,128)S(1)}, u32[]{:S(2)}, u32[]{:S(2)}) %collective-permute-start.39) | collective-permute-done | bytes 81952 | tf_op jit(solution)/shard_map/ppermute | solution.py:363
  101.1 2.9 %collective-permute-done.41 = f32[32,640]{1,0:T(8,128)S(1)} collective-permute-done((f32[32,640]{1,0:T(8,128)S(1)}, f32[32,640]{1,0:T(8,128)S(1)}, u32[]{:S(2)}, u32[]{:S(2)}) %collective-permute-start.41) | collective-permute-done | bytes 81952 | tf_op jit(solution)/shard_map/ppermute | solution.py:363
  104.0 2.4 %collective-permute-start.44 = (f32[8,640]{1,0:T(8,128)S(1)}, f32[8,640]{1,0:T(8,128)S(1)}, u32[]{:S(2)}, u32[]{:S(2)}) collective-permute-start(f32[8,640]{1,0:T(8,128)S(1)} %get-tuple-element.75), channel_id=1, source_target_pairs={{0,24},{1,25},{2,26},{3,27},{4,28},{5,29},{6,30},{7,31},{8,16},{9,... | collective-permute-start | bytes 61448 | tf_op jit(solution)/shard_map/ppermute | solution.py:363
  106.4 2.1 %collective-permute-start.42 = (f32[8,640]{1,0:T(8,128)S(1)}, f32[8,640]{1,0:T(8,128)S(1)}, u32[]{:S(2)}, u32[]{:S(2)}) collective-permute-start(f32[8,640]{1,0:T(8,128)S(1)} %get-tuple-element.77), channel_id=1, source_target_pairs={{0,8},{1,9},{2,10},{3,11},{4,12},{5,13},{6,14},{7,15},{8,0},{9,1},... | collective-permute-start | bytes 61448 | tf_op jit(solution)/shard_map/ppermute | solution.py:363
  108.5 1.2 %collective-permute-done.44.refs_3_ = f32[8,640]{1,0:T(8,128)S(1)} collective-permute-done((f32[8,640]{1,0:T(8,128)S(1)}, f32[8,640]{1,0:T(8,128)S(1)}, u32[]{:S(2)}, u32[]{:S(2)}) %collective-permute-start.44) | collective-permute-done | bytes 20512 | tf_op jit(solution)/shard_map/ppermute | solution.py:363
  109.7 1.4 %collective-permute-done.43.refs_2_ = f32[8,640]{1,0:T(8,128)S(1)} collective-permute-done((f32[8,640]{1,0:T(8,128)S(1)}, f32[8,640]{1,0:T(8,128)S(1)}, u32[]{:S(2)}, u32[]{:S(2)}) %collective-permute-start.43) | collective-permute-done | bytes 20512 | tf_op jit(solution)/shard_map/ppermute | solution.py:363
  111.1 0.7 shard_map.112
  (61 shorter events, 3.2 us)
Async XLA Ops:
  1.4 10.7 %collective-permute-start.2 = (f32[2,8,640]{2,1,0:T(8,128)S(1)}, f32[2,8,640]{2,1,0:T(8,128)S(1)}, u32[]{:S(2)}, u32[]{:S(2)}) collective-permute-start(f32[2,8,640]{2,1,0:T(8,128)S(1)} %select_maximum_fusion.refs_0_), channel_id=1, source_target_pairs={{0,24},{1,25},{2,26},{3,27},{4,28},{5,29},{6,30},{7,31},{8,16},{9,... | collective-permute-start | bytes 122888 | tf_op jit(solution)/shard_map/ppermute | solution.py:363
  6.4 5.6 %collective-permute-start.1 = (f32[2,8,640]{2,1,0:T(8,128)S(1)}, f32[2,8,640]{2,1,0:T(8,128)S(1)}, u32[]{:S(2)}, u32[]{:S(2)}) collective-permute-start(f32[2,8,640]{2,1,0:T(8,128)S(1)} %select_maximum_fusion.refs_0_), channel_id=1, source_target_pairs={{0,16},{1,17},{2,18},{3,19},{4,20},{5,21},{6,22},{7,23},{8,24},{9,... | collective-permute-start | bytes 122888 | tf_op jit(solution)/shard_map/ppermute | solution.py:363
  6.4 5.6 %collective-permute-start = (f32[2,8,640]{2,1,0:T(8,128)S(1)}, f32[2,8,640]{2,1,0:T(8,128)S(1)}, u32[]{:S(2)}, u32[]{:S(2)}) collective-permute-start(f32[2,8,640]{2,1,0:T(8,128)S(1)} %select_maximum_fusion.refs_0_), channel_id=1, source_target_pairs={{0,8},{1,9},{2,10},{3,11},{4,12},{5,13},{6,14},{7,15},{8,0},{9,1},... | collective-permute-start | bytes 122888 | tf_op jit(solution)/shard_map/ppermute | solution.py:363
  12.2 7.7 %collective-permute-start.5 = (f32[32,640]{1,0:T(8,128)S(1)}, f32[32,640]{1,0:T(8,128)S(1)}, u32[]{:S(2)}, u32[]{:S(2)}) collective-permute-start(f32[32,640]{1,0:T(8,128)S(1)} %get-tuple-element.45.refs_13_), channel_id=1, source_target_pairs={{0,5},{1,4},{2,7},{3,6},{4,1},{5,0},{6,3},{7,2},{8,13},{9,12},{10,... | collective-permute-start | bytes 245768 | tf_op jit(solution)/shard_map/ppermute | solution.py:363
  14.9 5.0 %collective-permute-start.4 = (f32[32,640]{1,0:T(8,128)S(1)}, f32[32,640]{1,0:T(8,128)S(1)}, u32[]{:S(2)}, u32[]{:S(2)}) collective-permute-start(f32[32,640]{1,0:T(8,128)S(1)} %get-tuple-element.45.refs_13_), channel_id=1, source_target_pairs={{0,1},{1,0},{2,3},{3,2},{4,5},{5,4},{6,7},{7,6},{8,9},{9,8},{10,11... | collective-permute-start | bytes 245768 | tf_op jit(solution)/shard_map/ppermute | solution.py:363
  15.4 4.5 %collective-permute-start.3 = (f32[32,640]{1,0:T(8,128)S(1)}, f32[32,640]{1,0:T(8,128)S(1)}, u32[]{:S(2)}, u32[]{:S(2)}) collective-permute-start(f32[32,640]{1,0:T(8,128)S(1)} %get-tuple-element.45.refs_13_), channel_id=1, source_target_pairs={{0,4},{1,5},{2,6},{3,7},{4,0},{5,1},{6,2},{7,3},{8,12},{9,13},{10,... | collective-permute-start | bytes 245768 | tf_op jit(solution)/shard_map/ppermute | solution.py:363
  15.9 5.3 %copy-start = (f32[1,8,576]{2,1,0:T(8,128)S(1)}, f32[1,8,576]{2,1,0:T(8,128)}, u32[]{:S(2)}) copy-start(f32[1,8,576]{2,1,0:T(8,128)} %param.10) | copy-start | bytes 55300
  20.0 1.3 %collective-permute-start.6 = (f32[32,640]{1,0:T(8,128)S(1)}, f32[32,640]{1,0:T(8,128)S(1)}, u32[]{:S(2)}, u32[]{:S(2)}) collective-permute-start(f32[32,640]{1,0:T(8,128)S(1)} %get-tuple-element.45.refs_13_), channel_id=1, source_target_pairs={{0,2},{1,3},{2,0},{3,1},{4,6},{5,7},{6,4},{7,5},{8,10},{9,11},{10,... | collective-permute-start | bytes 245768 | tf_op jit(solution)/shard_map/ppermute | solution.py:363
  20.0 1.4 %collective-permute-start.7 = (f32[32,640]{1,0:T(8,128)S(1)}, f32[32,640]{1,0:T(8,128)S(1)}, u32[]{:S(2)}, u32[]{:S(2)}) collective-permute-start(f32[32,640]{1,0:T(8,128)S(1)} %collective-permute-done.3.refs_14_), channel_id=1, source_target_pairs={{0,2},{1,3},{2,0},{3,1},{4,6},{5,7},{6,4},{7,5},{8,10},{9,11},{10,... | collective-permute-start | bytes 245768 | tf_op jit(solution)/shard_map/ppermute | solution.py:363
  20.5 1.3 %collective-permute-start.8 = (f32[32,640]{1,0:T(8,128)S(1)}, f32[32,640]{1,0:T(8,128)S(1)}, u32[]{:S(2)}, u32[]{:S(2)}) collective-permute-start(f32[32,640]{1,0:T(8,128)S(1)} %collective-permute-done.4.refs_15_), channel_id=1, source_target_pairs={{0,2},{1,3},{2,0},{3,1},{4,6},{5,7},{6,4},{7,5},{8,10},{9,11},{10,... | collective-permute-start | bytes 245768 | tf_op jit(solution)/shard_map/ppermute | solution.py:363
  20.6 1.4 %collective-permute-start.9 = (f32[32,640]{1,0:T(8,128)S(1)}, f32[32,640]{1,0:T(8,128)S(1)}, u32[]{:S(2)}, u32[]{:S(2)}) collective-permute-start(f32[32,640]{1,0:T(8,128)S(1)} %collective-permute-done.5.refs_16_), channel_id=1, source_target_pairs={{0,2},{1,3},{2,0},{3,1},{4,6},{5,7},{6,4},{7,5},{8,10},{9,11},{10,... | collective-permute-start | bytes 245768 | tf_op jit(solution)/shard_map/ppermute | solution.py:363
  27.4 1.7 %collective-permute-start.10 = (f32[128,640]{1,0:T(8,128)S(1)}, f32[128,640]{1,0:T(8,128)S(1)}, u32[]{:S(2)}, u32[]{:S(2)}) collective-permute-start(f32[128,640]{1,0:T(8,128)S(1)} %slice.67), channel_id=1, source_target_pairs={{0,2},{1,3},{2,0},{3,1},{4,6},{5,7},{6,4},{7,5},{8,10},{9,11},{10,... | collective-permute-start | bytes 983048 | tf_op jit(solution)/shard_map/ppermute | solution.py:363
  29.1 5.8 %collective-permute-start.11 = (f32[32,640]{1,0:T(8,128)S(1)}, f32[32,640]{1,0:T(8,128)S(1)}, u32[]{:S(2)}, u32[]{:S(2)}) collective-permute-start(f32[32,640]{1,0:T(8,128)S(1)} %get-tuple-element.72), channel_id=1, source_target_pairs={{0,4},{1,5},{2,6},{3,7},{4,0},{5,1},{6,2},{7,3},{8,12},{9,13},{10,... | collective-permute-start | bytes 245768 | tf_op jit(solution)/shard_map/ppermute | solution.py:363
  30.9 5.9 %collective-permute-start.13 = (f32[32,640]{1,0:T(8,128)S(1)}, f32[32,640]{1,0:T(8,128)S(1)}, u32[]{:S(2)}, u32[]{:S(2)}) collective-permute-start(f32[32,640]{1,0:T(8,128)S(1)} %get-tuple-element.73), channel_id=1, source_target_pairs={{0,5},{1,4},{2,7},{3,6},{4,1},{5,0},{6,3},{7,2},{8,13},{9,12},{10,... | collective-permute-start | bytes 245768 | tf_op jit(solution)/shard_map/ppermute | solution.py:363
  32.3 4.6 %collective-permute-start.12 = (f32[32,640]{1,0:T(8,128)S(1)}, f32[32,640]{1,0:T(8,128)S(1)}, u32[]{:S(2)}, u32[]{:S(2)}) collective-permute-start(f32[32,640]{1,0:T(8,128)S(1)} %get-tuple-element.74), channel_id=1, source_target_pairs={{0,1},{1,0},{2,3},{3,2},{4,5},{5,4},{6,7},{7,6},{8,9},{9,8},{10,11... | collective-permute-start | bytes 245768 | tf_op jit(solution)/shard_map/ppermute | solution.py:363
  36.9 7.0 %collective-permute-start.16 = (f32[32,640]{1,0:T(8,128)S(1)}, f32[32,640]{1,0:T(8,128)S(1)}, u32[]{:S(2)}, u32[]{:S(2)}) collective-permute-start(f32[32,640]{1,0:T(8,128)S(1)} %fusion.7.refs_0_), channel_id=1, source_target_pairs={{0,24},{1,25},{2,26},{3,27},{4,28},{5,29},{6,30},{7,31},{8,16},{9,... | collective-permute-start | bytes 245768 | tf_op jit(solution)/shard_map/ppermute | solution.py:363
  40.7 6.5 %collective-permute-start.15 = (f32[32,640]{1,0:T(8,128)S(1)}, f32[32,640]{1,0:T(8,128)S(1)}, u32[]{:S(2)}, u32[]{:S(2)}) collective-permute-start(f32[32,640]{1,0:T(8,128)S(1)} %fusion.7.refs_0_), channel_id=1, source_target_pairs={{0,16},{1,17},{2,18},{3,19},{4,20},{5,21},{6,22},{7,23},{8,24},{9,... | collective-permute-start | bytes 245768 | tf_op jit(solution)/shard_map/ppermute | solution.py:363
  40.7 6.5 %collective-permute-start.14 = (f32[32,640]{1,0:T(8,128)S(1)}, f32[32,640]{1,0:T(8,128)S(1)}, u32[]{:S(2)}, u32[]{:S(2)}) collective-permute-start(f32[32,640]{1,0:T(8,128)S(1)} %fusion.7.refs_0_), channel_id=1, source_target_pairs={{0,8},{1,9},{2,10},{3,11},{4,12},{5,13},{6,14},{7,15},{8,0},{9,1},... | collective-permute-start | bytes 245768 | tf_op jit(solution)/shard_map/ppermute | solution.py:363
  47.5 5.6 %collective-permute-start.19 = (f32[32,640]{1,0:T(8,128)S(1)}, f32[32,640]{1,0:T(8,128)S(1)}, u32[]{:S(2)}, u32[]{:S(2)}) collective-permute-start(f32[32,640]{1,0:T(8,128)S(1)} %get-tuple-element.54.refs_13_), channel_id=1, source_target_pairs={{0,5},{1,4},{2,7},{3,6},{4,1},{5,0},{6,3},{7,2},{8,13},{9,12},{10,... | collective-permute-start | bytes 245768 | tf_op jit(solution)/shard_map/ppermute | solution.py:363
  49.7 4.4 %collective-permute-start.18 = (f32[32,640]{1,0:T(8,128)S(1)}, f32[32,640]{1,0:T(8,128)S(1)}, u32[]{:S(2)}, u32[]{:S(2)}) collective-permute-start(f32[32,640]{1,0:T(8,128)S(1)} %get-tuple-element.54.refs_13_), channel_id=1, source_target_pairs={{0,1},{1,0},{2,3},{3,2},{4,5},{5,4},{6,7},{7,6},{8,9},{9,8},{10,11... | collective-permute-start | bytes 245768 | tf_op jit(solution)/shard_map/ppermute | solution.py:363
  50.5 4.4 %collective-permute-start.17 = (f32[32,640]{1,0:T(8,128)S(1)}, f32[32,640]{1,0:T(8,128)S(1)}, u32[]{:S(2)}, u32[]{:S(2)}) collective-permute-start(f32[32,640]{1,0:T(8,128)S(1)} %get-tuple-element.54.refs_13_), channel_id=1, source_target_pairs={{0,4},{1,5},{2,6},{3,7},{4,0},{5,1},{6,2},{7,3},{8,12},{9,13},{10,... | collective-permute-start | bytes 245768 | tf_op jit(solution)/shard_map/ppermute | solution.py:363
  51.1 3.9 %collective-permute-start.20 = (f32[32,640]{1,0:T(8,128)S(1)}, f32[32,640]{1,0:T(8,128)S(1)}, u32[]{:S(2)}, u32[]{:S(2)}) collective-permute-start(f32[32,640]{1,0:T(8,128)S(1)} %get-tuple-element.54.refs_13_), channel_id=1, source_target_pairs={{0,2},{1,3},{2,0},{3,1},{4,6},{5,7},{6,4},{7,5},{8,10},{9,11},{10,... | collective-permute-start | bytes 245768 | tf_op jit(solution)/shard_map/ppermute | solution.py:363
  53.1 1.9 %collective-permute-start.23 = (f32[32,640]{1,0:T(8,128)S(1)}, f32[32,640]{1,0:T(8,128)S(1)}, u32[]{:S(2)}, u32[]{:S(2)}) collective-permute-start(f32[32,640]{1,0:T(8,128)S(1)} %collective-permute-done.19.refs_16_), channel_id=1, source_target_pairs={{0,2},{1,3},{2,0},{3,1},{4,6},{5,7},{6,4},{7,5},{8,10},{9,11},{10,... | collective-permute-start | bytes 245768 | tf_op jit(solution)/shard_map/ppermute | solution.py:363
  54.1 1.3 %collective-permute-start.22 = (f32[32,640]{1,0:T(8,128)S(1)}, f32[32,640]{1,0:T(8,128)S(1)}, u32[]{:S(2)}, u32[]{:S(2)}) collective-permute-start(f32[32,640]{1,0:T(8,128)S(1)} %collective-permute-done.18.refs_15_), channel_id=1, source_target_pairs={{0,2},{1,3},{2,0},{3,1},{4,6},{5,7},{6,4},{7,5},{8,10},{9,11},{10,... | collective-permute-start | bytes 245768 | tf_op jit(solution)/shard_map/ppermute | solution.py:363
  54.9 1.3 %collective-permute-start.21 = (f32[32,640]{1,0:T(8,128)S(1)}, f32[32,640]{1,0:T(8,128)S(1)}, u32[]{:S(2)}, u32[]{:S(2)}) collective-permute-start(f32[32,640]{1,0:T(8,128)S(1)} %collective-permute-done.17.refs_14_), channel_id=1, source_target_pairs={{0,2},{1,3},{2,0},{3,1},{4,6},{5,7},{6,4},{7,5},{8,10},{9,11},{10,... | collective-permute-start | bytes 245768 | tf_op jit(solution)/shard_map/ppermute | solution.py:363
  62.0 1.7 %collective-permute-start.24 = (f32[128,640]{1,0:T(8,128)S(1)}, f32[128,640]{1,0:T(8,128)S(1)}, u32[]{:S(2)}, u32[]{:S(2)}) collective-permute-start(f32[128,640]{1,0:T(8,128)S(1)} %slice.73), channel_id=1, source_target_pairs={{0,2},{1,3},{2,0},{3,1},{4,6},{5,7},{6,4},{7,5},{8,10},{9,11},{10,... | collective-permute-start | bytes 983048 | tf_op jit(solution)/shard_map/ppermute | solution.py:363
  63.8 5.8 %collective-permute-start.25 = (f32[32,640]{1,0:T(8,128)S(1)}, f32[32,640]{1,0:T(8,128)S(1)}, u32[]{:S(2)}, u32[]{:S(2)}) collective-permute-start(f32[32,640]{1,0:T(8,128)S(1)} %get-tuple-element.69), channel_id=1, source_target_pairs={{0,4},{1,5},{2,6},{3,7},{4,0},{5,1},{6,2},{7,3},{8,12},{9,13},{10,... | collective-permute-start | bytes 245768 | tf_op jit(solution)/shard_map/ppermute | solution.py:363
  64.4 6.0 %collective-permute-start.27 = (f32[32,640]{1,0:T(8,128)S(1)}, f32[32,640]{1,0:T(8,128)S(1)}, u32[]{:S(2)}, u32[]{:S(2)}) collective-permute-start(f32[32,640]{1,0:T(8,128)S(1)} %get-tuple-element.70), channel_id=1, source_target_pairs={{0,5},{1,4},{2,7},{3,6},{4,1},{5,0},{6,3},{7,2},{8,13},{9,12},{10,... | collective-permute-start | bytes 245768 | tf_op jit(solution)/shard_map/ppermute | solution.py:363
  66.5 4.8 %collective-permute-start.26 = (f32[32,640]{1,0:T(8,128)S(1)}, f32[32,640]{1,0:T(8,128)S(1)}, u32[]{:S(2)}, u32[]{:S(2)}) collective-permute-start(f32[32,640]{1,0:T(8,128)S(1)} %get-tuple-element.71), channel_id=1, source_target_pairs={{0,1},{1,0},{2,3},{3,2},{4,5},{5,4},{6,7},{7,6},{8,9},{9,8},{10,11... | collective-permute-start | bytes 245768 | tf_op jit(solution)/shard_map/ppermute | solution.py:363
  71.3 6.4 %collective-permute-start.30 = (f32[32,640]{1,0:T(8,128)S(1)}, f32[32,640]{1,0:T(8,128)S(1)}, u32[]{:S(2)}, u32[]{:S(2)}) collective-permute-start(f32[32,640]{1,0:T(8,128)S(1)} %fusion.5.refs_0_), channel_id=1, source_target_pairs={{0,24},{1,25},{2,26},{3,27},{4,28},{5,29},{6,30},{7,31},{8,16},{9,... | collective-permute-start | bytes 245768 | tf_op jit(solution)/shard_map/ppermute | solution.py:363
  74.1 6.9 %collective-permute-start.29 = (f32[32,640]{1,0:T(8,128)S(1)}, f32[32,640]{1,0:T(8,128)S(1)}, u32[]{:S(2)}, u32[]{:S(2)}) collective-permute-start(f32[32,640]{1,0:T(8,128)S(1)} %fusion.5.refs_0_), channel_id=1, source_target_pairs={{0,16},{1,17},{2,18},{3,19},{4,20},{5,21},{6,22},{7,23},{8,24},{9,... | collective-permute-start | bytes 245768 | tf_op jit(solution)/shard_map/ppermute | solution.py:363
  74.1 6.9 %collective-permute-start.28 = (f32[32,640]{1,0:T(8,128)S(1)}, f32[32,640]{1,0:T(8,128)S(1)}, u32[]{:S(2)}, u32[]{:S(2)}) collective-permute-start(f32[32,640]{1,0:T(8,128)S(1)} %fusion.5.refs_0_), channel_id=1, source_target_pairs={{0,8},{1,9},{2,10},{3,11},{4,12},{5,13},{6,14},{7,15},{8,0},{9,1},... | collective-permute-start | bytes 245768 | tf_op jit(solution)/shard_map/ppermute | solution.py:363
  81.3 5.5 %collective-permute-start.33 = (f32[32,640]{1,0:T(8,128)S(1)}, f32[32,640]{1,0:T(8,128)S(1)}, u32[]{:S(2)}, u32[]{:S(2)}) collective-permute-start(f32[32,640]{1,0:T(8,128)S(1)} %get-tuple-element.60.refs_13_), channel_id=1, source_target_pairs={{0,5},{1,4},{2,7},{3,6},{4,1},{5,0},{6,3},{7,2},{8,13},{9,12},{10,... | collective-permute-start | bytes 245768 | tf_op jit(solution)/shard_map/ppermute | solution.py:363
  82.4 4.4 %collective-permute-start.32 = (f32[32,640]{1,0:T(8,128)S(1)}, f32[32,640]{1,0:T(8,128)S(1)}, u32[]{:S(2)}, u32[]{:S(2)}) collective-permute-start(f32[32,640]{1,0:T(8,128)S(1)} %get-tuple-element.60.refs_13_), channel_id=1, source_target_pairs={{0,1},{1,0},{2,3},{3,2},{4,5},{5,4},{6,7},{7,6},{8,9},{9,8},{10,11... | collective-permute-start | bytes 245768 | tf_op jit(solution)/shard_map/ppermute | solution.py:363
  83.3 4.4 %collective-permute-start.31 = (f32[32,640]{1,0:T(8,128)S(1)}, f32[32,640]{1,0:T(8,128)S(1)}, u32[]{:S(2)}, u32[]{:S(2)}) collective-permute-start(f32[32,640]{1,0:T(8,128)S(1)} %get-tuple-element.60.refs_13_), channel_id=1, source_target_pairs={{0,4},{1,5},{2,6},{3,7},{4,0},{5,1},{6,2},{7,3},{8,12},{9,13},{10,... | collective-permute-start | bytes 245768 | tf_op jit(solution)/shard_map/ppermute | solution.py:363
  84.8 2.9 %collective-permute-start.34 = (f32[32,640]{1,0:T(8,128)S(1)}, f32[32,640]{1,0:T(8,128)S(1)}, u32[]{:S(2)}, u32[]{:S(2)}) collective-permute-start(f32[32,640]{1,0:T(8,128)S(1)} %get-tuple-element.60.refs_13_), channel_id=1, source_target_pairs={{0,2},{1,3},{2,0},{3,1},{4,6},{5,7},{6,4},{7,5},{8,10},{9,11},{10,... | collective-permute-start | bytes 245768 | tf_op jit(solution)/shard_map/ppermute | solution.py:363
  86.8 1.3 %collective-permute-start.37 = (f32[32,640]{1,0:T(8,128)S(1)}, f32[32,640]{1,0:T(8,128)S(1)}, u32[]{:S(2)}, u32[]{:S(2)}) collective-permute-start(f32[32,640]{1,0:T(8,128)S(1)} %collective-permute-done.33.refs_16_), channel_id=1, source_target_pairs={{0,2},{1,3},{2,0},{3,1},{4,6},{5,7},{6,4},{7,5},{8,10},{9,11},{10,... | collective-permute-start | bytes 245768 | tf_op jit(solution)/shard_map/ppermute | solution.py:363
  86.9 1.4 %collective-permute-start.36 = (f32[32,640]{1,0:T(8,128)S(1)}, f32[32,640]{1,0:T(8,128)S(1)}, u32[]{:S(2)}, u32[]{:S(2)}) collective-permute-start(f32[32,640]{1,0:T(8,128)S(1)} %collective-permute-done.32.refs_15_), channel_id=1, source_target_pairs={{0,2},{1,3},{2,0},{3,1},{4,6},{5,7},{6,4},{7,5},{8,10},{9,11},{10,... | collective-permute-start | bytes 245768 | tf_op jit(solution)/shard_map/ppermute | solution.py:363
  87.8 1.3 %collective-permute-start.35 = (f32[32,640]{1,0:T(8,128)S(1)}, f32[32,640]{1,0:T(8,128)S(1)}, u32[]{:S(2)}, u32[]{:S(2)}) collective-permute-start(f32[32,640]{1,0:T(8,128)S(1)} %collective-permute-done.31.refs_14_), channel_id=1, source_target_pairs={{0,2},{1,3},{2,0},{3,1},{4,6},{5,7},{6,4},{7,5},{8,10},{9,11},{10,... | collective-permute-start | bytes 245768 | tf_op jit(solution)/shard_map/ppermute | solution.py:363
  94.6 1.7 %collective-permute-start.38 = (f32[128,640]{1,0:T(8,128)S(1)}, f32[128,640]{1,0:T(8,128)S(1)}, u32[]{:S(2)}, u32[]{:S(2)}) collective-permute-start(f32[128,640]{1,0:T(8,128)S(1)} %slice.79), channel_id=1, source_target_pairs={{0,2},{1,3},{2,0},{3,1},{4,6},{5,7},{6,4},{7,5},{8,10},{9,11},{10,... | collective-permute-start | bytes 983048 | tf_op jit(solution)/shard_map/ppermute | solution.py:363
  96.4 4.7 %collective-permute-start.39 = (f32[32,640]{1,0:T(8,128)S(1)}, f32[32,640]{1,0:T(8,128)S(1)}, u32[]{:S(2)}, u32[]{:S(2)}) collective-permute-start(f32[32,640]{1,0:T(8,128)S(1)} %get-tuple-element.66), channel_id=1, source_target_pairs={{0,4},{1,5},{2,6},{3,7},{4,0},{5,1},{6,2},{7,3},{8,12},{9,13},{10,... | collective-permute-start | bytes 245768 | tf_op jit(solution)/shard_map/ppermute | solution.py:363
  98.0 6.0 %collective-permute-start.41 = (f32[32,640]{1,0:T(8,128)S(1)}, f32[32,640]{1,0:T(8,128)S(1)}, u32[]{:S(2)}, u32[]{:S(2)}) collective-permute-start(f32[32,640]{1,0:T(8,128)S(1)} %get-tuple-element.67), channel_id=1, source_target_pairs={{0,5},{1,4},{2,7},{3,6},{4,1},{5,0},{6,3},{7,2},{8,13},{9,12},{10,... | collective-permute-start | bytes 245768 | tf_op jit(solution)/shard_map/ppermute | solution.py:363
  99.1 4.9 %collective-permute-start.40 = (f32[32,640]{1,0:T(8,128)S(1)}, f32[32,640]{1,0:T(8,128)S(1)}, u32[]{:S(2)}, u32[]{:S(2)}) collective-permute-start(f32[32,640]{1,0:T(8,128)S(1)} %get-tuple-element.68), channel_id=1, source_target_pairs={{0,1},{1,0},{2,3},{3,2},{4,5},{5,4},{6,7},{7,6},{8,9},{9,8},{10,11... | collective-permute-start | bytes 245768 | tf_op jit(solution)/shard_map/ppermute | solution.py:363
  104.0 5.6 %collective-permute-start.44 = (f32[8,640]{1,0:T(8,128)S(1)}, f32[8,640]{1,0:T(8,128)S(1)}, u32[]{:S(2)}, u32[]{:S(2)}) collective-permute-start(f32[8,640]{1,0:T(8,128)S(1)} %get-tuple-element.75), channel_id=1, source_target_pairs={{0,24},{1,25},{2,26},{3,27},{4,28},{5,29},{6,30},{7,31},{8,16},{9,... | collective-permute-start | bytes 61448 | tf_op jit(solution)/shard_map/ppermute | solution.py:363
  106.4 4.7 %collective-permute-start.43 = (f32[8,640]{1,0:T(8,128)S(1)}, f32[8,640]{1,0:T(8,128)S(1)}, u32[]{:S(2)}, u32[]{:S(2)}) collective-permute-start(f32[8,640]{1,0:T(8,128)S(1)} %get-tuple-element.76), channel_id=1, source_target_pairs={{0,16},{1,17},{2,18},{3,19},{4,20},{5,21},{6,22},{7,23},{8,24},{9,... | collective-permute-start | bytes 61448 | tf_op jit(solution)/shard_map/ppermute | solution.py:363
  106.4 4.7 %collective-permute-start.42 = (f32[8,640]{1,0:T(8,128)S(1)}, f32[8,640]{1,0:T(8,128)S(1)}, u32[]{:S(2)}, u32[]{:S(2)}) collective-permute-start(f32[8,640]{1,0:T(8,128)S(1)} %get-tuple-element.77), channel_id=1, source_target_pairs={{0,8},{1,9},{2,10},{3,11},{4,12},{5,13},{6,14},{7,15},{8,0},{9,1},... | collective-permute-start | bytes 61448 | tf_op jit(solution)/shard_map/ppermute | solution.py:363
